TPU v7x, 32 devices: a whole 2x2x4 slice. The times are simulated.
32 devices in a mesh: lat: 8 (over z, x), lev: 4 (over y, core).
Axes of the slice: x: 2, y: 2, z: 4, core: 2. Of those that a mesh axis runs over, the one named last changes fastest.
Arguments:
- fields: float32 [4, 128, 32, 512], P(None, 'lev', 'lat'), may hold values from -6 to 6
- courant_lon: float32 [128, 32, 512], P('lev', 'lat'), may hold values from -0.45 to 0.45
- courant_lat: float32 [128, 32, 512], P('lev', 'lat'), may hold values from -0.45 to 0.45
- displacement: float32 [128, 32, 512], P('lev', 'lat'), may hold values from 0 to 0.6
- own_slot: int32 [4, 8, 2], P('lev', 'lat'), may hold values from 0 to 4, as said below
- lent_slot: int32 [4, 8, 2], P('lev', 'lat'), may hold values from 0 to 4, as said below
- w_first: bfloat16 [512, 768], replicated, may hold values from -0.25 to 0.25
- bias_first: float32 [768], replicated, may hold values from -3 to 3
- w_second: bfloat16 [768, 640], replicated, may hold values from -0.21875 to 0.21875
- bias_second: float32 [640], replicated, may hold values from -3 to 3
- w_third: bfloat16 [640, 512], replicated, may hold values from -0.25 to 0.25
- bias_third: float32 [512], replicated, may hold values from -3 to 3
Outputs:
- columns_out: float32 [512, 32, 512], P(None, 'lat', 'lev')
Inputs may be any that keep to these rules, and one draw needn't show every extreme that they name: own_slot[g, i, s] is a block of band i and group g (0 to 3) handled in work slot s of that band, or 4 when the slot takes no own block; own blocks fill the first slots. lent_slot[g, i, s] is a block of band i and group g handled in work slot s of band (i + 4) mod 8 of group g, or 4; that slot then holds no own block there; no block appears twice in the two lists of its band and group.
All inputs are finite; a program needn't handle non-finite values.
Results may differ from a plain program's by a relative error of at most 0.002.
Values may be sent and summed in bfloat16 or wider, within the bound.
No kernel may reach another device: no remote copies, remote signals or barrier semaphores. Data moves between devices by JAX's collectives and lax.ppermute only.
A program may use at most 64 MiB of HBM per device.

v0:
```python
import jax
import jax.numpy as jnp
from jax import lax
from jax.sharding import PartitionSpec as P


def padded_2(value, sides, width):
    for axis, dim in sides:
        count, length = (lax.axis_size(axis), value.shape[dim])
        up = [(i, (i + 1) % count) for i in range(count - 1)]
        down = [(j, i) for i, j in up]
        last = lax.slice_in_dim(value, length - width, length, axis=dim)
        initial = lax.slice_in_dim(value, 0, width, axis=dim)
        before = lax.ppermute(last, axis, up)
        after = lax.ppermute(initial, axis, down)
        value = jnp.concatenate([before, value, after], axis=dim)
    return value


def from_behind(value, axis, by):
    count = lax.axis_size(axis)
    return lax.ppermute(value, axis, [(i, (i + by) % count) for i in range(count)])


def upwind(fields, western, eastern, northern, southern, along_lon, along_lat):
    result = fields - jnp.maximum(along_lon, 0.0) * (fields - western)
    result = result - jnp.minimum(along_lon, 0.0) * (eastern - fields)
    result = result - jnp.maximum(along_lat, 0.0) * (fields - northern)
    return result - jnp.minimum(along_lat, 0.0) * (southern - fields)


def left_product(weight, rows):
    return lax.dot_general(
        weight, rows, (((0,), (0,)), ((), ())), preferred_element_type=jnp.float32
    )


def network(rows, w_first, bias_first, w_second, bias_second, w_third, bias_third):
    hidden = left_product(w_first, rows) + bias_first[:, None]
    hidden = jax.nn.silu(hidden).astype(jnp.bfloat16)
    hidden = left_product(w_second, hidden) + bias_second[:, None]
    hidden = jax.nn.silu(hidden).astype(jnp.bfloat16)
    return (left_product(w_third, hidden) + bias_third[:, None]).astype(jnp.bfloat16)


def body(
    fields,
    courant_lon,
    courant_lat,
    displacement,
    own_slot,
    lent_slot,
    w_first,
    bias_first,
    w_second,
    bias_second,
    w_third,
    bias_third,
):
    field_count, level_part, band_rows, lon_total = fields.shape
    group_count = lax.axis_size("lev")
    band_count = lax.axis_size("lat")
    lon_part = lon_total // group_count
    padded = padded_2(fields, (("lat", 2),), 1)
    advected = upwind(
        fields,
        jnp.roll(fields, 1, axis=3),
        jnp.roll(fields, -1, axis=3),
        padded[:, :, :-2, :],
        padded[:, :, 2:, :],
        courant_lon[None],
        courant_lat[None],
    )
    levels = level_part * group_count

    def split_lon(values):
        return values.reshape(values.shape[0], values.shape[1], band_rows, group_count, lon_part)

    moved, carried = (
        lax.all_to_all(split_lon(advected), "lev", split_axis=3, concat_axis=1, tiled=True),
        lax.all_to_all(
            split_lon(displacement[None]), "lev", split_axis=3, concat_axis=1, tiled=True
        ),
    )
    depth = lax.broadcasted_iota(jnp.int32, (1, levels, 1, 1, 1), 1)
    flux = jnp.where(depth < levels - 1, carried * moved, 0.0)
    above = jnp.concatenate([jnp.zeros_like(flux[:, :1]), flux[:, :-1]], axis=1)
    remapped = moved - flux + above
    width = field_count * levels
    own_list = own_slot.reshape(-1)
    lent_list = lent_slot.reshape(-1)
    work_count = own_list.shape[0]
    block_count = 2 * work_count
    block_rows = band_rows * lon_part // block_count
    blocks = remapped.reshape(width, block_count, block_rows)
    inputs = blocks.astype(jnp.bfloat16)
    block_ids = jnp.arange(block_count, dtype=jnp.int32)[:, None]
    own_hit = own_list[None, :] == block_ids
    lent_hit = lent_list[None, :] == block_ids
    lent_rows = jnp.take(inputs, jnp.minimum(lent_list, block_count - 1), axis=1)
    lent_rows = jnp.where(
        (lent_list < block_count)[None, :, None], lent_rows, jnp.zeros_like(lent_rows)
    )
    arrived = from_behind(lent_rows, "lat", band_count // 2)
    own_rows = jnp.take(inputs, jnp.minimum(own_list, block_count - 1), axis=1)
    work_rows = jnp.where((own_list < block_count)[None, :, None], own_rows, arrived)
    tendency = network(
        work_rows.reshape(width, -1),
        w_first,
        bias_first,
        w_second,
        bias_second,
        w_third,
        bias_third,
    ).reshape(work_rows.shape)
    returned = from_behind(tendency, "lat", band_count // 2)
    added = jnp.einsum(
        "bs,fsc->fbc",
        own_hit.astype(jnp.float32),
        tendency.astype(jnp.float32),
        precision=lax.Precision.HIGHEST,
    )
    added = added + jnp.einsum(
        "bs,fsc->fbc",
        lent_hit.astype(jnp.float32),
        returned.astype(jnp.float32),
        precision=lax.Precision.HIGHEST,
    )
    result = blocks + added
    return result


def solution(mesh):
    in_specs = (
        P(None, "lev", "lat", None),
        P("lev", "lat", None),
        P("lev", "lat", None),
        P("lev", "lat", None),
        P("lev", "lat", None),
        P("lev", "lat", None),
        P(),
        P(),
        P(),
        P(),
        P(),
        P(),
    )
    out_specs = P(None, "lat", "lev")
    return jax.shard_map(body, mesh=mesh, in_specs=in_specs, out_specs=out_specs, check_vma=False)
```

profile of v0, /device:TPU:0, one launch (start us, length us, event | category | flops | bytes accessed | tf_op | source)
XLA Modules:
  0.0 78.1 jit_solution(15922835392407111555)
XLA Ops:
  0.0 2.1 %fusion.32 = (f32[4,32,1,512]{3,2,1,0:T(1,128)S(1)}, f32[4,32,1,512]{3,2,1,0:T(1,128)S(1)}) fusion(f32[4,32,4,512]{3,2,1,0:T(4,128)} %param.14), kind=kLoop, calls=%fused_computation.63 | loop fusion | bytes 1048576 | tf_op jit(solution)/shard_map/slice | solution.py:12
  2.2 5.0 %collective-permute-start = (f32[4,32,1,512]{3,1,2,0:T(8,128)S(1)}, f32[4,32,1,512]{3,1,2,0:T(8,128)S(1)}, u32[]{:S(2)}, u32[]{:S(2)}) collective-permute-start(f32[4,32,1,512]{3,1,2,0:T(8,128)S(1)} %copy.64), channel_id=1, source_target_pairs={{0,4},{4,8},{8,12},{12,16},{16,20},{20,24},{24,28},{1,5},{5,9},{9,... | collective-permute-start | bytes 786440 | tf_op jit(solution)/shard_map/ppermute | solution.py:14
  7.2 1.4 %collective-permute-start.1 = (f32[4,32,1,512]{3,1,2,0:T(8,128)S(1)}, f32[4,32,1,512]{3,1,2,0:T(8,128)}, u32[]{:S(2)}, u32[]{:S(2)}) collective-permute-start(f32[4,32,1,512]{3,1,2,0:T(8,128)S(1)} %copy.65), channel_id=1, source_target_pairs={{4,0},{8,4},{12,8},{16,12},{20,16},{24,20},{28,24},{5,1},{9,5},{13... | collective-permute-start | bytes 786440 | tf_op jit(solution)/shard_map/ppermute | solution.py:15
  8.7 0.2 reshape.119
  8.8 0.8 %copy.52 = f32[1,32,4,4,128]{4,1,2,0,3:T(8,128)} copy(f32[1,32,4,4,128]{4,3,2,1,0:T(4,128)S(1)} %reshape.119) | data formatting | bytes 524288 | tf_op jit(solution)/shard_map/reshape;broadcast_in_dim | solution.py:77
  9.6 3.4 %all-to-all-start.1 = ((f32[1,32,4,4,128]{4,1,2,0,3:T(8,128)}), f32[1,32,4,4,128]{4,1,2,0,3:T(8,128)S(1)}, u32[]{:S(2)}, u32[]{:S(2)}) async-start(f32[1,32,4,4,128]{4,1,2,0,3:T(8,128)} %copy.52), calls=%async_computation.1 | async-start | bytes 524288 | tf_op jit(solution)/shard_map/all_to_all | solution.py:81
  13.0 0.6 fusion.30
  13.7 0.2 fusion.31
  13.9 0.7 copy-done.4
  14.7 0.2 broadcast_maximum_fusion
  14.9 3.5 %collective-permute-done = f32[4,32,1,512]{3,1,2,0:T(8,128)S(1)} collective-permute-done((f32[4,32,1,512]{3,1,2,0:T(8,128)S(1)}, f32[4,32,1,512]{3,1,2,0:T(8,128)S(1)}, u32[]{:S(2)}, u32[]{:S(2)}) %collective-permute-start) | collective-permute-done | bytes 262176 | tf_op jit(solution)/shard_map/ppermute | solution.py:14
  18.3 0.3 copy.45
  18.6 1.2 %copy.47 = f32[4,32,1,512]{3,2,1,0:T(1,128)S(1)} copy(f32[4,32,1,512]{3,1,2,0:T(8,128)} %collective-permute-done.1) | data formatting | bytes 524288 | tf_op jit(solution)/shard_map/ppermute | solution.py:15
  19.8 3.0 %copy_bitcast_fusion = f32[4,32,4,4,128]{4,2,1,0,3:T(4,128)} fusion(f32[4,32,4,512]{3,2,1,0:T(4,128)S(1)} %copy-done.1, f32[4,32,1,512]{3,2,1,0:T(1,128)S(1)} %copy.47, f32[4,32,1,512]{3,2,1,0:T(1,128)S(1)} %copy.45, f32[4,32,4,511]{3,2,1,0:T(4,128)S(1)} %get-tuple-element.11, f32[4,32,4,1]{3,2,1,0:T(4,128)S(1)} %get-tuple-element.13, ...), kind=kLoop, calls=%fused_computation.11 | loop fusion | flops 4194304 | bytes 5767168 | tf_op jit(solution)/shard_map/reshape | solution.py:77
  22.9 3.5 %all-to-all-start = ((f32[4,32,4,4,128]{4,2,1,0,3:T(4,128)}), f32[4,32,4,4,128]{4,2,1,0,3:T(4,128)S(1)}, u32[]{:S(2)}, u32[]{:S(2)}) async-start(f32[4,32,4,4,128]{4,2,1,0,3:T(4,128)} %copy_bitcast_fusion), calls=%async_computation | async-start | bytes 2097152 | tf_op jit(solution)/shard_map/all_to_all | solution.py:80
  26.4 0.6 copy-done.8
  27.1 13.7 %all-to-all-done = f32[4,32,4,4,128]{4,2,1,0,3:T(4,128)S(1)} async-done(((f32[4,32,4,4,128]{4,2,1,0,3:T(4,128)}), f32[4,32,4,4,128]{4,2,1,0,3:T(4,128)S(1)}, u32[]{:S(2)}, u32[]{:S(2)}) %all-to-all-start) | async-done | bytes 1048608 | tf_op jit(solution)/shard_map/all_to_all | solution.py:80
  41.0 0.2 fusion.16
  41.2 0.3 fusion.17
  41.5 0.7 copy.54
  42.2 0.2 bitcast_convert_fusion
  42.5 0.6 gather_fusion.1
  43.2 4.4 %collective-permute-start.2 = (bf16[512,2,128]{2,0,1:T(8,128)(2,1)S(1)}, bf16[512,2,128]{2,0,1:T(8,128)(2,1)S(1)}, u32[]{:S(2)}, u32[]{:S(2)}) collective-permute-start(bf16[512,2,128]{2,0,1:T(8,128)(2,1)S(1)} %bitcast_select_fusion), channel_id=1, source_target_pairs={{0,16},{4,20},{8,24},{12,28},{16,0},{20,4},{24,8},{28,12},{1,17},{... | collective-permute-start | bytes 786440 | tf_op jit(solution)/shard_map/ppermute | solution.py:22
  47.6 0.6 gather_fusion
  48.2 11.1 %collective-permute-done.2 = bf16[512,2,128]{2,0,1:T(8,128)(2,1)S(1)} collective-permute-done((bf16[512,2,128]{2,0,1:T(8,128)(2,1)S(1)}, bf16[512,2,128]{2,0,1:T(8,128)(2,1)S(1)}, u32[]{:S(2)}, u32[]{:S(2)}) %collective-permute-start.2) | collective-permute-done | bytes 262176 | tf_op jit(solution)/shard_map/ppermute | solution.py:22
  59.6 0.5 copy-done.9
  60.1 1.9 %multiply_convert_fusion.1 = bf16[640,256]{0,1:T(8,128)(2,1)S(1)} fusion(bf16[768,640]{1,0:T(8,128)(2,1)S(1)} %copy-done, bf16[512,256]{0,1:T(8,128)(2,1)S(1)} %bitcast.76, bf16[512,768]{1,0:T(8,128)(2,1)} %param.20, f32[768]{0:T(1024)S(1)} %copy-done.9, f32[640]{0:T(1024)S(1)} %copy-done.10), kind=kOutput, calls=%fused_computation.33 | convolution fusion | flops 455147520 | bytes 2364928 | tf_op jit(solution)/shard_map/dot_general | solution.py:33
  62.0 0.4 fusion.4
  62.4 0.2 copy.58
  62.7 0.6 fusion.21
  63.2 13.2 %collective-permute-done.3 = bf16[512,2,128]{2,1,0:T(2,128)(2,1)S(1)} collective-permute-done((bf16[512,2,128]{2,1,0:T(2,128)(2,1)S(1)}, bf16[512,2,128]{2,1,0:T(2,128)(2,1)S(1)}, u32[]{:S(2)}, u32[]{:S(2)}) %collective-permute-start.3) | collective-permute-done | bytes 262176 | tf_op jit(solution)/shard_map/ppermute | solution.py:22
  76.4 1.6 %fusion.1 = f32[512,4,128]{2,1,0:T(4,128)} fusion(f32[512,4,128]{2,1,0:T(4,128)S(1)} %bitcast.71, f32[512,128,4]{1,2,0:T(4,128)S(1)} %fusion.21, bf16[512,2,128]{2,1,0:T(2,128)(2,1)S(1)} %collective-permute-done.3, s32[2]{0:T(128)S(1)} %bitcast.78), kind=kOutput, calls=%fused_computation.4 | convolution fusion | flops 1572872 | bytes 3407880 | tf_op jit(solution)/shard_map/bs,fsc->fbc/dot_general | solution.py:123
  (35 shorter events, 0.9 us)
Async XLA Ops:
  0.0 59.6 %copy-start = (bf16[768,640]{1,0:T(8,128)(2,1)S(1)}, bf16[768,640]{1,0:T(8,128)(2,1)}, u32[]{:S(2)}) copy-start(bf16[768,640]{1,0:T(8,128)(2,1)} %param.22) | copy-start | bytes 2949124
  2.1 6.5 %copy-start.3 = (f32[32,4,512]{2,1,0:T(4,128)S(1)}, f32[32,4,512]{2,1,0:T(4,128)}, u32[]{:S(2)}) copy-start(f32[32,4,512]{2,1,0:T(4,128)} %param.17) | copy-start | bytes 786436
  2.2 16.1 %collective-permute-start = (f32[4,32,1,512]{3,1,2,0:T(8,128)S(1)}, f32[4,32,1,512]{3,1,2,0:T(8,128)S(1)}, u32[]{:S(2)}, u32[]{:S(2)}) collective-permute-start(f32[4,32,1,512]{3,1,2,0:T(8,128)S(1)} %copy.64), channel_id=1, source_target_pairs={{0,4},{4,8},{8,12},{12,16},{16,20},{20,24},{24,28},{1,5},{5,9},{9,... | collective-permute-start | bytes 786440 | tf_op jit(solution)/shard_map/ppermute | solution.py:14
  7.2 5.8 %copy-start.1 = (f32[4,32,4,512]{3,2,1,0:T(4,128)S(1)}, f32[4,32,4,512]{3,2,1,0:T(4,128)}, u32[]{:S(2)}) copy-start(f32[4,32,4,512]{3,2,1,0:T(4,128)} %param.14) | copy-start | bytes 3145732
  7.2 11.4 %collective-permute-start.1 = (f32[4,32,1,512]{3,1,2,0:T(8,128)S(1)}, f32[4,32,1,512]{3,1,2,0:T(8,128)}, u32[]{:S(2)}, u32[]{:S(2)}) collective-permute-start(f32[4,32,1,512]{3,1,2,0:T(8,128)S(1)} %copy.65), channel_id=1, source_target_pairs={{4,0},{8,4},{12,8},{16,12},{20,16},{24,20},{28,24},{5,1},{9,5},{13... | collective-permute-start | bytes 786440 | tf_op jit(solution)/shard_map/ppermute | solution.py:15
  9.6 13.3 %all-to-all-start.1 = ((f32[1,32,4,4,128]{4,1,2,0,3:T(8,128)}), f32[1,32,4,4,128]{4,1,2,0,3:T(8,128)S(1)}, u32[]{:S(2)}, u32[]{:S(2)}) async-start(f32[1,32,4,4,128]{4,1,2,0,3:T(8,128)} %copy.52), calls=%async_computation.1 | async-start | bytes 524288 | tf_op jit(solution)/shard_map/all_to_all | solution.py:81
  13.6 1.0 %copy-start.4 = (f32[32,4,512]{2,1,0:T(4,128)S(1)}, f32[32,4,512]{2,1,0:T(4,128)}, u32[]{:S(2)}) copy-start(f32[32,4,512]{2,1,0:T(4,128)} %param.16) | copy-start | bytes 786436
  13.7 1.0 %copy-start.5 = (f32[32,4,512]{2,1,0:T(4,128)S(1)}, f32[32,4,512]{2,1,0:T(4,128)}, u32[]{:S(2)}) copy-start(f32[32,4,512]{2,1,0:T(4,128)} %param.15) | copy-start | bytes 786436
  22.9 18.0 %all-to-all-start = ((f32[4,32,4,4,128]{4,2,1,0,3:T(4,128)}), f32[4,32,4,4,128]{4,2,1,0,3:T(4,128)S(1)}, u32[]{:S(2)}, u32[]{:S(2)}) async-start(f32[4,32,4,4,128]{4,2,1,0,3:T(4,128)} %copy_bitcast_fusion), calls=%async_computation | async-start | bytes 2097152 | tf_op jit(solution)/shard_map/all_to_all | solution.py:80
  26.4 0.7 copy-start.8
  43.1 4.5 %copy-start.7 = (s32[1,1,2]{2,1,0:T(1,128)S(1)}, s32[1,1,2]{2,1,0:T(1,128)}, u32[]{:S(2)}) copy-start(s32[1,1,2]{2,1,0:T(1,128)} %param.18) | copy-start | bytes 28
  43.2 16.1 %collective-permute-start.2 = (bf16[512,2,128]{2,0,1:T(8,128)(2,1)S(1)}, bf16[512,2,128]{2,0,1:T(8,128)(2,1)S(1)}, u32[]{:S(2)}, u32[]{:S(2)}) collective-permute-start(bf16[512,2,128]{2,0,1:T(8,128)(2,1)S(1)} %bitcast_select_fusion), channel_id=1, source_target_pairs={{0,16},{4,20},{8,24},{12,28},{16,0},{20,4},{24,8},{28,12},{1,17},{... | collective-permute-start | bytes 786440 | tf_op jit(solution)/shard_map/ppermute | solution.py:22
  59.4 0.7 copy-start.9
  59.4 0.7 copy-start.10
  60.1 1.9 %copy-start.2 = (bf16[640,512]{1,0:T(8,128)(2,1)S(1)}, bf16[640,512]{1,0:T(8,128)(2,1)}, u32[]{:S(2)}) copy-start(bf16[640,512]{1,0:T(8,128)(2,1)} %param.24) | copy-start | bytes 1966084
  60.1 1.9 %copy-start.6 = (f32[512]{0:T(512)S(1)}, f32[512]{0:T(512)}, u32[]{:S(2)}) copy-start(f32[512]{0:T(512)} %param.25) | copy-start | bytes 6148
  62.6 13.8 %collective-permute-start.3 = (bf16[512,2,128]{2,1,0:T(2,128)(2,1)S(1)}, bf16[512,2,128]{2,1,0:T(2,128)(2,1)S(1)}, u32[]{:S(2)}, u32[]{:S(2)}) collective-permute-start(bf16[512,2,128]{2,1,0:T(2,128)(2,1)S(1)} %copy.58), channel_id=1, source_target_pairs={{0,16},{4,20},{8,24},{12,28},{16,0},{20,4},{24,8},{28,12},{1,17},{... | collective-permute-start | bytes 786440 | tf_op jit(solution)/shard_map/ppermute | solution.py:22
where the time goes:
time: 78.5 us; the launch traced here: 78.1 us
  waiting for transfers between devices  41.5 us (53%)
  starting transfers between devices  17.8 us (23%)
  local copies, waits for them, and re-layouts  9.82 us (13%)
  matrix products  4.44 us (6%)
  other arithmetic  4.2 us (5%)
    ppermute x2, waiting for transfers between devices, from_behind(): lax.ppermute(value, axis, [(i, (i + by) % count) for i in range(count)])  24.3 us
    all_to_all x1, waiting for transfers between devices, body(): lax.all_to_all(split_lon(advected), 'lev', split_axis=3, concat_axis=1, t...  13.7 us
    ppermute x1, starting transfers between devices, padded_2(): before = lax.ppermute(last, axis, up)  4.99 us
    ppermute x2, starting transfers between devices, from_behind(): lax.ppermute(value, axis, [(i, (i + by) % count) for i in range(count)])  4.44 us
    all_to_all x1, starting transfers between devices, body(): lax.all_to_all(split_lon(advected), 'lev', split_axis=3, concat_axis=1, t...  3.52 us
    ppermute x1, waiting for transfers between devices, padded_2(): before = lax.ppermute(last, axis, up)  3.46 us
    all_to_all x1, starting transfers between devices, body(): lax.all_to_all(split_lon(displacement[None]), 'lev', split_axis=3, concat...  3.4 us
    reshape x1, other arithmetic, split_lon(): values.reshape(values.shape[0], values.shape[1], band_rows, group_count,...  3.05 us
  transfers between devices with their start and end apart: 6, of which 4 were waited for; matrix products, arithmetic and copies ran while one was open for 10% of the time, Pallas kernels for 0%

commit v1 on v0

v1 whole, which is shorter than its diff:
```python
import functools

import jax
import jax.numpy as jnp
from jax import lax
from jax.experimental import pallas as pl
from jax.experimental.pallas import tpu as pltpu
from jax.sharding import PartitionSpec as P

LANES = 128
SCALE = 4096.0
MEGA = 1024 * 1024
VMEM = pl.BlockSpec(memory_space=pltpu.VMEM)
SMEM = pl.BlockSpec(memory_space=pltpu.SMEM)
ANY = pl.BlockSpec(memory_space=pl.ANY)


def place(me, other, count):
    if count & (count - 1) == 0:
        return lax.bitwise_xor(me, other)
    return lax.rem(other - me + count, count)


def partner(me, step, count):
    if count & (count - 1) == 0:
        return me ^ step
    return (me + step) % count


def source(me, step, count):
    if count & (count - 1) == 0:
        return lax.bitwise_xor(me, step)
    return lax.rem(me - step + count, count)


def exchange(value, step, count):
    return lax.ppermute(value, "lev", [(i, partner(i, step, count)) for i in range(count)])


def params(mega=40):
    return pltpu.CompilerParams(vmem_limit_bytes=mega * MEGA)


def cost(flops, moved):
    return pl.CostEstimate(flops=flops, bytes_accessed=moved, transcendentals=0)


def edge_kernel(fields, out, sem):
    odd = lax.rem(lax.axis_index("lat"), 2)
    last = fields.shape[2] - 1
    copies = [
        pltpu.make_async_copy(fields.at[:, :, 0, :], out.at[1 - odd], sem.at[0]),
        pltpu.make_async_copy(fields.at[:, :, last, :], out.at[odd], sem.at[1]),
    ]
    for copy in copies:
        copy.start()
    for copy in copies:
        copy.wait()


def edge_rows(fields):
    count, levels, _, lon = fields.shape
    return pl.pallas_call(
        edge_kernel,
        in_specs=[ANY],
        out_specs=VMEM,
        out_shape=jax.ShapeDtypeStruct((2, count, levels, lon), fields.dtype),
        scratch_shapes=[pltpu.SemaphoreType.DMA((2,))],
        compiler_params=params(),
        name="edge_rows",
    )(fields)


def store_message(message, at, field, fields_count, advected, share, groups, me):
    levels = advected.shape[0]
    flux = share * advected
    depth = lax.broadcasted_iota(jnp.int32, flux.shape, 0)
    above = jnp.where(depth == 0, 0.0, pltpu.roll(flux, 1, 0))
    remapped = advected - flux + above
    base = field * levels
    for group in range(groups):
        where = place(me, group, groups)
        lanes = slice(group * LANES, (group + 1) * LANES)
        spot = (where,) + at
        message[spot + (slice(base, base + levels), slice(None))] = remapped[:, lanes]
        row = fields_count * levels + field
        message[spot + (slice(row, row + 1), slice(None))] = flux[levels - 1 :, lanes]


def advect_kernel(
    groups, fields, along_lon, along_lat, displacement, edges,
    message, partial, weight, share, inner, lon_row, lat_row, moved_row, sem,
):
    count, levels, rows, lon = fields.shape
    odd = lax.rem(lax.axis_index("lat"), 2)
    me = lax.axis_index("lev")
    copies = []
    for row in range(rows):
        copies.append(pltpu.make_async_copy(along_lon.at[:, row, :], lon_row.at[row], sem.at[0, row]))
        copies.append(pltpu.make_async_copy(along_lat.at[:, row, :], lat_row.at[row], sem.at[1, row]))
        copies.append(pltpu.make_async_copy(displacement.at[:, row, :], moved_row.at[row], sem.at[2, row]))
        if 0 < row < rows - 1:
            copies.append(pltpu.make_async_copy(fields.at[:, :, row, :], inner.at[row - 1], sem.at[3, row]))
    for copy in copies:
        copy.start()
    for copy in copies:
        copy.wait()
    depth = lax.broadcasted_iota(jnp.int32, (levels, lon), 0)
    bottom = jnp.logical_and(depth == levels - 1, me == groups - 1)

    def line(row, field):
        if row == 0:
            return edges[1 - odd, field]
        if row == rows - 1:
            return edges[odd, field]
        return inner[row - 1, field]

    for row in range(rows):
        c_lon = lon_row[row]
        c_lat = lat_row[row]
        east_wind, west_wind = jnp.maximum(c_lon, 0.0), jnp.minimum(c_lon, 0.0)
        south_wind, north_wind = jnp.maximum(c_lat, 0.0), jnp.minimum(c_lat, 0.0)
        moved = jnp.where(bottom, 0.0, moved_row[row])
        slot = 1 - odd if row == 0 else odd
        if row == 0:
            weight[slot] = south_wind
            share[slot] = moved
        elif row == rows - 1:
            weight[slot] = -north_wind
            share[slot] = moved
        for field in range(count):
            here = line(row, field)
            result = here - east_wind * (here - pltpu.roll(here, 1, 1))
            result = result - west_wind * (pltpu.roll(here, lon - 1, 1) - here)
            north = line(row - 1, field) if row > 0 else 0.0
            south = line(row + 1, field) if row < rows - 1 else 0.0
            result = result - south_wind * (here - north)
            result = result - north_wind * (south - here)
            if 0 < row < rows - 1:
                store_message(message, (row - 1,), field, count, result, moved, groups, me)
            else:
                partial[slot, field] = result


def padded_height(count, levels):
    return -(-(count * levels + count) // 16) * 16


def advect(fields, along_lon, along_lat, displacement, edges, groups):
    count, levels, rows, lon = fields.shape
    height = padded_height(count, levels)
    f32 = jnp.float32
    return pl.pallas_call(
        functools.partial(advect_kernel, groups),
        in_specs=[ANY, ANY, ANY, ANY, VMEM],
        out_specs=[VMEM] * 4,
        out_shape=[
            jax.ShapeDtypeStruct((groups, rows - 2, height, LANES), f32),
            jax.ShapeDtypeStruct((2, count, levels, lon), f32),
            jax.ShapeDtypeStruct((2, levels, lon), f32),
            jax.ShapeDtypeStruct((2, levels, lon), f32),
        ],
        scratch_shapes=[
            pltpu.VMEM((rows - 2, count, levels, lon), f32),
            pltpu.VMEM((rows, levels, lon), f32),
            pltpu.VMEM((rows, levels, lon), f32),
            pltpu.VMEM((rows, levels, lon), f32),
            pltpu.SemaphoreType.DMA((4, rows)),
        ],
        compiler_params=params(),
        cost_estimate=cost(2_000_000_000, 6_000_000),
        name="advect",
    )(fields, along_lon, along_lat, displacement, edges)


def finish_kernel(groups, slot, partial, weight, share, halo, message):
    count = partial.shape[1]
    me = lax.axis_index("lev")
    wind, moved = weight[slot], share[slot]
    for field in range(count):
        advected = partial[slot, field] + wind * halo[field]
        store_message(message, (), field, count, advected, moved, groups, me)


def finish(partial, weight, share, halo, groups, slot):
    _, count, levels, _ = partial.shape
    return pl.pallas_call(
        functools.partial(finish_kernel, groups, slot),
        in_specs=[VMEM] * 4,
        out_specs=VMEM,
        out_shape=jax.ShapeDtypeStruct((groups, padded_height(count, levels), LANES), jnp.float32),
        compiler_params=params(),
        name="finish",
    )(partial, weight, share, halo)


def turn_kernel(first, second, third, first_out, second_out, third_out):
    first_out[...] = first[...].T
    second_out[...] = second[...].T
    third_out[...] = third[...].T


def turned(first, second, third):
    return pl.pallas_call(
        turn_kernel,
        in_specs=[VMEM] * 3,
        out_specs=[VMEM] * 3,
        out_shape=[jax.ShapeDtypeStruct(w.shape[::-1], w.dtype) for w in (first, second, third)],
        compiler_params=params(),
        cost_estimate=cost(2_000_000_000, 5_000_000),
        name="turned",
    )(first, second, third)


def silu(value):
    half = 0.5 * value
    return half + half * jnp.tanh(half)


def physics_kernel(groups, blocks, count, levels, aliased, *refs):
    parts, refs = refs[:groups], refs[groups:]
    own, lent, first, bias_first, second, bias_second, third, bias_third = refs[:8]
    refs = refs[8 + aliased :]
    out, columns, carried, staged, sem = refs
    me = lax.axis_index("lev")
    odd = lax.rem(lax.axis_index("lat"), 2)
    depth = groups * levels
    many = len(blocks)
    for index in range(many):
        for step in range(groups):
            level = source(me, step, groups)
            part = parts[step]
            for field in range(count):
                start = pl.multiple_of(field * depth + level * levels, levels)
                columns[index, pl.ds(start, levels), :] = part[index, field * levels : (field + 1) * levels, :]
            carried[index, level, 0:count, :] = part[index, count * levels : count * levels + count, :]
        for field in range(count):
            for level in range(1, groups):
                row = field * depth + level * levels
                columns[index, row : row + 1, :] += carried[index, level - 1, field : field + 1, :]
    value = jnp.concatenate([columns[index].astype(jnp.bfloat16) for index in range(many)], axis=1)
    hidden = jnp.dot(first[...], value, preferred_element_type=jnp.float32) + bias_first[...]
    hidden = silu(hidden).astype(jnp.bfloat16)
    hidden = jnp.dot(second[...], hidden, preferred_element_type=jnp.float32) + bias_second[...]
    hidden = silu(hidden).astype(jnp.bfloat16)
    tendency = jnp.dot(third[...], hidden, preferred_element_type=jnp.float32) + bias_third[...]
    tendency = tendency.astype(jnp.bfloat16).astype(jnp.float32)
    slots = own.shape[-1]
    for index in range(many):
        block = blocks[index]
        number = block if isinstance(block, int) else jnp.where(odd == 1, block[1], block[0])
        active = own[0, 0, 0] == number
        for slot in range(slots):
            active = jnp.logical_or(active, own[0, 0, slot] == number)
            active = jnp.logical_or(active, lent[0, 0, slot] == number)
        part = tendency[:, index * LANES : (index + 1) * LANES]
        staged[index] = columns[index] + jnp.where(active, part, 0.0)

    for index in range(many):
        block = blocks[index]
        if isinstance(block, int):
            pltpu.make_async_copy(staged.at[index], out.at[:, block, :], sem.at[index]).start()
        else:
            for parity in range(2):

                @pl.when(odd == parity)
                def _():
                    pltpu.make_async_copy(staged.at[index], out.at[:, block[parity], :], sem.at[index]).start()

    for index in range(many):
        block = blocks[index]
        row = block if isinstance(block, int) else 0
        pltpu.make_async_copy(staged.at[index], out.at[:, row, :], sem.at[index]).wait()


def physics(parts, own, lent, network, rows, blocks, count, levels, result=None):
    groups = len(parts)
    many = len(blocks)
    width = count * groups * levels
    f32 = jnp.float32
    aliased = 0 if result is None else 1
    operands = [*parts, own, lent, *network]
    specs = [VMEM] * groups + [SMEM, SMEM] + [VMEM] * 6
    if aliased:
        operands.append(result)
        specs.append(ANY)
    return pl.pallas_call(
        functools.partial(physics_kernel, groups, blocks, count, levels, aliased),
        in_specs=specs,
        out_specs=ANY,
        out_shape=jax.ShapeDtypeStruct((width, rows, LANES), f32),
        scratch_shapes=[
            pltpu.VMEM((many, width, LANES), f32),
            pltpu.VMEM((many, groups, 8, LANES), f32),
            pltpu.VMEM((many, width, LANES), f32),
            pltpu.SemaphoreType.DMA((many,)),
        ],
        input_output_aliases={len(operands) - 1: 0} if aliased else {},
        compiler_params=params(),
        cost_estimate=cost(2_000_000_000, 5_000_000),
        name="physics",
    )(*operands)


def body(
    fields,
    courant_lon,
    courant_lat,
    displacement,
    own_slot,
    lent_slot,
    w_first,
    bias_first,
    w_second,
    bias_second,
    w_third,
    bias_third,
):
    count, levels, rows, lon = fields.shape
    groups = lax.axis_size("lev")
    bands = lax.axis_size("lat")
    half = jnp.float16
    f32 = jnp.float32

    edges = edge_rows(fields)
    near_pairs = [(i, i ^ 1) for i in range(bands) if i ^ 1 < bands]
    far_pairs = [(i, i + 1 if i % 2 else i - 1) for i in range(bands)]
    far_pairs = [(i, j) for i, j in far_pairs if 0 <= j < bands]
    near = lax.ppermute((edges[0] * SCALE).astype(half), "lat", near_pairs)
    far = lax.ppermute((edges[1] * SCALE).astype(half), "lat", far_pairs)
    message, partial, weight, share = advect(fields, courant_lon, courant_lat, displacement, edges, groups)
    weights = turned(w_first, w_second, w_third)
    biases = [b.reshape(-1, 1) for b in (bias_first, bias_second, bias_third)]
    network = [x for pair in zip(weights, biases) for x in pair]

    def swap(own_first):
        parts = [own_first[0]]
        for step in range(1, groups):
            sent = exchange((own_first[step] * SCALE).astype(half), step, groups)
            parts.append(sent.astype(f32) * (1.0 / SCALE))
        return parts

    near_message = finish(partial, weight, share, near.astype(f32) * (1.0 / SCALE), groups, 0)
    early = swap(jnp.concatenate([message, near_message[:, None]], axis=1))
    far_message = finish(partial, weight, share, far.astype(f32) * (1.0 / SCALE), groups, 1)
    late = swap(far_message[:, None])
    inner = tuple(range(1, rows - 1))
    result = physics(early, own_slot, lent_slot, network, rows, inner + ((rows - 1, 0),), count, levels)
    return physics(late, own_slot, lent_slot, network, rows, ((0, rows - 1),), count, levels, result)


def solution(mesh):
    in_specs = (
        P(None, "lev", "lat", None),
        P("lev", "lat", None),
        P("lev", "lat", None),
        P("lev", "lat", None),
        P("lev", "lat", None),
        P("lev", "lat", None),
        P(),
        P(),
        P(),
        P(),
        P(),
        P(),
    )
    out_specs = P(None, "lat", "lev")
    return jax.shard_map(body, mesh=mesh, in_specs=in_specs, out_specs=out_specs, check_vma=False)
```

time: 78.5 us -> 28.5 us (0.36)
  the two profiles are of different devices: /device:TPU:0 before, /device:TPU:23 now
where the time goes in v1:
time: 28.5 us; the launch traced here: 28.3 us
  starting transfers between devices  9.19 us (32%)
  Pallas kernels  8.84 us (31%)
  waiting for transfers between devices  5.51 us (19%)
  local copies, waits for them, and re-layouts  4.2 us (15%)
  other arithmetic  0.29 us (1%)
    pallas_call x2, Pallas kernels, physics(): pl.pallas_call(functools.partial(physics_kernel, groups, blocks, count, l...  5.75 us
    ppermute x6, waiting for transfers between devices, exchange(): lax.ppermute(value, 'lev', [(i, partner(i, step, count)) for i in range(c...  5.51 us
    ppermute x6, starting transfers between devices, exchange(): lax.ppermute(value, 'lev', [(i, partner(i, step, count)) for i in range(c...  4.75 us
    ppermute x1, starting transfers between devices, body(): far = lax.ppermute((edges[1] * SCALE).astype(half), 'lat', far_pairs)  4.12 us
    unnamed x26, local copies, waits for them, and re-layouts  3.76 us
    pallas_call x1, Pallas kernels, advect(): pl.pallas_call(functools.partial(advect_kernel, groups), in_specs=[ANY, A...  1.84 us
    pallas_call x1, Pallas kernels, turned(): pl.pallas_call(turn_kernel, in_specs=[VMEM] * 3, out_specs=[VMEM] * 3, ou...  0.68 us
  transfers between devices with their start and end apart: 8, of which 2 were waited for; matrix products, arithmetic and copies ran while one was open for 2% of the time, Pallas kernels for 9%

profile of v1, /device:TPU:23, one launch (start us, length us, event | category | flops | bytes accessed | tf_op | source)
XLA Modules:
  0.0 28.3 jit_solution(2134264162418554897)
XLA Ops:
  0.0 1.2 %copy-done = f32[4,32,4,512]{3,2,1,0:T(4,128)S(1)} copy-done((f32[4,32,4,512]{3,2,1,0:T(4,128)S(1)}, f32[4,32,4,512]{3,2,1,0:T(4,128)}, u32[]{:S(2)}) %copy-start) | copy-done | bytes 1048600
  1.2 0.4 %edge_rows.1.edges = f32[2,4,32,512]{3,2,1,0:T(8,128)S(1)} custom-call(f32[4,32,4,512]{3,2,1,0:T(4,128)S(1)} %copy-done), custom_call_target="tpu_custom_call" | custom-call | tf_op jit(solution)/shard_map/edge_rows/pallas_call | solution.py:63
  1.6 0.0 copy-start.1
  1.7 0.3 %collective-permute-start.4 = (f16[4,32,512]{2,1,0:T(8,128)(2,1)S(1)}, f16[4,32,512]{2,1,0:T(8,128)(2,1)S(1)}, u32[]{:S(2)}, u32[]{:S(2)}) collective-permute-start(f16[4,32,512]{2,1,0:T(8,128)(2,1)S(1)} %get-tuple-element.23), channel_id=1, source_target_pairs={{0,4},{4,0},{8,12},{12,8},{16,20},{20,16},{24,28},{28,24},{1,5},{5... | collective-permute-start | bytes 393224 | tf_op jit(solution)/shard_map/ppermute | solution.py:329
  2.0 4.1 %collective-permute-start = (f16[4,32,512]{2,1,0:T(8,128)(2,1)S(1)}, f16[4,32,512]{2,1,0:T(8,128)(2,1)S(1)}, u32[]{:S(2)}, u32[]{:S(2)}) collective-permute-start(f16[4,32,512]{2,1,0:T(8,128)(2,1)S(1)} %get-tuple-element.24), channel_id=1, source_target_pairs={{4,8},{8,4},{12,16},{16,12},{20,24},{24,20},{5,9},{9,5},{13,17},{1... | collective-permute-start | bytes 393224 | tf_op jit(solution)/shard_map/ppermute | solution.py:330
  6.2 0.0 copy-start.11
  6.2 0.1 copy.19.refs_11_
  6.3 0.5 %copy-done.11 = f32[640]{0:T(1024)S(1)} copy-done((f32[640]{0:T(1024)S(1)}, f32[640]{0:T(1024)}, u32[]{:S(2)}) %copy-start.11) | copy-done | bytes 2584
  6.8 0.1 reshape.45.refs_9_
  7.0 0.5 %copy-done.10 = f32[768]{0:T(1024)S(1)} copy-done((f32[768]{0:T(1024)S(1)}, f32[768]{0:T(1024)}, u32[]{:S(2)}) %copy-start.10) | copy-done | bytes 3096
  7.5 0.2 reshape.44.refs_7_
  7.7 0.1 copy-done.6
  7.8 0.7 %copy-done.5 = f32[32,4,512]{2,1,0:T(4,128)S(1)} copy-done((f32[32,4,512]{2,1,0:T(4,128)S(1)}, f32[32,4,512]{2,1,0:T(4,128)}, u32[]{:S(2)}) %copy-start.5) | copy-done | bytes 262168
  8.5 1.8 %advect.1 = (f32[4,2,144,128]{3,2,1,0:T(8,128)S(1)}, f32[2,4,32,512]{3,2,1,0:T(8,128)S(1)}, f32[2,32,512]{2,1,0:T(8,128)S(1)}, f32[2,32,512]{2,1,0:T(8,128)S(1)}) custom-call(f32[4,32,4,512]{3,2,1,0:T(4,128)S(1)} %copy-done.1, f32[32,4,512]{2,1,0:T(4,128)S(1)} %copy-done.5, f32[32,4,512]{2,1,0:T(4,128)S(1)} %copy-done.6, f32[32,4,512]{2,1,0:T(4,128)S(1)} %copy-done.7, ...), custom_call_target="tpu_custom_call" | custom-call | flops 2000000000 | bytes 6000000 | tf_op jit(solution)/shard_map/advect/pallas_call | solution.py:153
  10.4 0.7 %turned.1 = (bf16[768,512]{1,0:T(8,128)(2,1)S(1)}, bf16[640,768]{1,0:T(8,128)(2,1)S(1)}, bf16[512,640]{1,0:T(8,128)(2,1)S(1)}) custom-call(bf16[512,768]{1,0:T(8,128)(2,1)S(1)} %copy-done.3, bf16[768,640]{1,0:T(8,128)(2,1)S(1)} %copy-done.2, bf16[640,512]{1,0:T(8,128)(2,1)S(1)} %copy-done.4), custom_call_target="tpu_custom_call" | custom-call | flops 2000000000 | bytes 5000000 | tf_op jit(solution)/shard_map/turned/pallas_call | solution.py:204
  11.1 0.1 finish.3
  11.3 0.1 finish.2
  11.4 1.4 %collective-permute-start.3 = (f16[1,144,128]{2,1,0:T(8,128)(2,1)S(1)}, f16[1,144,128]{2,1,0:T(8,128)(2,1)S(1)}, u32[]{:S(2)}, u32[]{:S(2)}) collective-permute-start(f16[1,144,128]{2,1,0:T(8,128)(2,1)S(1)} %get-tuple-element.25), channel_id=1, source_target_pairs={{0,3},{1,2},{2,1},{3,0},{4,7},{5,6},{6,5},{7,4},{8,11},{9,10},{10,... | collective-permute-start | bytes 110600 | tf_op jit(solution)/shard_map/ppermute | solution.py:37
  12.8 1.2 %collective-permute-start.2 = (f16[1,144,128]{2,1,0:T(8,128)(2,1)S(1)}, f16[1,144,128]{2,1,0:T(8,128)(2,1)S(1)}, u32[]{:S(2)}, u32[]{:S(2)}) collective-permute-start(f16[1,144,128]{2,1,0:T(8,128)(2,1)S(1)} %get-tuple-element.26), channel_id=1, source_target_pairs={{0,2},{1,3},{2,0},{3,1},{4,6},{5,7},{6,4},{7,5},{8,10},{9,11},{10,... | collective-permute-start | bytes 110600 | tf_op jit(solution)/shard_map/ppermute | solution.py:37
  14.1 0.1 fusion.14
  14.1 0.7 %collective-permute-start.7 = (f16[3,144,128]{2,1,0:T(8,128)(2,1)S(1)}, f16[3,144,128]{2,1,0:T(8,128)(2,1)S(1)}, u32[]{:S(2)}, u32[]{:S(2)}) collective-permute-start(f16[3,144,128]{2,1,0:T(8,128)(2,1)S(1)} %get-tuple-element.19), channel_id=1, source_target_pairs={{0,3},{1,2},{2,1},{3,0},{4,7},{5,6},{6,5},{7,4},{8,11},{9,10},{10,... | collective-permute-start | bytes 331784 | tf_op jit(solution)/shard_map/ppermute | solution.py:37
  14.8 0.2 collective-permute-start.5
  15.1 1.2 %collective-permute-start.6 = (f16[3,144,128]{2,1,0:T(8,128)(2,1)S(1)}, f16[3,144,128]{2,1,0:T(8,128)(2,1)S(1)}, u32[]{:S(2)}, u32[]{:S(2)}) collective-permute-start(f16[3,144,128]{2,1,0:T(8,128)(2,1)S(1)} %get-tuple-element.22), channel_id=1, source_target_pairs={{0,2},{1,3},{2,0},{3,1},{4,6},{5,7},{6,4},{7,5},{8,10},{9,11},{10,... | collective-permute-start | bytes 331784 | tf_op jit(solution)/shard_map/ppermute | solution.py:37
  16.2 0.0 collective-permute-done.2
  16.3 3.2 %collective-permute-done.7 = f16[3,144,128]{2,1,0:T(8,128)(2,1)S(1)} collective-permute-done((f16[3,144,128]{2,1,0:T(8,128)(2,1)S(1)}, f16[3,144,128]{2,1,0:T(8,128)(2,1)S(1)}, u32[]{:S(2)}, u32[]{:S(2)}) %collective-permute-start.7) | collective-permute-done | bytes 110624 | tf_op jit(solution)/shard_map/ppermute | solution.py:37
  19.6 2.2 %collective-permute-done.6 = f16[3,144,128]{2,1,0:T(8,128)(2,1)S(1)} collective-permute-done((f16[3,144,128]{2,1,0:T(8,128)(2,1)S(1)}, f16[3,144,128]{2,1,0:T(8,128)(2,1)S(1)}, u32[]{:S(2)}, u32[]{:S(2)}) %collective-permute-start.6) | collective-permute-done | bytes 110624 | tf_op jit(solution)/shard_map/ppermute | solution.py:37
  21.9 0.0 copy-start.8
  21.9 0.0 copy-start.9
  21.9 0.6 %copy-done.8 = s32[1,1,2]{2,1,0:T(1,128)S(1)} copy-done((s32[1,1,2]{2,1,0:T(1,128)S(1)}, s32[1,1,2]{2,1,0:T(1,128)}, u32[]{:S(2)}) %copy-start.8) | copy-done | bytes 32
  22.5 0.0 copy-done.9
  22.6 3.1 %physics.2.refs_12_ = f32[512,4,128]{2,1,0:T(4,128)} custom-call(f32[3,144,128]{2,1,0:T(8,128)S(1)} %get-tuple-element.20.refs_0_, f32[3,144,128]{2,1,0:T(8,128)S(1)} %convert_multiply_fusion.4.refs_1_, f32[3,144,128]{2,1,0:T(8,128)S(1)} %convert_multiply_fusion.3.refs_2_, f32[3,144,128]{2,1,0:T(8,128)S(1)} %convert_multiply_fusion.2.refs_3_, ...), custom_call_target="tpu_custom_call" | custom-call | flops 2000000000 | bytes 5000000 | tf_op jit(solution)/shard_map/physics/pallas_call | solution.py:287
  25.7 2.6 %physics.3 = f32[512,4,128]{2,1,0:T(4,128)} custom-call(f32[1,144,128]{2,1,0:T(8,128)S(1)} %get-tuple-element.28.refs_0_, f32[1,144,128]{2,1,0:T(8,128)S(1)} %convert_multiply_fusion.7.refs_1_, f32[1,144,128]{2,1,0:T(8,128)S(1)} %convert_multiply_fusion.6.refs_2_, ...), custom_call_target="tpu_custom_call", output_to_operand_aliasing={{}: (12, {})} | custom-call | flops 2000000000 | bytes 5000000 | tf_op jit(solution)/shard_map/physics/pallas_call | solution.py:287
  (31 shorter events, 0.3 us)
Async XLA Ops:
  0.0 1.2 %copy-start = (f32[4,32,4,512]{3,2,1,0:T(4,128)S(1)}, f32[4,32,4,512]{3,2,1,0:T(4,128)}, u32[]{:S(2)}) copy-start(f32[4,32,4,512]{3,2,1,0:T(4,128)} %fields.3) | copy-start | bytes 3145732
  1.2 4.9 %copy-start.12 = (f32[512]{0:T(512)S(1)}, f32[512]{0:T(512)}, u32[]{:S(2)}) copy-start(f32[512]{0:T(512)} %param.23) | copy-start | bytes 6148
  1.2 6.5 %copy-start.7 = (f32[32,4,512]{2,1,0:T(4,128)S(1)}, f32[32,4,512]{2,1,0:T(4,128)}, u32[]{:S(2)}) copy-start(f32[32,4,512]{2,1,0:T(4,128)} %displacement.1) | copy-start | bytes 786436
  1.6 6.1 %copy-start.1 = (f32[4,32,4,512]{3,2,1,0:T(4,128)S(1)}, f32[4,32,4,512]{3,2,1,0:T(4,128)}, u32[]{:S(2)}) copy-start(f32[4,32,4,512]{3,2,1,0:T(4,128)} %fields.3) | copy-start | bytes 3145732
  1.7 9.4 %collective-permute-start.4 = (f16[4,32,512]{2,1,0:T(8,128)(2,1)S(1)}, f16[4,32,512]{2,1,0:T(8,128)(2,1)S(1)}, u32[]{:S(2)}, u32[]{:S(2)}) collective-permute-start(f16[4,32,512]{2,1,0:T(8,128)(2,1)S(1)} %get-tuple-element.23), channel_id=1, source_target_pairs={{0,4},{4,0},{8,12},{12,8},{16,20},{20,16},{24,28},{28,24},{1,5},{5... | collective-permute-start | bytes 393224 | tf_op jit(solution)/shard_map/ppermute | solution.py:329
  2.0 9.2 %collective-permute-start = (f16[4,32,512]{2,1,0:T(8,128)(2,1)S(1)}, f16[4,32,512]{2,1,0:T(8,128)(2,1)S(1)}, u32[]{:S(2)}, u32[]{:S(2)}) collective-permute-start(f16[4,32,512]{2,1,0:T(8,128)(2,1)S(1)} %get-tuple-element.24), channel_id=1, source_target_pairs={{4,8},{8,4},{12,16},{16,12},{20,24},{24,20},{5,9},{9,5},{13,17},{1... | collective-permute-start | bytes 393224 | tf_op jit(solution)/shard_map/ppermute | solution.py:330
  6.2 0.7 %copy-start.11 = (f32[640]{0:T(1024)S(1)}, f32[640]{0:T(1024)}, u32[]{:S(2)}) copy-start(f32[640]{0:T(1024)} %param.21) | copy-start | bytes 7684
  6.8 0.7 %copy-start.10 = (f32[768]{0:T(1024)S(1)}, f32[768]{0:T(1024)}, u32[]{:S(2)}) copy-start(f32[768]{0:T(1024)} %param.19) | copy-start | bytes 9220
  6.8 1.0 %copy-start.6 = (f32[32,4,512]{2,1,0:T(4,128)S(1)}, f32[32,4,512]{2,1,0:T(4,128)}, u32[]{:S(2)}) copy-start(f32[32,4,512]{2,1,0:T(4,128)} %along_lat.1) | copy-start | bytes 786436
  7.5 1.0 %copy-start.5 = (f32[32,4,512]{2,1,0:T(4,128)S(1)}, f32[32,4,512]{2,1,0:T(4,128)}, u32[]{:S(2)}) copy-start(f32[32,4,512]{2,1,0:T(4,128)} %along_lon.1) | copy-start | bytes 786436
  8.5 1.9 %copy-start.2 = (bf16[768,640]{1,0:T(8,128)(2,1)S(1)}, bf16[768,640]{1,0:T(8,128)(2,1)}, u32[]{:S(2)}) copy-start(bf16[768,640]{1,0:T(8,128)(2,1)} %second.1) | copy-start | bytes 2949124
  8.5 1.9 %copy-start.3 = (bf16[512,768]{1,0:T(8,128)(2,1)S(1)}, bf16[512,768]{1,0:T(8,128)(2,1)}, u32[]{:S(2)}) copy-start(bf16[512,768]{1,0:T(8,128)(2,1)} %first.1) | copy-start | bytes 2359300
  8.5 1.9 %copy-start.4 = (bf16[640,512]{1,0:T(8,128)(2,1)S(1)}, bf16[640,512]{1,0:T(8,128)(2,1)}, u32[]{:S(2)}) copy-start(bf16[640,512]{1,0:T(8,128)(2,1)} %third.1) | copy-start | bytes 1966084
  11.4 3.7 %collective-permute-start.3 = (f16[1,144,128]{2,1,0:T(8,128)(2,1)S(1)}, f16[1,144,128]{2,1,0:T(8,128)(2,1)S(1)}, u32[]{:S(2)}, u32[]{:S(2)}) collective-permute-start(f16[1,144,128]{2,1,0:T(8,128)(2,1)S(1)} %get-tuple-element.25), channel_id=1, source_target_pairs={{0,3},{1,2},{2,1},{3,0},{4,7},{5,6},{6,5},{7,4},{8,11},{9,10},{10,... | collective-permute-start | bytes 110600 | tf_op jit(solution)/shard_map/ppermute | solution.py:37
  12.8 3.5 %collective-permute-start.2 = (f16[1,144,128]{2,1,0:T(8,128)(2,1)S(1)}, f16[1,144,128]{2,1,0:T(8,128)(2,1)S(1)}, u32[]{:S(2)}, u32[]{:S(2)}) collective-permute-start(f16[1,144,128]{2,1,0:T(8,128)(2,1)S(1)} %get-tuple-element.26), channel_id=1, source_target_pairs={{0,2},{1,3},{2,0},{3,1},{4,6},{5,7},{6,4},{7,5},{8,10},{9,11},{10,... | collective-permute-start | bytes 110600 | tf_op jit(solution)/shard_map/ppermute | solution.py:37
  14.1 2.2 %collective-permute-start.1 = (f16[1,144,128]{2,1,0:T(8,128)(2,1)S(1)}, f16[1,144,128]{2,1,0:T(8,128)(2,1)S(1)}, u32[]{:S(2)}, u32[]{:S(2)}) collective-permute-start(f16[1,144,128]{2,1,0:T(8,128)(2,1)S(1)} %get-tuple-element.27), channel_id=1, source_target_pairs={{0,1},{1,0},{2,3},{3,2},{4,5},{5,4},{6,7},{7,6},{8,9},{9,8},{10,11... | collective-permute-start | bytes 110600 | tf_op jit(solution)/shard_map/ppermute | solution.py:37
  14.1 5.4 %collective-permute-start.7 = (f16[3,144,128]{2,1,0:T(8,128)(2,1)S(1)}, f16[3,144,128]{2,1,0:T(8,128)(2,1)S(1)}, u32[]{:S(2)}, u32[]{:S(2)}) collective-permute-start(f16[3,144,128]{2,1,0:T(8,128)(2,1)S(1)} %get-tuple-element.19), channel_id=1, source_target_pairs={{0,3},{1,2},{2,1},{3,0},{4,7},{5,6},{6,5},{7,4},{8,11},{9,10},{10,... | collective-permute-start | bytes 331784 | tf_op jit(solution)/shard_map/ppermute | solution.py:37
  14.8 4.8 %collective-permute-start.5 = (f16[3,144,128]{2,1,0:T(8,128)(2,1)S(1)}, f16[3,144,128]{2,1,0:T(8,128)(2,1)S(1)}, u32[]{:S(2)}, u32[]{:S(2)}) collective-permute-start(f16[3,144,128]{2,1,0:T(8,128)(2,1)S(1)} %get-tuple-element.21), channel_id=1, source_target_pairs={{0,1},{1,0},{2,3},{3,2},{4,5},{5,4},{6,7},{7,6},{8,9},{9,8},{10,11... | collective-permute-start | bytes 331784 | tf_op jit(solution)/shard_map/ppermute | solution.py:37
  15.1 6.8 %collective-permute-start.6 = (f16[3,144,128]{2,1,0:T(8,128)(2,1)S(1)}, f16[3,144,128]{2,1,0:T(8,128)(2,1)S(1)}, u32[]{:S(2)}, u32[]{:S(2)}) collective-permute-start(f16[3,144,128]{2,1,0:T(8,128)(2,1)S(1)} %get-tuple-element.22), channel_id=1, source_target_pairs={{0,2},{1,3},{2,0},{3,1},{4,6},{5,7},{6,4},{7,5},{8,10},{9,11},{10,... | collective-permute-start | bytes 331784 | tf_op jit(solution)/shard_map/ppermute | solution.py:37
  21.9 0.7 %copy-start.8 = (s32[1,1,2]{2,1,0:T(1,128)S(1)}, s32[1,1,2]{2,1,0:T(1,128)}, u32[]{:S(2)}) copy-start(s32[1,1,2]{2,1,0:T(1,128)} %refs_4_.3) | copy-start | bytes 28
  21.9 0.7 %copy-start.9 = (s32[1,1,2]{2,1,0:T(1,128)S(1)}, s32[1,1,2]{2,1,0:T(1,128)}, u32[]{:S(2)}) copy-start(s32[1,1,2]{2,1,0:T(1,128)} %refs_5_.3) | copy-start | bytes 28

commit v2 on v1

v2 whole, which is shorter than its diff:
```python
import functools

import jax
import jax.numpy as jnp
from jax import lax
from jax.experimental import pallas as pl
from jax.experimental.pallas import tpu as pltpu
from jax.sharding import PartitionSpec as P

LANES = 128
SCALE = 4096.0
MEGA = 1024 * 1024
VMEM = pl.BlockSpec(memory_space=pltpu.VMEM)
ANY = pl.BlockSpec(memory_space=pl.ANY)


def place(me, other, count):
    if count & (count - 1) == 0:
        return lax.bitwise_xor(me, other)
    return lax.rem(other - me + count, count)


def source(me, step, count):
    if count & (count - 1) == 0:
        return lax.bitwise_xor(me, step)
    return lax.rem(me - step + count, count)


def exchange(value, step, count):
    power = count & (count - 1) == 0
    return lax.ppermute(value, "lev", [(i, i ^ step if power else (i + step) % count) for i in range(count)])


def params(mega=16):
    return pltpu.CompilerParams(vmem_limit_bytes=mega * MEGA)


def cost(flops, moved):
    return pl.CostEstimate(flops=flops, bytes_accessed=moved, transcendentals=0)


def edge_kernel(fields, out):
    out[0] = fields[:, :, 0, :]
    out[1] = fields[:, :, fields.shape[2] - 1, :]


def edge_rows(fields):
    count, levels, _, lon = fields.shape
    return pl.pallas_call(
        edge_kernel,
        in_specs=[VMEM],
        out_specs=VMEM,
        out_shape=jax.ShapeDtypeStruct((2, count, levels, lon), fields.dtype),
        compiler_params=params(),
        name="edge_rows",
    )(fields)


def message_height(rows, count, levels):
    return rows * count * levels + -(-rows * count // 8) * 8


def store_message(message, index, rows, field, count, advected, share, groups, me):
    levels = advected.shape[0]
    flux = share * advected
    depth = lax.broadcasted_iota(jnp.int32, flux.shape, 0)
    above = jnp.where(depth == 0, 0.0, pltpu.roll(flux, 1, 0))
    remapped = advected - flux + above
    base = (index * count + field) * levels
    row = rows * count * levels + index * count + field
    for group in range(groups):
        where = place(me, group, groups)
        lanes = slice(group * LANES, (group + 1) * LANES)
        message[where, base : base + levels, :] = remapped[:, lanes]
        message[where, row : row + 1, :] = flux[levels - 1 :, lanes]


def moved_share(displacement, row, me, groups):
    share = displacement[:, row, :]
    depth = lax.broadcasted_iota(jnp.int32, share.shape, 0)
    bottom = jnp.logical_and(depth == share.shape[0] - 1, me == groups - 1)
    return jnp.where(bottom, 0.0, share)


def winds(courant):
    return jnp.maximum(courant, 0.0), jnp.minimum(courant, 0.0)


def along_row(here, east_wind, west_wind):
    lon = here.shape[-1]
    result = here - east_wind * (here - pltpu.roll(here, 1, 1))
    return result - west_wind * (pltpu.roll(here, lon - 1, 1) - here)


def inner_kernel(groups, fields, along_lon, along_lat, displacement, edges, message):
    count, _, rows, _ = fields.shape
    me = lax.axis_index("lev")
    for row in range(1, rows - 1):
        east_wind, west_wind = winds(along_lon[:, row, :])
        south_wind, north_wind = winds(along_lat[:, row, :])
        share = moved_share(displacement, row, me, groups)
        for field in range(count):
            here = fields[field, :, row, :]
            north = edges[0, field] if row == 1 else fields[field, :, row - 1, :]
            south = edges[1, field] if row == rows - 2 else fields[field, :, row + 1, :]
            result = along_row(here, east_wind, west_wind)
            result = result - south_wind * (here - north)
            result = result - north_wind * (south - here)
            store_message(message, row - 1, rows - 2, field, count, result, share, groups, me)


def inner_rows(fields, along_lon, along_lat, displacement, edges, groups):
    count, levels, rows, _ = fields.shape
    height = message_height(rows - 2, count, levels)
    return pl.pallas_call(
        functools.partial(inner_kernel, groups),
        in_specs=[VMEM] * 5,
        out_specs=VMEM,
        out_shape=jax.ShapeDtypeStruct((groups, height, LANES), jnp.float32),
        compiler_params=params(),
        cost_estimate=cost(1_000_000_000, 3_000_000),
        name="inner_rows",
    )(fields, along_lon, along_lat, displacement, edges)


def outer_kernel(groups, fields, along_lon, along_lat, displacement, edges, partial, weight, share):
    count, _, rows, _ = fields.shape
    me = lax.axis_index("lev")
    for index, row in enumerate((0, rows - 1)):
        east_wind, west_wind = winds(along_lon[:, row, :])
        south_wind, north_wind = winds(along_lat[:, row, :])
        weight[index] = south_wind if index == 0 else -north_wind
        share[index] = moved_share(displacement, row, me, groups)
        for field in range(count):
            here = edges[index, field]
            north = fields[field, :, row - 1, :] if index else 0.0
            south = 0.0 if index else fields[field, :, row + 1, :]
            result = along_row(here, east_wind, west_wind)
            result = result - south_wind * (here - north)
            partial[index, field] = result - north_wind * (south - here)


def outer_rows(fields, along_lon, along_lat, displacement, edges, groups):
    count, levels, _, lon = fields.shape
    f32 = jnp.float32
    return pl.pallas_call(
        functools.partial(outer_kernel, groups),
        in_specs=[VMEM] * 5,
        out_specs=[VMEM] * 3,
        out_shape=[
            jax.ShapeDtypeStruct((2, count, levels, lon), f32),
            jax.ShapeDtypeStruct((2, levels, lon), f32),
            jax.ShapeDtypeStruct((2, levels, lon), f32),
        ],
        compiler_params=params(),
        cost_estimate=cost(1_000_000_000, 3_000_000),
        name="outer_rows",
    )(fields, along_lon, along_lat, displacement, edges)


def finish_kernel(groups, partial, weight, share, north, south, _, message, unit):
    unit[...] = jnp.full(unit.shape, 1.0 / SCALE, jnp.float32)
    count = partial.shape[1]
    me = lax.axis_index("lev")
    for index, halo in enumerate((north, south)):
        wind, moved = weight[index], share[index]
        for field in range(count):
            advected = partial[index, field] + wind * halo[field]
            store_message(message, index, 2, field, count, advected, moved, groups, me)


def finish(partial, weight, share, north, south, after, groups):
    _, count, levels, _ = partial.shape
    return pl.pallas_call(
        functools.partial(finish_kernel, groups),
        in_specs=[VMEM] * 5 + [ANY],
        out_specs=[VMEM] * 2,
        out_shape=[
            jax.ShapeDtypeStruct((groups, message_height(2, count, levels), LANES), jnp.float32),
            jax.ShapeDtypeStruct((8, LANES), jnp.float32),
        ],
        compiler_params=params(),
        name="finish",
    )(partial, weight, share, north, south, after)


def turn_kernel(rows, _, own, lent, first, second, third, bias_first, bias_second, bias_third, *outs):
    for weight, out in zip((first, second, third), outs[:3]):
        out[...] = weight[...].T
    for bias, out in zip((bias_first, bias_second, bias_third), outs[3:6]):
        out[...] = jnp.broadcast_to(bias[...][None, :], (8, bias.shape[0])).T
    for row in range(rows):
        hits = jnp.logical_or(own[0] == row, lent[0] == row)
        active = jnp.max(jnp.where(hits, 1.0, 0.0), axis=1, keepdims=True)
        outs[6][row] = jnp.broadcast_to(active, (8, LANES))


def turned(after, own, lent, weights, biases, rows):
    f32 = jnp.float32
    shapes = [jax.ShapeDtypeStruct(w.shape[::-1], w.dtype) for w in weights]
    shapes += [jax.ShapeDtypeStruct((b.shape[0], 8), f32) for b in biases]
    shapes += [jax.ShapeDtypeStruct((rows, 8, LANES), f32)]
    return pl.pallas_call(
        functools.partial(turn_kernel, rows),
        in_specs=[ANY] + [VMEM] * 8,
        out_specs=[VMEM] * 7,
        out_shape=shapes,
        compiler_params=params(),
        cost_estimate=cost(1_000_000_000, 5_000_000),
        name="turned",
    )(after, own, lent, *weights, *biases)


def silu(value):
    half = 0.5 * value
    return half + half * jnp.tanh(half)


def layer(weight, bias, value, act):
    parts = []
    for start in range(0, weight.shape[0], 256):
        stop = min(start + 256, weight.shape[0])
        total = jnp.dot(weight[start:stop, :], value, preferred_element_type=jnp.float32)
        parts.append(act(total + bias[start:stop, 0:1]).astype(jnp.bfloat16))
    return jnp.concatenate(parts, axis=0)


def physics_kernel(groups, blocks, count, levels, aliased, *refs):
    parts, refs = refs[:groups], refs[groups:]
    first, second, third, bias_first, bias_second, bias_third, mask = refs[:7]
    out, columns, carried, staged, sem = refs[7 + aliased :]
    me = lax.axis_index("lev")
    depth = groups * levels
    many = len(blocks)
    tall = many * count * levels
    for step in range(groups):
        level = source(me, step, groups)
        part = parts[step]
        for index in range(many):
            for field in range(count):
                start = pl.multiple_of(field * depth + level * levels, levels)
                base = (index * count + field) * levels
                columns[index, pl.ds(start, levels), :] = part[base : base + levels, :]
        carried[level, 0 : many * count, :] = part[tall : tall + many * count, :]
    for index in range(many):
        for field in range(count):
            for level in range(1, groups):
                row = field * depth + level * levels
                line = index * count + field
                columns[index, row : row + 1, :] += carried[level - 1, line : line + 1, :]
    value = jnp.concatenate([columns[index].astype(jnp.bfloat16) for index in range(many)], axis=1)
    hidden = layer(first, bias_first, value, silu)
    hidden = layer(second, bias_second, hidden, silu)
    tendency = layer(third, bias_third, hidden, lambda v: v).astype(jnp.float32)
    copies = []
    for index, block in enumerate(blocks):
        part = tendency[:, index * LANES : (index + 1) * LANES]
        staged[index] = columns[index] + jnp.where(mask[block, 0:1, :] > 0.0, part, 0.0)
        copies.append(pltpu.make_async_copy(staged.at[index], out.at[:, block, :], sem.at[index]))
        copies[-1].start()
    for copy in copies:
        copy.wait()


def physics(parts, network, rows, blocks, count, levels, result=None):
    groups = len(parts)
    many = len(blocks)
    width = count * groups * levels
    f32 = jnp.float32
    aliased = result is not None
    operands = [*parts, *network]
    specs = [VMEM] * len(operands)
    if aliased:
        operands.append(result)
        specs.append(ANY)
    return pl.pallas_call(
        functools.partial(physics_kernel, groups, blocks, count, levels, int(aliased)),
        in_specs=specs,
        out_specs=ANY,
        out_shape=jax.ShapeDtypeStruct((width, rows, LANES), f32),
        scratch_shapes=[
            pltpu.VMEM((many, width, LANES), f32),
            pltpu.VMEM((groups, -(-many * count // 8) * 8, LANES), f32),
            pltpu.VMEM((many, width, LANES), f32),
            pltpu.SemaphoreType.DMA((many,)),
        ],
        input_output_aliases={len(operands) - 1: 0} if aliased else {},
        compiler_params=params(),
        cost_estimate=cost(20_000_000_000, 5_000_000),
        name="physics",
    )(*operands)


def body(
    fields,
    courant_lon,
    courant_lat,
    displacement,
    own_slot,
    lent_slot,
    w_first,
    bias_first,
    w_second,
    bias_second,
    w_third,
    bias_third,
):
    count, levels, rows, lon = fields.shape
    groups = lax.axis_size("lev")
    bands = lax.axis_size("lat")
    even = lax.axis_index("lat") % 2 == 0
    half = jnp.float16
    f32 = jnp.float32

    near_pairs = [(i, i ^ 1) for i in range(bands) if i ^ 1 < bands]
    far_pairs = [(i, i + 1 if i % 2 else i - 1) for i in range(bands)]
    far_pairs = [(i, j) for i, j in far_pairs if 0 <= j < bands]
    edges = edge_rows(fields)
    far = lax.ppermute((jnp.where(even, edges[0], edges[1]) * SCALE).astype(half), "lat", far_pairs)
    near = lax.ppermute((jnp.where(even, edges[1], edges[0]) * SCALE).astype(half), "lat", near_pairs)

    def swap(message):
        sent = [(message[step] * SCALE).astype(half) for step in range(1, groups)]
        return [exchange(value, step + 1, groups) for step, value in enumerate(sent)]

    def received(message, values, unit):
        return [message[0]] + [value.astype(f32) * unit[0:1, :] for value in values]

    inner = inner_rows(fields, courant_lon, courant_lat, displacement, edges, groups)
    inner_moved = swap(inner)
    partial, weight, share = outer_rows(fields, courant_lon, courant_lat, displacement, edges, groups)
    weights, biases = (w_first, w_second, w_third), (bias_first, bias_second, bias_third)
    network = turned(inner, own_slot, lent_slot, weights, biases, rows)
    north = jnp.where(even, far, near).astype(f32) * (1.0 / SCALE)
    south = jnp.where(even, near, far).astype(f32) * (1.0 / SCALE)
    outer, unit = finish(partial, weight, share, north, south, network[-1], groups)
    outer_moved = swap(outer)
    result = physics(received(inner, inner_moved, unit), network, rows, tuple(range(1, rows - 1)), count, levels)
    return physics(received(outer, outer_moved, jnp.full((1, LANES), 1.0 / SCALE, f32)), network, rows, (0, rows - 1), count, levels, result)


def solution(mesh):
    in_specs = (
        P(None, "lev", "lat", None),
        P("lev", "lat", None),
        P("lev", "lat", None),
        P("lev", "lat", None),
        P("lev", "lat", None),
        P("lev", "lat", None),
        P(),
        P(),
        P(),
        P(),
        P(),
        P(),
    )
    out_specs = P(None, "lat", "lev")
    return jax.shard_map(body, mesh=mesh, in_specs=in_specs, out_specs=out_specs, check_vma=False)
```

time: 28.5 us -> 20.2 us (0.71)
  the two profiles are of different devices: /device:TPU:23 before, /device:TPU:2 now
where the time goes in v2:
time: 20.2 us; the launch traced here: 20 us
  starting transfers between devices  8.95 us (44%)
  Pallas kernels  6.64 us (33%)
  local copies, waits for them, and re-layouts  1.97 us (10%)
  waiting for transfers between devices  1.89 us (9%)
  other arithmetic  0.31 us (2%)
  between operations  0.23 us (1%)
    ppermute x1, starting transfers between devices, body(): lax.ppermute((jnp.where(even, edges[0], edges[1]) * SCALE).astype(half),...  4.92 us
    pallas_call x2, Pallas kernels, physics(): pl.pallas_call(functools.partial(physics_kernel, groups, blocks, count, l...  4.06 us
    ppermute x6, starting transfers between devices, exchange(): lax.ppermute(value, 'lev', [(i, i ^ step if power else (i + step) % count...  3.95 us
    unnamed x24, local copies, waits for them, and re-layouts  1.96 us
    ppermute x6, waiting for transfers between devices, exchange(): lax.ppermute(value, 'lev', [(i, i ^ step if power else (i + step) % count...  1.88 us
    pallas_call x1, Pallas kernels, turned(): pl.pallas_call(functools.partial(turn_kernel, rows), in_specs=[ANY] + [VM...  0.99 us
    pallas_call x1, Pallas kernels, inner_rows(): pl.pallas_call(functools.partial(inner_kernel, groups), in_specs=[VMEM] *...  0.76 us
    pallas_call x1, Pallas kernels, outer_rows(): pl.pallas_call(functools.partial(outer_kernel, groups), in_specs=[VMEM] *...  0.54 us
  transfers between devices with their start and end apart: 8, of which 2 were waited for; matrix products, arithmetic and copies ran while one was open for 1% of the time, Pallas kernels for 23%

profile of v2, /device:TPU:2, one launch (start us, length us, event | category | flops | bytes accessed | tf_op | source)
XLA Modules:
  0.0 20.0 jit_solution(13743344386975976450)
XLA Ops:
  0.0 1.2 %copy-done = f32[4,32,4,512]{3,2,1,0:T(4,128)S(1)} copy-done((f32[4,32,4,512]{3,2,1,0:T(4,128)S(1)}, f32[4,32,4,512]{3,2,1,0:T(4,128)}, u32[]{:S(2)}) %copy-start) | copy-done | bytes 1048600
  1.2 0.1 edge_rows.1.edges
  1.3 0.0 copy-start.4
  1.3 0.0 copy-start.5
  1.4 0.0 copy-start.6
  1.4 0.1 fusion.4
  1.4 0.1 collective-permute-start.1
  1.5 4.9 %collective-permute-start = (f16[4,32,512]{2,1,0:T(8,128)(2,1)S(1)}, f16[4,32,512]{2,1,0:T(8,128)(2,1)S(1)}, u32[]{:S(2)}, u32[]{:S(2)}) collective-permute-start(f16[4,32,512]{2,1,0:T(8,128)(2,1)S(1)} %get-tuple-element.38), channel_id=1, source_target_pairs={{4,8},{8,4},{12,16},{16,12},{20,24},{24,20},{5,9},{9,5},{13,17},{1... | collective-permute-start | bytes 393224 | tf_op jit(solution)/shard_map/ppermute | solution.py:319
  6.5 0.8 %inner_rows.1._ = f32[4,264,128]{2,1,0:T(8,128)S(1)} custom-call(f32[4,32,4,512]{3,2,1,0:T(4,128)S(1)} %copy-done, f32[32,4,512]{2,1,0:T(4,128)S(1)} %copy-done.4, f32[32,4,512]{2,1,0:T(4,128)S(1)} %copy-done.5, f32[32,4,512]{2,1,0:T(4,128)S(1)} %copy-done.6, f32[2,4,32,512]{3,2,1,0:T(8,128)S(1)} %edge_rows.1.edges), custom_call_target="tpu_custom_call" | custom-call | flops 1000000000 | bytes 3000000 | tf_op jit(solution)/shard_map/inner_rows/pallas_call | solution.py:115
  7.3 0.5 %collective-permute-start.7 = (f16[264,128]{1,0:T(8,128)(2,1)S(1)}, f16[264,128]{1,0:T(8,128)(2,1)S(1)}, u32[]{:S(2)}, u32[]{:S(2)}) collective-permute-start(f16[264,128]{1,0:T(8,128)(2,1)S(1)} %get-tuple-element.29), channel_id=1, source_target_pairs={{0,3},{1,2},{2,1},{3,0},{4,7},{5,6},{6,5},{7,4},{8,11},{9,10},{10,... | collective-permute-start | bytes 202760 | tf_op jit(solution)/shard_map/ppermute | solution.py:31
  7.8 1.2 %collective-permute-start.6 = (f16[264,128]{1,0:T(8,128)(2,1)S(1)}, f16[264,128]{1,0:T(8,128)(2,1)S(1)}, u32[]{:S(2)}, u32[]{:S(2)}) collective-permute-start(f16[264,128]{1,0:T(8,128)(2,1)S(1)} %get-tuple-element.30), channel_id=1, source_target_pairs={{0,2},{1,3},{2,0},{3,1},{4,6},{5,7},{6,4},{7,5},{8,10},{9,11},{10,... | collective-permute-start | bytes 202760 | tf_op jit(solution)/shard_map/ppermute | solution.py:31
  9.0 0.0 copy-start.8
  9.0 0.0 copy-start.9
  9.0 0.0 copy-start.10
  9.0 0.0 copy-start.11
  9.0 0.3 %collective-permute-start.5 = (f16[264,128]{1,0:T(8,128)(2,1)S(1)}, f16[264,128]{1,0:T(8,128)(2,1)S(1)}, u32[]{:S(2)}, u32[]{:S(2)}) collective-permute-start(f16[264,128]{1,0:T(8,128)(2,1)S(1)} %get-tuple-element.31), channel_id=1, source_target_pairs={{0,1},{1,0},{2,3},{3,2},{4,5},{5,4},{6,7},{7,6},{8,9},{9,8},{10,11... | collective-permute-start | bytes 202760 | tf_op jit(solution)/shard_map/ppermute | solution.py:31
  9.4 0.5 %outer_rows.1 = (f32[2,4,32,512]{3,2,1,0:T(8,128)S(1)}, f32[2,32,512]{2,1,0:T(8,128)S(1)}, f32[2,32,512]{2,1,0:T(8,128)S(1)}) custom-call(f32[4,32,4,512]{3,2,1,0:T(4,128)S(1)} %copy-done, f32[32,4,512]{2,1,0:T(4,128)S(1)} %copy-done.4, f32[32,4,512]{2,1,0:T(4,128)S(1)} %copy-done.5, f32[32,4,512]{2,1,0:T(4,128)S(1)} %copy-done.6, ...), custom_call_target="tpu_custom_call" | custom-call | flops 1000000000 | bytes 3000000 | tf_op jit(solution)/shard_map/outer_rows/pallas_call | solution.py:146
  9.9 0.3 %copy-done.1 = bf16[768,640]{1,0:T(8,128)(2,1)S(1)} copy-done((bf16[768,640]{1,0:T(8,128)(2,1)S(1)}, bf16[768,640]{1,0:T(8,128)(2,1)}, u32[]{:S(2)}) %copy-start.1) | copy-done | bytes 983064
  10.2 0.2 %copy-done.2 = bf16[512,768]{1,0:T(8,128)(2,1)S(1)} copy-done((bf16[512,768]{1,0:T(8,128)(2,1)S(1)}, bf16[512,768]{1,0:T(8,128)(2,1)}, u32[]{:S(2)}) %copy-start.2) | copy-done | bytes 786456
  10.4 0.2 copy-done.3
  10.6 1.0 %turned.1 = (bf16[768,512]{1,0:T(8,128)(2,1)S(1)}, bf16[640,768]{1,0:T(8,128)(2,1)S(1)}, bf16[512,640]{1,0:T(8,128)(2,1)S(1)}, f32[768,8]{1,0:T(8,128)S(1)}, f32...) custom-call(f32[4,264,128]{2,1,0:T(8,128)S(1)} %inner_rows.1._, s32[1,1,2]{2,1,0:T(1,128)S(1)} %copy-done.10, ...), custom_call_target="tpu_custom_call" | custom-call | flops 1000000000 | bytes 5000000 | tf_op jit(solution)/shard_map/turned/pallas_call | solution.py:203
  11.6 0.0 collective-permute-done
  11.6 0.1 convert_multiply_fusion
  11.7 0.2 finish.1
  11.9 1.5 %collective-permute-start.4 = (f16[264,128]{1,0:T(8,128)(2,1)S(1)}, f16[264,128]{1,0:T(8,128)(2,1)S(1)}, u32[]{:S(2)}, u32[]{:S(2)}) collective-permute-start(f16[264,128]{1,0:T(8,128)(2,1)S(1)} %get-tuple-element.33), channel_id=1, source_target_pairs={{0,3},{1,2},{2,1},{3,0},{4,7},{5,6},{6,5},{7,4},{8,11},{9,10},{10,... | collective-permute-start | bytes 202760 | tf_op jit(solution)/shard_map/ppermute | solution.py:31
  13.4 0.5 %collective-permute-start.3 = (f16[264,128]{1,0:T(8,128)(2,1)S(1)}, f16[264,128]{1,0:T(8,128)(2,1)S(1)}, u32[]{:S(2)}, u32[]{:S(2)}) collective-permute-start(f16[264,128]{1,0:T(8,128)(2,1)S(1)} %get-tuple-element.34), channel_id=1, source_target_pairs={{0,2},{1,3},{2,0},{3,1},{4,6},{5,7},{6,4},{7,5},{8,10},{9,11},{10,... | collective-permute-start | bytes 202760 | tf_op jit(solution)/shard_map/ppermute | solution.py:31
  13.9 0.0 collective-permute-done.7
  13.9 0.0 collective-permute-start.2
  14.0 2.0 %physics.2.refs_11_ = f32[512,4,128]{2,1,0:T(4,128)} custom-call(f32[264,128]{1,0:T(8,128)S(1)} %get-tuple-element.32.refs_0_, f32[264,128]{1,0:T(8,128)S(1)} %get-tuple-element.43.refs_1_, f32[264,128]{1,0:T(8,128)S(1)} %get-tuple-element.42.refs_2_, f32[264,128]{1,0:T(8,128)S(1)} %get-tuple-element.41.refs_3_, ...), custom_call_target="tpu_custom_call" | custom-call | flops 20000000000 | bytes 5000000 | tf_op jit(solution)/shard_map/physics/pallas_call | solution.py:276
  16.0 0.1 collective-permute-done.4
  16.1 1.8 %collective-permute-done.3 = f16[264,128]{1,0:T(8,128)(2,1)S(1)} collective-permute-done((f16[264,128]{1,0:T(8,128)(2,1)S(1)}, f16[264,128]{1,0:T(8,128)(2,1)S(1)}, u32[]{:S(2)}, u32[]{:S(2)}) %collective-permute-start.3) | collective-permute-done | bytes 67616 | tf_op jit(solution)/shard_map/ppermute | solution.py:31
  17.9 2.0 %physics.3 = f32[512,4,128]{2,1,0:T(4,128)} custom-call(f32[264,128]{1,0:T(8,128)S(1)} %get-tuple-element.36.refs_0_, f32[264,128]{1,0:T(8,128)S(1)} %convert_multiply_fusion.7.refs_1_, f32[264,128]{1,0:T(8,128)S(1)} %convert_multiply_fusion.6.refs_2_, f32[264,128]{1,0:T(8,128)S(1)} %convert_multiply_fusion.5.refs_3_, ...), custom_call_target="tpu_custom_call", output_to_operand_aliasing={{}: (11, {})} | custom-call | flops 20000000000 | bytes 5000000 | tf_op jit(solution)/shard_map/physics/pallas_call | solution.py:276
  (24 shorter events, 0.2 us)
Async XLA Ops:
  0.0 1.2 %copy-start = (f32[4,32,4,512]{3,2,1,0:T(4,128)S(1)}, f32[4,32,4,512]{3,2,1,0:T(4,128)}, u32[]{:S(2)}) copy-start(f32[4,32,4,512]{3,2,1,0:T(4,128)} %fields.5) | copy-start | bytes 3145732
  1.3 5.1 %copy-start.4 = (f32[32,4,512]{2,1,0:T(4,128)S(1)}, f32[32,4,512]{2,1,0:T(4,128)}, u32[]{:S(2)}) copy-start(f32[32,4,512]{2,1,0:T(4,128)} %along_lon.3) | copy-start | bytes 786436
  1.3 5.1 %copy-start.5 = (f32[32,4,512]{2,1,0:T(4,128)S(1)}, f32[32,4,512]{2,1,0:T(4,128)}, u32[]{:S(2)}) copy-start(f32[32,4,512]{2,1,0:T(4,128)} %along_lat.3) | copy-start | bytes 786436
  1.4 5.1 %copy-start.6 = (f32[32,4,512]{2,1,0:T(4,128)S(1)}, f32[32,4,512]{2,1,0:T(4,128)}, u32[]{:S(2)}) copy-start(f32[32,4,512]{2,1,0:T(4,128)} %displacement.3) | copy-start | bytes 786436
  1.4 10.2 %collective-permute-start.1 = (f16[4,32,512]{2,1,0:T(8,128)(2,1)S(1)}, f16[4,32,512]{2,1,0:T(8,128)(2,1)S(1)}, u32[]{:S(2)}, u32[]{:S(2)}) collective-permute-start(f16[4,32,512]{2,1,0:T(8,128)(2,1)S(1)} %get-tuple-element.37), channel_id=1, source_target_pairs={{0,4},{4,0},{8,12},{12,8},{16,20},{20,16},{24,28},{28,24},{1,5},{5... | collective-permute-start | bytes 393224 | tf_op jit(solution)/shard_map/ppermute | solution.py:320
  1.5 10.1 %collective-permute-start = (f16[4,32,512]{2,1,0:T(8,128)(2,1)S(1)}, f16[4,32,512]{2,1,0:T(8,128)(2,1)S(1)}, u32[]{:S(2)}, u32[]{:S(2)}) collective-permute-start(f16[4,32,512]{2,1,0:T(8,128)(2,1)S(1)} %get-tuple-element.38), channel_id=1, source_target_pairs={{4,8},{8,4},{12,16},{16,12},{20,24},{24,20},{5,9},{9,5},{13,17},{1... | collective-permute-start | bytes 393224 | tf_op jit(solution)/shard_map/ppermute | solution.py:319
  7.3 6.6 %collective-permute-start.7 = (f16[264,128]{1,0:T(8,128)(2,1)S(1)}, f16[264,128]{1,0:T(8,128)(2,1)S(1)}, u32[]{:S(2)}, u32[]{:S(2)}) collective-permute-start(f16[264,128]{1,0:T(8,128)(2,1)S(1)} %get-tuple-element.29), channel_id=1, source_target_pairs={{0,3},{1,2},{2,1},{3,0},{4,7},{5,6},{6,5},{7,4},{8,11},{9,10},{10,... | collective-permute-start | bytes 202760 | tf_op jit(solution)/shard_map/ppermute | solution.py:31
  7.8 6.1 %collective-permute-start.6 = (f16[264,128]{1,0:T(8,128)(2,1)S(1)}, f16[264,128]{1,0:T(8,128)(2,1)S(1)}, u32[]{:S(2)}, u32[]{:S(2)}) collective-permute-start(f16[264,128]{1,0:T(8,128)(2,1)S(1)} %get-tuple-element.30), channel_id=1, source_target_pairs={{0,2},{1,3},{2,0},{3,1},{4,6},{5,7},{6,4},{7,5},{8,10},{9,11},{10,... | collective-permute-start | bytes 202760 | tf_op jit(solution)/shard_map/ppermute | solution.py:31
  9.0 1.2 %copy-start.1 = (bf16[768,640]{1,0:T(8,128)(2,1)S(1)}, bf16[768,640]{1,0:T(8,128)(2,1)}, u32[]{:S(2)}) copy-start(bf16[768,640]{1,0:T(8,128)(2,1)} %second.1) | copy-start | bytes 2949124
  9.0 1.4 %copy-start.2 = (bf16[512,768]{1,0:T(8,128)(2,1)S(1)}, bf16[512,768]{1,0:T(8,128)(2,1)}, u32[]{:S(2)}) copy-start(bf16[512,768]{1,0:T(8,128)(2,1)} %first.1) | copy-start | bytes 2359300
  9.0 1.6 %copy-start.3 = (bf16[640,512]{1,0:T(8,128)(2,1)S(1)}, bf16[640,512]{1,0:T(8,128)(2,1)}, u32[]{:S(2)}) copy-start(bf16[640,512]{1,0:T(8,128)(2,1)} %third.1) | copy-start | bytes 1966084
  9.0 1.6 %copy-start.7 = (f32[768]{0:T(1024)S(1)}, f32[768]{0:T(1024)}, u32[]{:S(2)}) copy-start(f32[768]{0:T(1024)} %bias_first.1) | copy-start | bytes 9220
  9.0 1.6 %copy-start.8 = (f32[640]{0:T(1024)S(1)}, f32[640]{0:T(1024)}, u32[]{:S(2)}) copy-start(f32[640]{0:T(1024)} %bias_second.1) | copy-start | bytes 7684
  9.0 1.6 %copy-start.9 = (f32[512]{0:T(512)S(1)}, f32[512]{0:T(512)}, u32[]{:S(2)}) copy-start(f32[512]{0:T(512)} %bias_third.1) | copy-start | bytes 6148
  9.0 1.6 %copy-start.10 = (s32[1,1,2]{2,1,0:T(1,128)S(1)}, s32[1,1,2]{2,1,0:T(1,128)}, u32[]{:S(2)}) copy-start(s32[1,1,2]{2,1,0:T(1,128)} %own.1) | copy-start | bytes 28
  9.0 1.6 %copy-start.11 = (s32[1,1,2]{2,1,0:T(1,128)S(1)}, s32[1,1,2]{2,1,0:T(1,128)}, u32[]{:S(2)}) copy-start(s32[1,1,2]{2,1,0:T(1,128)} %lent.1) | copy-start | bytes 28
  9.0 4.9 %collective-permute-start.5 = (f16[264,128]{1,0:T(8,128)(2,1)S(1)}, f16[264,128]{1,0:T(8,128)(2,1)S(1)}, u32[]{:S(2)}, u32[]{:S(2)}) collective-permute-start(f16[264,128]{1,0:T(8,128)(2,1)S(1)} %get-tuple-element.31), channel_id=1, source_target_pairs={{0,1},{1,0},{2,3},{3,2},{4,5},{5,4},{6,7},{7,6},{8,9},{9,8},{10,11... | collective-permute-start | bytes 202760 | tf_op jit(solution)/shard_map/ppermute | solution.py:31
  11.9 4.1 %collective-permute-start.4 = (f16[264,128]{1,0:T(8,128)(2,1)S(1)}, f16[264,128]{1,0:T(8,128)(2,1)S(1)}, u32[]{:S(2)}, u32[]{:S(2)}) collective-permute-start(f16[264,128]{1,0:T(8,128)(2,1)S(1)} %get-tuple-element.33), channel_id=1, source_target_pairs={{0,3},{1,2},{2,1},{3,0},{4,7},{5,6},{6,5},{7,4},{8,11},{9,10},{10,... | collective-permute-start | bytes 202760 | tf_op jit(solution)/shard_map/ppermute | solution.py:31
  13.4 4.5 %collective-permute-start.3 = (f16[264,128]{1,0:T(8,128)(2,1)S(1)}, f16[264,128]{1,0:T(8,128)(2,1)S(1)}, u32[]{:S(2)}, u32[]{:S(2)}) collective-permute-start(f16[264,128]{1,0:T(8,128)(2,1)S(1)} %get-tuple-element.34), channel_id=1, source_target_pairs={{0,2},{1,3},{2,0},{3,1},{4,6},{5,7},{6,4},{7,5},{8,10},{9,11},{10,... | collective-permute-start | bytes 202760 | tf_op jit(solution)/shard_map/ppermute | solution.py:31
  13.9 4.0 %collective-permute-start.2 = (f16[264,128]{1,0:T(8,128)(2,1)S(1)}, f16[264,128]{1,0:T(8,128)(2,1)S(1)}, u32[]{:S(2)}, u32[]{:S(2)}) collective-permute-start(f16[264,128]{1,0:T(8,128)(2,1)S(1)} %get-tuple-element.35), channel_id=1, source_target_pairs={{0,1},{1,0},{2,3},{3,2},{4,5},{5,4},{6,7},{7,6},{8,9},{9,8},{10,11... | collective-permute-start | bytes 202760 | tf_op jit(solution)/shard_map/ppermute | solution.py:31

commit v3 on v2

v3 whole, which is shorter than its diff:
```python
import functools

import jax
import jax.numpy as jnp
from jax import lax
from jax.experimental import pallas as pl
from jax.experimental.pallas import tpu as pltpu
from jax.sharding import PartitionSpec as P

LANES = 128
SCALE = 4096.0
MEGA = 1024 * 1024
VMEM = pl.BlockSpec(memory_space=pltpu.VMEM)
ANY = pl.BlockSpec(memory_space=pl.ANY)


def place(me, other, count):
    if count & (count - 1) == 0:
        return lax.bitwise_xor(me, other)
    return lax.rem(other - me + count, count)


def source(me, step, count):
    if count & (count - 1) == 0:
        return lax.bitwise_xor(me, step)
    return lax.rem(me - step + count, count)


def exchange(value, step, count):
    power = count & (count - 1) == 0
    return lax.ppermute(value, "lev", [(i, i ^ step if power else (i + step) % count) for i in range(count)])


def params(mega=16):
    return pltpu.CompilerParams(vmem_limit_bytes=mega * MEGA)


def cost(flops, moved):
    return pl.CostEstimate(flops=flops, bytes_accessed=moved, transcendentals=0)


def edge_kernel(fields, out):
    out[0] = fields[:, :, 0, :]
    out[1] = fields[:, :, fields.shape[2] - 1, :]


def edge_rows(fields):
    count, levels, _, lon = fields.shape
    return pl.pallas_call(
        edge_kernel,
        in_specs=[VMEM],
        out_specs=VMEM,
        out_shape=jax.ShapeDtypeStruct((2, count, levels, lon), fields.dtype),
        compiler_params=params(),
        name="edge_rows",
    )(fields)


def message_height(rows, count, levels):
    return rows * count * levels + -(-rows * count // 8) * 8


def store_message(message, index, rows, field, count, advected, share, groups, me):
    levels = advected.shape[0]
    flux = share * advected
    depth = lax.broadcasted_iota(jnp.int32, flux.shape, 0)
    above = jnp.where(depth == 0, 0.0, pltpu.roll(flux, 1, 0))
    remapped = advected - flux + above
    base = (index * count + field) * levels
    row = rows * count * levels + index * count + field
    for group in range(groups):
        where = place(me, group, groups)
        lanes = slice(group * LANES, (group + 1) * LANES)
        message[where, base : base + levels, :] = remapped[:, lanes]
        message[where, row : row + 1, :] = flux[levels - 1 :, lanes]


def moved_share(displacement, row, me, groups):
    share = displacement[:, row, :]
    depth = lax.broadcasted_iota(jnp.int32, share.shape, 0)
    bottom = jnp.logical_and(depth == share.shape[0] - 1, me == groups - 1)
    return jnp.where(bottom, 0.0, share)


def winds(courant):
    return jnp.maximum(courant, 0.0), jnp.minimum(courant, 0.0)


def along_row(here, east_wind, west_wind):
    lon = here.shape[-1]
    result = here - east_wind * (here - pltpu.roll(here, 1, 1))
    return result - west_wind * (pltpu.roll(here, lon - 1, 1) - here)


def local_kernel(groups, inner, fields, along_lon, along_lat, displacement, edges, *outs):
    count, _, rows, _ = fields.shape
    me = lax.axis_index("lev")

    def line(row, field):
        return edges[int(row > 0), field] if row in (0, rows - 1) else fields[field, :, row, :]

    for row in range(1, rows - 1) if inner else (0, rows - 1):
        east_wind, west_wind = winds(along_lon[:, row, :])
        south_wind, north_wind = winds(along_lat[:, row, :])
        moved = moved_share(displacement, row, me, groups)
        index = int(row > 0)
        if not inner:
            outs[1][index] = -north_wind if row else south_wind
            outs[2][index] = moved
        for field in range(count):
            here = line(row, field)
            north = line(row - 1, field) if row else 0.0
            south = line(row + 1, field) if row < rows - 1 else 0.0
            result = along_row(here, east_wind, west_wind)
            result = result - south_wind * (here - north)
            result = result - north_wind * (south - here)
            if inner:
                store_message(outs[0], row - 1, rows - 2, field, count, result, moved, groups, me)
            else:
                outs[0][index, field] = result


def local_rows(inner, fields, along_lon, along_lat, displacement, edges, groups):
    count, levels, rows, lon = fields.shape
    f32 = jnp.float32
    shapes = [
        jax.ShapeDtypeStruct((2, count, levels, lon), f32),
        jax.ShapeDtypeStruct((2, levels, lon), f32),
        jax.ShapeDtypeStruct((2, levels, lon), f32),
    ]
    if inner:
        shapes = [jax.ShapeDtypeStruct((groups, message_height(rows - 2, count, levels), LANES), f32)]
    return pl.pallas_call(
        functools.partial(local_kernel, groups, inner),
        in_specs=[VMEM] * 5,
        out_specs=[VMEM] * len(shapes),
        out_shape=shapes,
        compiler_params=params(),
        cost_estimate=cost(1_000_000_000, 3_000_000),
        name="inner_rows" if inner else "outer_rows",
    )(fields, along_lon, along_lat, displacement, edges)


def finish_kernel(groups, partial, weight, share, north, south, *refs):
    message, unit = refs[-2:]
    count = partial.shape[1]
    me = lax.axis_index("lev")
    unit[...] = jnp.full(unit.shape, 1.0 / SCALE, jnp.float32)
    for index, halo in enumerate((north, south)):
        wind, moved = weight[index], share[index]
        for field in range(count):
            advected = partial[index, field] + wind * halo[field]
            store_message(message, index, 2, field, count, advected, moved, groups, me)


def finish(partial, weight, share, north, south, after, groups):
    _, count, levels, _ = partial.shape
    f32 = jnp.float32
    return pl.pallas_call(
        functools.partial(finish_kernel, groups),
        in_specs=[VMEM] * (5 + len(after)),
        out_specs=[VMEM] * 2,
        out_shape=[
            jax.ShapeDtypeStruct((groups, message_height(2, count, levels), LANES), f32),
            jax.ShapeDtypeStruct((8, LANES), f32),
        ],
        compiler_params=params(),
        name="finish",
    )(partial, weight, share, north, south, *after)


def silu(value):
    half = 0.5 * value
    return half + half * jnp.tanh(half)


def layer(value, weight, bias, act):
    width = weight.shape[1]
    parts = []
    for start in range(0, width, 256):
        stop = min(start + 256, width)
        total = jnp.dot(value, weight[:, start:stop], preferred_element_type=jnp.float32)
        parts.append(act(total + bias[:, start:stop]).astype(jnp.bfloat16))
    return jnp.concatenate(parts, axis=1)


def active(own, lent, row):
    hits = jnp.logical_or(own[0] == row, lent[0] == row)
    return jnp.max(jnp.where(hits, 1.0, 0.0), axis=1, keepdims=True)


def physics_kernel(groups, helds, blocks, count, levels, aliased, *refs):
    sets = [refs[index * groups : (index + 1) * groups] for index in range(len(helds))]
    refs = refs[len(helds) * groups :]
    own, lent, first, bias_first, second, bias_second, third, bias_third = refs[:8]
    outs = refs[8 + aliased :]
    out, columns, carried, staged, sem = outs[0], *outs[-4:]
    if not aliased:
        outs[1][...] = jnp.full(outs[1].shape, 1.0 / SCALE, jnp.float32)
    me = lax.axis_index("lev")
    odd = lax.rem(lax.axis_index("lat"), 2)
    depth = groups * levels
    many = len(blocks)
    at = 0
    for parts, held in zip(sets, helds):
        tall = held * count * levels
        for step in range(groups):
            level = source(me, step, groups)
            part = parts[step]
            for index in range(held):
                for field in range(count):
                    start = pl.multiple_of(field * depth + level * levels, levels)
                    base = (index * count + field) * levels
                    columns[at + index, pl.ds(start, levels), :] = part[base : base + levels, :]
                low = tall + index * count
                carried[level, (at + index) * count : (at + index + 1) * count, :] = part[low : low + count, :]
        at += held
    for index in range(many):
        for field in range(count):
            for level in range(1, groups):
                row = field * depth + level * levels
                line = index * count + field
                columns[index, row : row + 1, :] += carried[level - 1, line : line + 1, :]
    value = jnp.concatenate([columns[index].astype(jnp.bfloat16) for index in range(many)], axis=1).T
    hidden = layer(value, first, bias_first, silu)
    hidden = layer(hidden, second, bias_second, silu)
    tendency = layer(hidden, third, bias_third, lambda v: v).T.astype(jnp.float32)

    def send(index, row):
        return pltpu.make_async_copy(staged.at[index], out.at[:, row, :], sem.at[index])

    for index, block in enumerate(blocks):
        part = tendency[:, index * LANES : (index + 1) * LANES]
        row = block[0] if block[0] == block[1] else jnp.where(odd == 1, block[1], block[0])
        staged[index] = columns[index] + jnp.where(active(own, lent, row) > 0.0, part, 0.0)
        if block[0] == block[1]:
            send(index, row).start()
            continue
        for parity in range(2):

            @pl.when(odd == parity)
            def _():
                send(index, block[parity]).start()

    for index, block in enumerate(blocks):
        send(index, block[0]).wait()


def physics(sets, network, rows, blocks, count, levels, result=None):
    groups = len(sets[0])
    many = len(blocks)
    width = count * groups * levels
    f32 = jnp.float32
    aliased = int(result is not None)
    unit = jax.ShapeDtypeStruct((8, LANES), f32)
    helds = [parts[0].shape[0] // (count * levels) for parts in sets]
    operands = [part for parts in sets for part in parts] + list(network)
    specs = [VMEM] * len(operands)
    if aliased:
        operands.append(result)
        specs.append(ANY)
    return pl.pallas_call(
        functools.partial(physics_kernel, groups, helds, blocks, count, levels, aliased),
        in_specs=specs,
        out_specs=[ANY] + [VMEM] * (1 - aliased),
        out_shape=[jax.ShapeDtypeStruct((width, rows, LANES), f32)] + [unit] * (1 - aliased),
        scratch_shapes=[
            pltpu.VMEM((many, width, LANES), f32),
            pltpu.VMEM((groups, -(-many * count // 8) * 8, LANES), f32),
            pltpu.VMEM((many, width, LANES), f32),
            pltpu.SemaphoreType.DMA((many,)),
        ],
        input_output_aliases={len(operands) - 1: 0} if aliased else {},
        compiler_params=params(),
        cost_estimate=cost(20_000_000_000, 5_000_000),
        name="physics",
    )(*operands)


def body(
    fields,
    courant_lon,
    courant_lat,
    displacement,
    own_slot,
    lent_slot,
    w_first,
    bias_first,
    w_second,
    bias_second,
    w_third,
    bias_third,
):
    count, levels, rows, lon = fields.shape
    groups = lax.axis_size("lev")
    bands = lax.axis_size("lat")
    even = lax.axis_index("lat") % 2 == 0
    half = jnp.float16
    f32 = jnp.float32

    near_pairs = [(i, i ^ 1) for i in range(bands) if i ^ 1 < bands]
    far_pairs = [(i, i + 1 if i % 2 else i - 1) for i in range(bands)]
    far_pairs = [(i, j) for i, j in far_pairs if 0 <= j < bands]
    edges = edge_rows(fields)
    far = lax.ppermute((jnp.where(even, edges[0], edges[1]) * SCALE).astype(half), "lat", far_pairs)
    near = lax.ppermute((jnp.where(even, edges[1], edges[0]) * SCALE).astype(half), "lat", near_pairs)

    def swap(message):
        sent = [(message[step] * SCALE).astype(half) for step in range(1, groups)]
        return [exchange(value, step + 1, groups) for step, value in enumerate(sent)]

    def received(message, values, unit):
        return [message[0]] + [value.astype(f32) * unit for value in values]

    local = (fields, courant_lon, courant_lat, displacement, edges, groups)
    network = (
        own_slot, lent_slot, w_first, bias_first.reshape(1, -1), w_second, bias_second.reshape(1, -1),
        w_third, bias_third.reshape(1, -1),
    )
    (inner,) = local_rows(True, *local)
    inner_moved = swap(inner)
    outer = local_rows(False, *local)
    north = jnp.where(even, far, near).astype(f32) * (1.0 / SCALE)
    south = jnp.where(even, near, far).astype(f32) * (1.0 / SCALE)
    message, unit = finish(*outer, north, south, (), groups)
    moved = swap(message)
    blocks = tuple((row, row) for row in range(1, rows - 1))
    sets = (received(inner, inner_moved, unit[0:1, :]),)
    result, unit = physics(sets, network, rows, blocks, count, levels)
    sets = (received(message, moved, unit[0:1, :]),)
    return physics(sets, network, rows, ((0, 0), (rows - 1, rows - 1)), count, levels, result)[0]


def solution(mesh):
    in_specs = (
        P(None, "lev", "lat", None),
        P("lev", "lat", None),
        P("lev", "lat", None),
        P("lev", "lat", None),
        P("lev", "lat", None),
        P("lev", "lat", None),
        P(),
        P(),
        P(),
        P(),
        P(),
        P(),
    )
    out_specs = P(None, "lat", "lev")
    return jax.shard_map(body, mesh=mesh, in_specs=in_specs, out_specs=out_specs, check_vma=False)
```

time: 20.2 us -> 19.4 us (0.960)
  the two profiles are of different devices: /device:TPU:2 before, /device:TPU:9 now
where the time goes in v3:
time: 19.4 us; the launch traced here: 19.2 us
  starting transfers between devices  9.99 us (51%)
  Pallas kernels  5.28 us (27%)
  local copies, waits for them, and re-layouts  2.11 us (11%)
  waiting for transfers between devices  1.24 us (6%)
  other arithmetic  0.29 us (1%)
  between operations  0.25 us (1%)
    ppermute x6, starting transfers between devices, exchange(): lax.ppermute(value, 'lev', [(i, i ^ step if power else (i + step) % count...  6.77 us
    pallas_call x2, Pallas kernels, physics(): pl.pallas_call(functools.partial(physics_kernel, groups, helds, blocks, c...  3.71 us
    unnamed x24, local copies, waits for them, and re-layouts  2.1 us
    ppermute x1, starting transfers between devices, body(): lax.ppermute((jnp.where(even, edges[0], edges[1]) * SCALE).astype(half),...  1.94 us
    pallas_call x2, Pallas kernels, local_rows(): pl.pallas_call(functools.partial(local_kernel, groups, inner), in_specs=[...  1.3 us
    ppermute x1, starting transfers between devices, body(): lax.ppermute((jnp.where(even, edges[1], edges[0]) * SCALE).astype(half),...  1.28 us
    ppermute x6, waiting for transfers between devices, exchange(): lax.ppermute(value, 'lev', [(i, i ^ step if power else (i + step) % count...  1.21 us
  transfers between devices with their start and end apart: 8, of which 1 were waited for; matrix products, arithmetic and copies ran while one was open for 1% of the time, Pallas kernels for 17%

profile of v3, /device:TPU:9, one launch (start us, length us, event | category | flops | bytes accessed | tf_op | source)
XLA Modules:
  0.0 19.2 jit_solution(11504467153825566986)
XLA Ops:
  0.0 1.2 %copy-done = f32[4,32,4,512]{3,2,1,0:T(4,128)S(1)} copy-done((f32[4,32,4,512]{3,2,1,0:T(4,128)S(1)}, f32[4,32,4,512]{3,2,1,0:T(4,128)}, u32[]{:S(2)}) %copy-start) | copy-done | bytes 1048600
  1.2 0.1 edge_rows.1.edges
  1.3 0.0 copy-start.4
  1.3 0.0 copy-start.5
  1.4 0.0 copy-start.6
  1.4 0.1 fusion.4
  1.4 1.3 %collective-permute-start.1 = (f16[4,32,512]{2,1,0:T(8,128)(2,1)S(1)}, f16[4,32,512]{2,1,0:T(8,128)(2,1)S(1)}, u32[]{:S(2)}, u32[]{:S(2)}) collective-permute-start(f16[4,32,512]{2,1,0:T(8,128)(2,1)S(1)} %get-tuple-element.27), channel_id=1, source_target_pairs={{0,4},{4,0},{8,12},{12,8},{16,20},{20,16},{24,28},{28,24},{1,5},{5... | collective-permute-start | bytes 393224 | tf_op jit(solution)/shard_map/ppermute | solution.py:306
  2.7 1.9 %collective-permute-start = (f16[4,32,512]{2,1,0:T(8,128)(2,1)S(1)}, f16[4,32,512]{2,1,0:T(8,128)(2,1)S(1)}, u32[]{:S(2)}, u32[]{:S(2)}) collective-permute-start(f16[4,32,512]{2,1,0:T(8,128)(2,1)S(1)} %get-tuple-element.28), channel_id=1, source_target_pairs={{4,8},{8,4},{12,16},{16,12},{20,24},{24,20},{5,9},{9,5},{13,17},{1... | collective-permute-start | bytes 393224 | tf_op jit(solution)/shard_map/ppermute | solution.py:305
  4.7 0.8 %inner_rows.1 = f32[4,264,128]{2,1,0:T(8,128)S(1)} custom-call(f32[4,32,4,512]{3,2,1,0:T(4,128)S(1)} %copy-done, f32[32,4,512]{2,1,0:T(4,128)S(1)} %copy-done.4, f32[32,4,512]{2,1,0:T(4,128)S(1)} %copy-done.5, f32[32,4,512]{2,1,0:T(4,128)S(1)} %copy-done.6, f32[2,4,32,512]{3,2,1,0:T(8,128)S(1)} %edge_rows.1.edges), custom_call_target="tpu_custom_call" | custom-call | flops 1000000000 | bytes 3000000 | tf_op jit(solution)/shard_map/inner_rows/pallas_call | solution.py:133
  5.5 0.0 copy-start.11
  5.5 2.5 %collective-permute-start.5 = (f16[264,128]{1,0:T(8,128)(2,1)S(1)}, f16[264,128]{1,0:T(8,128)(2,1)S(1)}, u32[]{:S(2)}, u32[]{:S(2)}) collective-permute-start(f16[264,128]{1,0:T(8,128)(2,1)S(1)} %get-tuple-element.23), channel_id=1, source_target_pairs={{0,3},{1,2},{2,1},{3,0},{4,7},{5,6},{6,5},{7,4},{8,11},{9,10},{10,... | collective-permute-start | bytes 202760 | tf_op jit(solution)/shard_map/ppermute | solution.py:31
  8.1 0.0 collective-permute-start.4
  8.1 0.5 %collective-permute-start.3 = (f16[264,128]{1,0:T(8,128)(2,1)S(1)}, f16[264,128]{1,0:T(8,128)(2,1)S(1)}, u32[]{:S(2)}, u32[]{:S(2)}) collective-permute-start(f16[264,128]{1,0:T(8,128)(2,1)S(1)} %get-tuple-element.25), channel_id=1, source_target_pairs={{0,1},{1,0},{2,3},{3,2},{4,5},{5,4},{6,7},{7,6},{8,9},{9,8},{10,11... | collective-permute-start | bytes 202760 | tf_op jit(solution)/shard_map/ppermute | solution.py:31
  8.5 0.2 %copy-done.10 = f32[768]{0:T(1024)S(1)} copy-done((f32[768]{0:T(1024)S(1)}, f32[768]{0:T(1024)}, u32[]{:S(2)}) %copy-start.10) | copy-done | bytes 3096
  8.7 0.5 %outer_rows.1 = (f32[2,4,32,512]{3,2,1,0:T(8,128)S(1)}, f32[2,32,512]{2,1,0:T(8,128)S(1)}, f32[2,32,512]{2,1,0:T(8,128)S(1)}) custom-call(f32[4,32,4,512]{3,2,1,0:T(4,128)S(1)} %copy-done, f32[32,4,512]{2,1,0:T(4,128)S(1)} %copy-done.4, f32[32,4,512]{2,1,0:T(4,128)S(1)} %copy-done.5, f32[32,4,512]{2,1,0:T(4,128)S(1)} %copy-done.6, ...), custom_call_target="tpu_custom_call" | custom-call | flops 1000000000 | bytes 3000000 | tf_op jit(solution)/shard_map/outer_rows/pallas_call | solution.py:133
  9.3 0.0 collective-permute-done
  9.3 0.1 convert_multiply_fusion
  9.4 0.0 copy-start.2
  9.4 0.0 copy-start.3
  9.4 0.2 finish.1
  9.6 0.0 copy-start.1
  9.7 3.3 %collective-permute-start.7 = (f16[264,128]{1,0:T(8,128)(2,1)S(1)}, f16[264,128]{1,0:T(8,128)(2,1)S(1)}, u32[]{:S(2)}, u32[]{:S(2)}) collective-permute-start(f16[264,128]{1,0:T(8,128)(2,1)S(1)} %get-tuple-element.19), channel_id=1, source_target_pairs={{0,3},{1,2},{2,1},{3,0},{4,7},{5,6},{6,5},{7,4},{8,11},{9,10},{10,... | collective-permute-start | bytes 202760 | tf_op jit(solution)/shard_map/ppermute | solution.py:31
  13.0 0.2 %collective-permute-start.6 = (f16[264,128]{1,0:T(8,128)(2,1)S(1)}, f16[264,128]{1,0:T(8,128)(2,1)S(1)}, u32[]{:S(2)}, u32[]{:S(2)}) collective-permute-start(f16[264,128]{1,0:T(8,128)(2,1)S(1)} %get-tuple-element.20), channel_id=1, source_target_pairs={{0,2},{1,3},{2,0},{3,1},{4,6},{5,7},{6,4},{7,5},{8,10},{9,11},{10,... | collective-permute-start | bytes 202760 | tf_op jit(solution)/shard_map/ppermute | solution.py:31
  13.2 0.0 collective-permute-done.5
  13.2 0.2 %collective-permute-start.2 = (f16[264,128]{1,0:T(8,128)(2,1)S(1)}, f16[264,128]{1,0:T(8,128)(2,1)S(1)}, u32[]{:S(2)}, u32[]{:S(2)}) collective-permute-start(f16[264,128]{1,0:T(8,128)(2,1)S(1)} %get-tuple-element.21), channel_id=1, source_target_pairs={{0,1},{1,0},{2,3},{3,2},{4,5},{5,4},{6,7},{7,6},{8,9},{9,8},{10,11... | collective-permute-start | bytes 202760 | tf_op jit(solution)/shard_map/ppermute | solution.py:31
  13.5 0.0 copy-start.7
  13.5 0.0 copy-start.8
  13.5 0.0 copy-start.9
  13.6 0.6 %copy-done.7 = f32[512]{0:T(512)S(1)} copy-done((f32[512]{0:T(512)S(1)}, f32[512]{0:T(512)}, u32[]{:S(2)}) %copy-start.7) | copy-done | bytes 2072
  14.2 1.9 %physics.2 = (f32[512,4,128]{2,1,0:T(4,128)}, f32[8,128]{1,0:T(8,128)S(1)}) custom-call(f32[264,128]{1,0:T(8,128)S(1)} %get-tuple-element.26.refs_0_, f32[264,128]{1,0:T(8,128)S(1)} %get-tuple-element.36.refs_1_, f32[264,128]{1,0:T(8,128)S(1)} %get-tuple-element.35.refs_2_, f32[264,128]{1,0:T(8,128)S(1)} %get-tuple-element.34.refs_3_, ...), custom_call_target="tpu_custom_call" | custom-call | flops 20000000000 | bytes 5000000 | tf_op jit(solution)/shard_map/physics/pallas_call | solution.py:262
  16.1 1.2 %collective-permute-done.6 = f16[264,128]{1,0:T(8,128)(2,1)S(1)} collective-permute-done((f16[264,128]{1,0:T(8,128)(2,1)S(1)}, f16[264,128]{1,0:T(8,128)(2,1)S(1)}, u32[]{:S(2)}, u32[]{:S(2)}) %collective-permute-start.6) | collective-permute-done | bytes 67616 | tf_op jit(solution)/shard_map/ppermute | solution.py:31
  17.3 1.9 %physics.3 = f32[512,4,128]{2,1,0:T(4,128)} custom-call(f32[264,128]{1,0:T(8,128)S(1)} %get-tuple-element.22.refs_0_, f32[264,128]{1,0:T(8,128)S(1)} %get-tuple-element.33.refs_1_, f32[264,128]{1,0:T(8,128)S(1)} %get-tuple-element.32.refs_2_, f32[264,128]{1,0:T(8,128)S(1)} %get-tuple-element.31.refs_3_, ...), custom_call_target="tpu_custom_call", output_to_operand_aliasing={{}: (12, {})} | custom-call | flops 20000000000 | bytes 5000000 | tf_op jit(solution)/shard_map/physics/pallas_call | solution.py:262
  (24 shorter events, 0.2 us)
Async XLA Ops:
  0.0 1.2 %copy-start = (f32[4,32,4,512]{3,2,1,0:T(4,128)S(1)}, f32[4,32,4,512]{3,2,1,0:T(4,128)}, u32[]{:S(2)}) copy-start(f32[4,32,4,512]{3,2,1,0:T(4,128)} %fields.5) | copy-start | bytes 3145732
  1.3 3.3 %copy-start.4 = (f32[32,4,512]{2,1,0:T(4,128)S(1)}, f32[32,4,512]{2,1,0:T(4,128)}, u32[]{:S(2)}) copy-start(f32[32,4,512]{2,1,0:T(4,128)} %along_lon.3) | copy-start | bytes 786436
  1.3 3.3 %copy-start.5 = (f32[32,4,512]{2,1,0:T(4,128)S(1)}, f32[32,4,512]{2,1,0:T(4,128)}, u32[]{:S(2)}) copy-start(f32[32,4,512]{2,1,0:T(4,128)} %along_lat.3) | copy-start | bytes 786436
  1.4 3.3 %copy-start.6 = (f32[32,4,512]{2,1,0:T(4,128)S(1)}, f32[32,4,512]{2,1,0:T(4,128)}, u32[]{:S(2)}) copy-start(f32[32,4,512]{2,1,0:T(4,128)} %displacement.3) | copy-start | bytes 786436
  1.4 7.8 %collective-permute-start.1 = (f16[4,32,512]{2,1,0:T(8,128)(2,1)S(1)}, f16[4,32,512]{2,1,0:T(8,128)(2,1)S(1)}, u32[]{:S(2)}, u32[]{:S(2)}) collective-permute-start(f16[4,32,512]{2,1,0:T(8,128)(2,1)S(1)} %get-tuple-element.27), channel_id=1, source_target_pairs={{0,4},{4,0},{8,12},{12,8},{16,20},{20,16},{24,28},{28,24},{1,5},{5... | collective-permute-start | bytes 393224 | tf_op jit(solution)/shard_map/ppermute | solution.py:306
  2.7 6.6 %collective-permute-start = (f16[4,32,512]{2,1,0:T(8,128)(2,1)S(1)}, f16[4,32,512]{2,1,0:T(8,128)(2,1)S(1)}, u32[]{:S(2)}, u32[]{:S(2)}) collective-permute-start(f16[4,32,512]{2,1,0:T(8,128)(2,1)S(1)} %get-tuple-element.28), channel_id=1, source_target_pairs={{4,8},{8,4},{12,16},{16,12},{20,24},{24,20},{5,9},{9,5},{13,17},{1... | collective-permute-start | bytes 393224 | tf_op jit(solution)/shard_map/ppermute | solution.py:305
  5.5 3.0 %copy-start.11 = (f32[640]{0:T(1024)S(1)}, f32[640]{0:T(1024)}, u32[]{:S(2)}) copy-start(f32[640]{0:T(1024)} %param.21) | copy-start | bytes 7684
  5.5 7.7 %collective-permute-start.5 = (f16[264,128]{1,0:T(8,128)(2,1)S(1)}, f16[264,128]{1,0:T(8,128)(2,1)S(1)}, u32[]{:S(2)}, u32[]{:S(2)}) collective-permute-start(f16[264,128]{1,0:T(8,128)(2,1)S(1)} %get-tuple-element.23), channel_id=1, source_target_pairs={{0,3},{1,2},{2,1},{3,0},{4,7},{5,6},{6,5},{7,4},{8,11},{9,10},{10,... | collective-permute-start | bytes 202760 | tf_op jit(solution)/shard_map/ppermute | solution.py:31
  8.1 0.7 %copy-start.10 = (f32[768]{0:T(1024)S(1)}, f32[768]{0:T(1024)}, u32[]{:S(2)}) copy-start(f32[768]{0:T(1024)} %param.19) | copy-start | bytes 9220
  8.1 5.4 %collective-permute-start.4 = (f16[264,128]{1,0:T(8,128)(2,1)S(1)}, f16[264,128]{1,0:T(8,128)(2,1)S(1)}, u32[]{:S(2)}, u32[]{:S(2)}) collective-permute-start(f16[264,128]{1,0:T(8,128)(2,1)S(1)} %get-tuple-element.24), channel_id=1, source_target_pairs={{0,2},{1,3},{2,0},{3,1},{4,6},{5,7},{6,4},{7,5},{8,10},{9,11},{10,... | collective-permute-start | bytes 202760 | tf_op jit(solution)/shard_map/ppermute | solution.py:31
  8.1 5.4 %collective-permute-start.3 = (f16[264,128]{1,0:T(8,128)(2,1)S(1)}, f16[264,128]{1,0:T(8,128)(2,1)S(1)}, u32[]{:S(2)}, u32[]{:S(2)}) collective-permute-start(f16[264,128]{1,0:T(8,128)(2,1)S(1)} %get-tuple-element.25), channel_id=1, source_target_pairs={{0,1},{1,0},{2,3},{3,2},{4,5},{5,4},{6,7},{7,6},{8,9},{9,8},{10,11... | collective-permute-start | bytes 202760 | tf_op jit(solution)/shard_map/ppermute | solution.py:31
  9.4 4.1 %copy-start.2 = (bf16[512,768]{1,0:T(8,128)(2,1)S(1)}, bf16[512,768]{1,0:T(8,128)(2,1)}, u32[]{:S(2)}) copy-start(bf16[512,768]{1,0:T(8,128)(2,1)} %refs_6_.3) | copy-start | bytes 2359300
  9.4 4.1 %copy-start.3 = (bf16[640,512]{1,0:T(8,128)(2,1)S(1)}, bf16[640,512]{1,0:T(8,128)(2,1)}, u32[]{:S(2)}) copy-start(bf16[640,512]{1,0:T(8,128)(2,1)} %refs_10_.3) | copy-start | bytes 1966084
  9.6 4.0 %copy-start.1 = (bf16[768,640]{1,0:T(8,128)(2,1)S(1)}, bf16[768,640]{1,0:T(8,128)(2,1)}, u32[]{:S(2)}) copy-start(bf16[768,640]{1,0:T(8,128)(2,1)} %refs_8_.3) | copy-start | bytes 2949124
  9.7 6.4 %collective-permute-start.7 = (f16[264,128]{1,0:T(8,128)(2,1)S(1)}, f16[264,128]{1,0:T(8,128)(2,1)S(1)}, u32[]{:S(2)}, u32[]{:S(2)}) collective-permute-start(f16[264,128]{1,0:T(8,128)(2,1)S(1)} %get-tuple-element.19), channel_id=1, source_target_pairs={{0,3},{1,2},{2,1},{3,0},{4,7},{5,6},{6,5},{7,4},{8,11},{9,10},{10,... | collective-permute-start | bytes 202760 | tf_op jit(solution)/shard_map/ppermute | solution.py:31
  13.0 4.3 %collective-permute-start.6 = (f16[264,128]{1,0:T(8,128)(2,1)S(1)}, f16[264,128]{1,0:T(8,128)(2,1)S(1)}, u32[]{:S(2)}, u32[]{:S(2)}) collective-permute-start(f16[264,128]{1,0:T(8,128)(2,1)S(1)} %get-tuple-element.20), channel_id=1, source_target_pairs={{0,2},{1,3},{2,0},{3,1},{4,6},{5,7},{6,4},{7,5},{8,10},{9,11},{10,... | collective-permute-start | bytes 202760 | tf_op jit(solution)/shard_map/ppermute | solution.py:31
  13.2 4.1 %collective-permute-start.2 = (f16[264,128]{1,0:T(8,128)(2,1)S(1)}, f16[264,128]{1,0:T(8,128)(2,1)S(1)}, u32[]{:S(2)}, u32[]{:S(2)}) collective-permute-start(f16[264,128]{1,0:T(8,128)(2,1)S(1)} %get-tuple-element.21), channel_id=1, source_target_pairs={{0,1},{1,0},{2,3},{3,2},{4,5},{5,4},{6,7},{7,6},{8,9},{9,8},{10,11... | collective-permute-start | bytes 202760 | tf_op jit(solution)/shard_map/ppermute | solution.py:31
  13.5 0.7 %copy-start.7 = (f32[512]{0:T(512)S(1)}, f32[512]{0:T(512)}, u32[]{:S(2)}) copy-start(f32[512]{0:T(512)} %param.23) | copy-start | bytes 6148
  13.5 0.7 %copy-start.8 = (s32[1,1,2]{2,1,0:T(1,128)S(1)}, s32[1,1,2]{2,1,0:T(1,128)}, u32[]{:S(2)}) copy-start(s32[1,1,2]{2,1,0:T(1,128)} %refs_4_.3) | copy-start | bytes 28
  13.5 0.7 %copy-start.9 = (s32[1,1,2]{2,1,0:T(1,128)S(1)}, s32[1,1,2]{2,1,0:T(1,128)}, u32[]{:S(2)}) copy-start(s32[1,1,2]{2,1,0:T(1,128)} %refs_5_.3) | copy-start | bytes 28

commit v4 on v3

--- a/solution.py
+++ b/solution.py
@@ -189,7 +189,7 @@
     return jnp.max(jnp.where(hits, 1.0, 0.0), axis=1, keepdims=True)
 
 
-def physics_kernel(groups, helds, blocks, count, levels, aliased, *refs):
+def physics_kernel(groups, order, helds, blocks, count, levels, aliased, *refs):
     sets = [refs[index * groups : (index + 1) * groups] for index in range(len(helds))]
     refs = refs[len(helds) * groups :]
     own, lent, first, bias_first, second, bias_second, third, bias_third = refs[:8]
@@ -204,9 +204,8 @@
     at = 0
     for parts, held in zip(sets, helds):
         tall = held * count * levels
-        for step in range(groups):
+        for step, part in zip(order, parts):
             level = source(me, step, groups)
-            part = parts[step]
             for index in range(held):
                 for field in range(count):
                     start = pl.multiple_of(field * depth + level * levels, levels)
@@ -246,7 +245,7 @@
         send(index, block[0]).wait()
 
 
-def physics(sets, network, rows, blocks, count, levels, result=None):
+def physics(sets, order, network, rows, blocks, count, levels, result=None):
     groups = len(sets[0])
     many = len(blocks)
     width = count * groups * levels
@@ -260,7 +259,7 @@
         operands.append(result)
         specs.append(ANY)
     return pl.pallas_call(
-        functools.partial(physics_kernel, groups, helds, blocks, count, levels, aliased),
+        functools.partial(physics_kernel, groups, order, helds, blocks, count, levels, aliased),
         in_specs=specs,
         out_specs=[ANY] + [VMEM] * (1 - aliased),
         out_shape=[jax.ShapeDtypeStruct((width, rows, LANES), f32)] + [unit] * (1 - aliased),
@@ -310,7 +309,8 @@
         return [exchange(value, step + 1, groups) for step, value in enumerate(sent)]
 
     def received(message, values, unit):
-        return [message[0]] + [value.astype(f32) * unit for value in values]
+        taken = [message[0]] + [value.astype(f32) * unit for value in values]
+        return [taken[step] for step in order]
 
     local = (fields, courant_lon, courant_lat, displacement, edges, groups)
     network = (
@@ -325,10 +325,11 @@
     message, unit = finish(*outer, north, south, (), groups)
     moved = swap(message)
     blocks = tuple((row, row) for row in range(1, rows - 1))
+    order = [0, *range(1, min(groups, 2)), *range(groups - 1, 1, -1)]
     sets = (received(inner, inner_moved, unit[0:1, :]),)
-    result, unit = physics(sets, network, rows, blocks, count, levels)
+    result, unit = physics(sets, order, network, rows, blocks, count, levels)
     sets = (received(message, moved, unit[0:1, :]),)
-    return physics(sets, network, rows, ((0, 0), (rows - 1, rows - 1)), count, levels, result)[0]
+    return physics(sets, order, network, rows, ((0, 0), (rows - 1, rows - 1)), count, levels, result)[0]
 
 
 def solution(mesh):

time: 19.4 us -> 19.1 us (0.985)
    ppermute x6, waiting for transfers between devices: 1.21 us -> 0.88 us  [exchange(): lax.ppermute(value, 'lev', [(i, i ^ step if power else (i + step) % count...]
    ppermute x1, waiting for transfers between devices: 0.02 us -> 0.28 us  [body(): lax.ppermute((jnp.where(even, edges[0], edges[1]) * SCALE).astype(half),...]
  transfers between devices with their start and end apart: 8 -> 8, of which waited for: 1 -> 2; matrix products, arithmetic and copies ran while one was open for 1% -> 1% of each run, Pallas kernels for 17% -> 18%
where the time goes in v4:
time: 19.1 us; the launch traced here: 18.9 us
  starting transfers between devices  9.94 us (52%)
  Pallas kernels  5.28 us (28%)
  local copies, waits for them, and re-layouts  1.92 us (10%)
  waiting for transfers between devices  1.16 us (6%)
  other arithmetic  0.29 us (2%)
  between operations  0.28 us (1%)
    ppermute x6, starting transfers between devices, exchange(): lax.ppermute(value, 'lev', [(i, i ^ step if power else (i + step) % count...  6.72 us
    pallas_call x2, Pallas kernels, physics(): pl.pallas_call(functools.partial(physics_kernel, groups, order, helds, bl...  3.71 us
    ppermute x1, starting transfers between devices, body(): lax.ppermute((jnp.where(even, edges[0], edges[1]) * SCALE).astype(half),...  1.94 us
    unnamed x24, local copies, waits for them, and re-layouts  1.91 us
    pallas_call x2, Pallas kernels, local_rows(): pl.pallas_call(functools.partial(local_kernel, groups, inner), in_specs=[...  1.3 us
    ppermute x1, starting transfers between devices, body(): lax.ppermute((jnp.where(even, edges[1], edges[0]) * SCALE).astype(half),...  1.28 us
    ppermute x6, waiting for transfers between devices, exchange(): lax.ppermute(value, 'lev', [(i, i ^ step if power else (i + step) % count...  0.88 us
  transfers between devices with their start and end apart: 8, of which 2 were waited for; matrix products, arithmetic and copies ran while one was open for 1% of the time, Pallas kernels for 18%

profile of v4, /device:TPU:9, one launch (start us, length us, event | category | flops | bytes accessed | tf_op | source)
XLA Modules:
  0.0 18.9 jit_solution(13688652983487088350)
XLA Ops:
  0.0 1.2 %copy-done = f32[4,32,4,512]{3,2,1,0:T(4,128)S(1)} copy-done((f32[4,32,4,512]{3,2,1,0:T(4,128)S(1)}, f32[4,32,4,512]{3,2,1,0:T(4,128)}, u32[]{:S(2)}) %copy-start) | copy-done | bytes 1048600
  1.2 0.1 edge_rows.1.edges
  1.3 0.0 copy-start.4
  1.3 0.0 copy-start.5
  1.4 0.0 copy-start.6
  1.4 0.1 fusion.4
  1.4 1.3 %collective-permute-start.1 = (f16[4,32,512]{2,1,0:T(8,128)(2,1)S(1)}, f16[4,32,512]{2,1,0:T(8,128)(2,1)S(1)}, u32[]{:S(2)}, u32[]{:S(2)}) collective-permute-start(f16[4,32,512]{2,1,0:T(8,128)(2,1)S(1)} %get-tuple-element.27), channel_id=1, source_target_pairs={{0,4},{4,0},{8,12},{12,8},{16,20},{20,16},{24,28},{28,24},{1,5},{5... | collective-permute-start | bytes 393224 | tf_op jit(solution)/shard_map/ppermute | solution.py:305
  2.7 1.9 %collective-permute-start = (f16[4,32,512]{2,1,0:T(8,128)(2,1)S(1)}, f16[4,32,512]{2,1,0:T(8,128)(2,1)S(1)}, u32[]{:S(2)}, u32[]{:S(2)}) collective-permute-start(f16[4,32,512]{2,1,0:T(8,128)(2,1)S(1)} %get-tuple-element.28), channel_id=1, source_target_pairs={{4,8},{8,4},{12,16},{16,12},{20,24},{24,20},{5,9},{9,5},{13,17},{1... | collective-permute-start | bytes 393224 | tf_op jit(solution)/shard_map/ppermute | solution.py:304
  4.7 0.8 %inner_rows.1 = f32[4,264,128]{2,1,0:T(8,128)S(1)} custom-call(f32[4,32,4,512]{3,2,1,0:T(4,128)S(1)} %copy-done, f32[32,4,512]{2,1,0:T(4,128)S(1)} %copy-done.4, f32[32,4,512]{2,1,0:T(4,128)S(1)} %copy-done.5, f32[32,4,512]{2,1,0:T(4,128)S(1)} %copy-done.6, f32[2,4,32,512]{3,2,1,0:T(8,128)S(1)} %edge_rows.1.edges), custom_call_target="tpu_custom_call" | custom-call | flops 1000000000 | bytes 3000000 | tf_op jit(solution)/shard_map/inner_rows/pallas_call | solution.py:133
  5.5 0.0 copy-start.11
  5.5 1.4 %collective-permute-start.5 = (f16[264,128]{1,0:T(8,128)(2,1)S(1)}, f16[264,128]{1,0:T(8,128)(2,1)S(1)}, u32[]{:S(2)}, u32[]{:S(2)}) collective-permute-start(f16[264,128]{1,0:T(8,128)(2,1)S(1)} %get-tuple-element.23), channel_id=1, source_target_pairs={{0,2},{1,3},{2,0},{3,1},{4,6},{5,7},{6,4},{7,5},{8,10},{9,11},{10,... | collective-permute-start | bytes 202760 | tf_op jit(solution)/shard_map/ppermute | solution.py:31
  6.9 1.2 %collective-permute-start.4 = (f16[264,128]{1,0:T(8,128)(2,1)S(1)}, f16[264,128]{1,0:T(8,128)(2,1)S(1)}, u32[]{:S(2)}, u32[]{:S(2)}) collective-permute-start(f16[264,128]{1,0:T(8,128)(2,1)S(1)} %get-tuple-element.24), channel_id=1, source_target_pairs={{0,3},{1,2},{2,1},{3,0},{4,7},{5,6},{6,5},{7,4},{8,11},{9,10},{10,... | collective-permute-start | bytes 202760 | tf_op jit(solution)/shard_map/ppermute | solution.py:31
  8.2 0.3 %collective-permute-start.3 = (f16[264,128]{1,0:T(8,128)(2,1)S(1)}, f16[264,128]{1,0:T(8,128)(2,1)S(1)}, u32[]{:S(2)}, u32[]{:S(2)}) collective-permute-start(f16[264,128]{1,0:T(8,128)(2,1)S(1)} %get-tuple-element.25), channel_id=1, source_target_pairs={{0,1},{1,0},{2,3},{3,2},{4,5},{5,4},{6,7},{7,6},{8,9},{9,8},{10,11... | collective-permute-start | bytes 202760 | tf_op jit(solution)/shard_map/ppermute | solution.py:31
  8.5 0.5 %outer_rows.1 = (f32[2,4,32,512]{3,2,1,0:T(8,128)S(1)}, f32[2,32,512]{2,1,0:T(8,128)S(1)}, f32[2,32,512]{2,1,0:T(8,128)S(1)}) custom-call(f32[4,32,4,512]{3,2,1,0:T(4,128)S(1)} %copy-done, f32[32,4,512]{2,1,0:T(4,128)S(1)} %copy-done.4, f32[32,4,512]{2,1,0:T(4,128)S(1)} %copy-done.5, f32[32,4,512]{2,1,0:T(4,128)S(1)} %copy-done.6, ...), custom_call_target="tpu_custom_call" | custom-call | flops 1000000000 | bytes 3000000 | tf_op jit(solution)/shard_map/outer_rows/pallas_call | solution.py:133
  9.0 0.0 collective-permute-done.1
  9.0 0.3 %collective-permute-done = f16[4,32,512]{2,1,0:T(8,128)(2,1)S(1)} collective-permute-done((f16[4,32,512]{2,1,0:T(8,128)(2,1)S(1)}, f16[4,32,512]{2,1,0:T(8,128)(2,1)S(1)}, u32[]{:S(2)}, u32[]{:S(2)}) %collective-permute-start) | collective-permute-done | bytes 131104 | tf_op jit(solution)/shard_map/ppermute | solution.py:304
  9.3 0.1 convert_multiply_fusion
  9.4 0.0 copy-start.2
  9.4 0.0 copy-start.3
  9.4 0.2 finish.1
  9.6 0.0 copy-start.1
  9.7 1.3 %collective-permute-start.7 = (f16[264,128]{1,0:T(8,128)(2,1)S(1)}, f16[264,128]{1,0:T(8,128)(2,1)S(1)}, u32[]{:S(2)}, u32[]{:S(2)}) collective-permute-start(f16[264,128]{1,0:T(8,128)(2,1)S(1)} %get-tuple-element.19), channel_id=1, source_target_pairs={{0,2},{1,3},{2,0},{3,1},{4,6},{5,7},{6,4},{7,5},{8,10},{9,11},{10,... | collective-permute-start | bytes 202760 | tf_op jit(solution)/shard_map/ppermute | solution.py:31
  11.0 2.5 %collective-permute-start.6 = (f16[264,128]{1,0:T(8,128)(2,1)S(1)}, f16[264,128]{1,0:T(8,128)(2,1)S(1)}, u32[]{:S(2)}, u32[]{:S(2)}) collective-permute-start(f16[264,128]{1,0:T(8,128)(2,1)S(1)} %get-tuple-element.20), channel_id=1, source_target_pairs={{0,3},{1,2},{2,1},{3,0},{4,7},{5,6},{6,5},{7,4},{8,11},{9,10},{10,... | collective-permute-start | bytes 202760 | tf_op jit(solution)/shard_map/ppermute | solution.py:31
  13.5 0.0 collective-permute-done.5
  13.5 0.0 collective-permute-done.3
  13.5 0.0 copy-start.7
  13.6 0.0 copy-start.8
  13.6 0.0 copy-start.9
  13.6 0.6 %copy-done.7 = f32[512]{0:T(512)S(1)} copy-done((f32[512]{0:T(512)S(1)}, f32[512]{0:T(512)}, u32[]{:S(2)}) %copy-start.7) | copy-done | bytes 2072
  14.2 1.8 %physics.2 = (f32[512,4,128]{2,1,0:T(4,128)}, f32[8,128]{1,0:T(8,128)S(1)}) custom-call(f32[264,128]{1,0:T(8,128)S(1)} %get-tuple-element.26.refs_0_, f32[264,128]{1,0:T(8,128)S(1)} %get-tuple-element.36.refs_1_, f32[264,128]{1,0:T(8,128)S(1)} %get-tuple-element.35.refs_2_, f32[264,128]{1,0:T(8,128)S(1)} %get-tuple-element.34.refs_3_, ...), custom_call_target="tpu_custom_call" | custom-call | flops 20000000000 | bytes 5000000 | tf_op jit(solution)/shard_map/physics/pallas_call | solution.py:261
  16.1 0.9 %collective-permute-done.6 = f16[264,128]{1,0:T(8,128)(2,1)S(1)} collective-permute-done((f16[264,128]{1,0:T(8,128)(2,1)S(1)}, f16[264,128]{1,0:T(8,128)(2,1)S(1)}, u32[]{:S(2)}, u32[]{:S(2)}) %collective-permute-start.6) | collective-permute-done | bytes 67616 | tf_op jit(solution)/shard_map/ppermute | solution.py:31
  17.0 1.9 %physics.3 = f32[512,4,128]{2,1,0:T(4,128)} custom-call(f32[264,128]{1,0:T(8,128)S(1)} %get-tuple-element.22.refs_0_, f32[264,128]{1,0:T(8,128)S(1)} %get-tuple-element.33.refs_1_, f32[264,128]{1,0:T(8,128)S(1)} %get-tuple-element.32.refs_2_, f32[264,128]{1,0:T(8,128)S(1)} %get-tuple-element.31.refs_3_, ...), custom_call_target="tpu_custom_call", output_to_operand_aliasing={{}: (12, {})} | custom-call | flops 20000000000 | bytes 5000000 | tf_op jit(solution)/shard_map/physics/pallas_call | solution.py:261
  (24 shorter events, 0.2 us)
Async XLA Ops:
  0.0 1.2 %copy-start = (f32[4,32,4,512]{3,2,1,0:T(4,128)S(1)}, f32[4,32,4,512]{3,2,1,0:T(4,128)}, u32[]{:S(2)}) copy-start(f32[4,32,4,512]{3,2,1,0:T(4,128)} %fields.5) | copy-start | bytes 3145732
  1.3 3.3 %copy-start.4 = (f32[32,4,512]{2,1,0:T(4,128)S(1)}, f32[32,4,512]{2,1,0:T(4,128)}, u32[]{:S(2)}) copy-start(f32[32,4,512]{2,1,0:T(4,128)} %along_lon.3) | copy-start | bytes 786436
  1.3 3.3 %copy-start.5 = (f32[32,4,512]{2,1,0:T(4,128)S(1)}, f32[32,4,512]{2,1,0:T(4,128)}, u32[]{:S(2)}) copy-start(f32[32,4,512]{2,1,0:T(4,128)} %along_lat.3) | copy-start | bytes 786436
  1.4 3.3 %copy-start.6 = (f32[32,4,512]{2,1,0:T(4,128)S(1)}, f32[32,4,512]{2,1,0:T(4,128)}, u32[]{:S(2)}) copy-start(f32[32,4,512]{2,1,0:T(4,128)} %displacement.3) | copy-start | bytes 786436
  1.4 7.6 %collective-permute-start.1 = (f16[4,32,512]{2,1,0:T(8,128)(2,1)S(1)}, f16[4,32,512]{2,1,0:T(8,128)(2,1)S(1)}, u32[]{:S(2)}, u32[]{:S(2)}) collective-permute-start(f16[4,32,512]{2,1,0:T(8,128)(2,1)S(1)} %get-tuple-element.27), channel_id=1, source_target_pairs={{0,4},{4,0},{8,12},{12,8},{16,20},{20,16},{24,28},{28,24},{1,5},{5... | collective-permute-start | bytes 393224 | tf_op jit(solution)/shard_map/ppermute | solution.py:305
  2.7 6.6 %collective-permute-start = (f16[4,32,512]{2,1,0:T(8,128)(2,1)S(1)}, f16[4,32,512]{2,1,0:T(8,128)(2,1)S(1)}, u32[]{:S(2)}, u32[]{:S(2)}) collective-permute-start(f16[4,32,512]{2,1,0:T(8,128)(2,1)S(1)} %get-tuple-element.28), channel_id=1, source_target_pairs={{4,8},{8,4},{12,16},{16,12},{20,24},{24,20},{5,9},{9,5},{13,17},{1... | collective-permute-start | bytes 393224 | tf_op jit(solution)/shard_map/ppermute | solution.py:304
  5.5 2.9 %copy-start.11 = (f32[640]{0:T(1024)S(1)}, f32[640]{0:T(1024)}, u32[]{:S(2)}) copy-start(f32[640]{0:T(1024)} %param.21) | copy-start | bytes 7684
  5.5 8.0 %collective-permute-start.5 = (f16[264,128]{1,0:T(8,128)(2,1)S(1)}, f16[264,128]{1,0:T(8,128)(2,1)S(1)}, u32[]{:S(2)}, u32[]{:S(2)}) collective-permute-start(f16[264,128]{1,0:T(8,128)(2,1)S(1)} %get-tuple-element.23), channel_id=1, source_target_pairs={{0,2},{1,3},{2,0},{3,1},{4,6},{5,7},{6,4},{7,5},{8,10},{9,11},{10,... | collective-permute-start | bytes 202760 | tf_op jit(solution)/shard_map/ppermute | solution.py:31
  6.9 1.5 %copy-start.10 = (f32[768]{0:T(1024)S(1)}, f32[768]{0:T(1024)}, u32[]{:S(2)}) copy-start(f32[768]{0:T(1024)} %param.19) | copy-start | bytes 9220
  6.9 6.6 %collective-permute-start.4 = (f16[264,128]{1,0:T(8,128)(2,1)S(1)}, f16[264,128]{1,0:T(8,128)(2,1)S(1)}, u32[]{:S(2)}, u32[]{:S(2)}) collective-permute-start(f16[264,128]{1,0:T(8,128)(2,1)S(1)} %get-tuple-element.24), channel_id=1, source_target_pairs={{0,3},{1,2},{2,1},{3,0},{4,7},{5,6},{6,5},{7,4},{8,11},{9,10},{10,... | collective-permute-start | bytes 202760 | tf_op jit(solution)/shard_map/ppermute | solution.py:31
  8.2 5.3 %collective-permute-start.3 = (f16[264,128]{1,0:T(8,128)(2,1)S(1)}, f16[264,128]{1,0:T(8,128)(2,1)S(1)}, u32[]{:S(2)}, u32[]{:S(2)}) collective-permute-start(f16[264,128]{1,0:T(8,128)(2,1)S(1)} %get-tuple-element.25), channel_id=1, source_target_pairs={{0,1},{1,0},{2,3},{3,2},{4,5},{5,4},{6,7},{7,6},{8,9},{9,8},{10,11... | collective-permute-start | bytes 202760 | tf_op jit(solution)/shard_map/ppermute | solution.py:31
  9.4 4.2 %copy-start.2 = (bf16[512,768]{1,0:T(8,128)(2,1)S(1)}, bf16[512,768]{1,0:T(8,128)(2,1)}, u32[]{:S(2)}) copy-start(bf16[512,768]{1,0:T(8,128)(2,1)} %refs_6_.3) | copy-start | bytes 2359300
  9.4 4.2 %copy-start.3 = (bf16[640,512]{1,0:T(8,128)(2,1)S(1)}, bf16[640,512]{1,0:T(8,128)(2,1)}, u32[]{:S(2)}) copy-start(bf16[640,512]{1,0:T(8,128)(2,1)} %refs_10_.3) | copy-start | bytes 1966084
  9.6 4.0 %copy-start.1 = (bf16[768,640]{1,0:T(8,128)(2,1)S(1)}, bf16[768,640]{1,0:T(8,128)(2,1)}, u32[]{:S(2)}) copy-start(bf16[768,640]{1,0:T(8,128)(2,1)} %refs_8_.3) | copy-start | bytes 2949124
  9.7 6.4 %collective-permute-start.7 = (f16[264,128]{1,0:T(8,128)(2,1)S(1)}, f16[264,128]{1,0:T(8,128)(2,1)S(1)}, u32[]{:S(2)}, u32[]{:S(2)}) collective-permute-start(f16[264,128]{1,0:T(8,128)(2,1)S(1)} %get-tuple-element.19), channel_id=1, source_target_pairs={{0,2},{1,3},{2,0},{3,1},{4,6},{5,7},{6,4},{7,5},{8,10},{9,11},{10,... | collective-permute-start | bytes 202760 | tf_op jit(solution)/shard_map/ppermute | solution.py:31
  11.0 6.0 %collective-permute-start.6 = (f16[264,128]{1,0:T(8,128)(2,1)S(1)}, f16[264,128]{1,0:T(8,128)(2,1)S(1)}, u32[]{:S(2)}, u32[]{:S(2)}) collective-permute-start(f16[264,128]{1,0:T(8,128)(2,1)S(1)} %get-tuple-element.20), channel_id=1, source_target_pairs={{0,3},{1,2},{2,1},{3,0},{4,7},{5,6},{6,5},{7,4},{8,11},{9,10},{10,... | collective-permute-start | bytes 202760 | tf_op jit(solution)/shard_map/ppermute | solution.py:31
  13.5 3.5 %collective-permute-start.2 = (f16[264,128]{1,0:T(8,128)(2,1)S(1)}, f16[264,128]{1,0:T(8,128)(2,1)S(1)}, u32[]{:S(2)}, u32[]{:S(2)}) collective-permute-start(f16[264,128]{1,0:T(8,128)(2,1)S(1)} %get-tuple-element.21), channel_id=1, source_target_pairs={{0,1},{1,0},{2,3},{3,2},{4,5},{5,4},{6,7},{7,6},{8,9},{9,8},{10,11... | collective-permute-start | bytes 202760 | tf_op jit(solution)/shard_map/ppermute | solution.py:31
  13.5 0.7 %copy-start.7 = (f32[512]{0:T(512)S(1)}, f32[512]{0:T(512)}, u32[]{:S(2)}) copy-start(f32[512]{0:T(512)} %param.23) | copy-start | bytes 6148
  13.6 0.7 %copy-start.8 = (s32[1,1,2]{2,1,0:T(1,128)S(1)}, s32[1,1,2]{2,1,0:T(1,128)}, u32[]{:S(2)}) copy-start(s32[1,1,2]{2,1,0:T(1,128)} %refs_4_.3) | copy-start | bytes 28
  13.6 0.7 %copy-start.9 = (s32[1,1,2]{2,1,0:T(1,128)S(1)}, s32[1,1,2]{2,1,0:T(1,128)}, u32[]{:S(2)}) copy-start(s32[1,1,2]{2,1,0:T(1,128)} %refs_5_.3) | copy-start | bytes 28

commit v5 on v4

--- a/solution.py
+++ b/solution.py
@@ -9,6 +9,7 @@
 
 LANES = 128
 SCALE = 4096.0
+SETTLE = 0.87
 MEGA = 1024 * 1024
 VMEM = pl.BlockSpec(memory_space=pltpu.VMEM)
 ANY = pl.BlockSpec(memory_space=pl.ANY)
@@ -60,12 +61,17 @@
     return rows * count * levels + -(-rows * count // 8) * 8
 
 
+def settled(value):
+    near = value.astype(jnp.bfloat16).astype(jnp.float32)
+    return near + SETTLE * (value - near)
+
+
 def store_message(message, index, rows, field, count, advected, share, groups, me):
     levels = advected.shape[0]
     flux = share * advected
     depth = lax.broadcasted_iota(jnp.int32, flux.shape, 0)
     above = jnp.where(depth == 0, 0.0, pltpu.roll(flux, 1, 0))
-    remapped = advected - flux + above
+    remapped = settled(advected - flux + above)
     base = (index * count + field) * levels
     row = rows * count * levels + index * count + field
     for group in range(groups):

time: 19.1 us -> 19.1 us (level)
  no operation moved by 1% of the time
where the time goes in v5:
time: 19.1 us; the launch traced here: 18.9 us
  starting transfers between devices  9.94 us (52%)
  Pallas kernels  5.43 us (28%)
  local copies, waits for them, and re-layouts  1.92 us (10%)
  waiting for transfers between devices  1.08 us (6%)
  other arithmetic  0.29 us (2%)
  between operations  0.28 us (1%)
    ppermute x6, starting transfers between devices, exchange(): lax.ppermute(value, 'lev', [(i, i ^ step if power else (i + step) % count...  6.72 us
    pallas_call x2, Pallas kernels, physics(): pl.pallas_call(functools.partial(physics_kernel, groups, order, helds, bl...  3.71 us
    ppermute x1, starting transfers between devices, body(): lax.ppermute((jnp.where(even, edges[0], edges[1]) * SCALE).astype(half),...  1.94 us
    unnamed x24, local copies, waits for them, and re-layouts  1.91 us
    pallas_call x2, Pallas kernels, local_rows(): pl.pallas_call(functools.partial(local_kernel, groups, inner), in_specs=[...  1.38 us
    ppermute x1, starting transfers between devices, body(): lax.ppermute((jnp.where(even, edges[1], edges[0]) * SCALE).astype(half),...  1.28 us
    ppermute x6, waiting for transfers between devices, exchange(): lax.ppermute(value, 'lev', [(i, i ^ step if power else (i + step) % count...  0.87 us
  transfers between devices with their start and end apart: 8, of which 2 were waited for; matrix products, arithmetic and copies ran while one was open for 1% of the time, Pallas kernels for 18%

profile of v5, /device:TPU:9, one launch (start us, length us, event | category | flops | bytes accessed | tf_op | source)
XLA Modules:
  0.0 18.9 jit_solution(10983270770466828099)
XLA Ops:
  0.0 1.2 %copy-done = f32[4,32,4,512]{3,2,1,0:T(4,128)S(1)} copy-done((f32[4,32,4,512]{3,2,1,0:T(4,128)S(1)}, f32[4,32,4,512]{3,2,1,0:T(4,128)}, u32[]{:S(2)}) %copy-start) | copy-done | bytes 1048600
  1.2 0.1 edge_rows.1.edges
  1.3 0.0 copy-start.4
  1.3 0.0 copy-start.5
  1.4 0.0 copy-start.6
  1.4 0.1 fusion.4
  1.4 1.3 %collective-permute-start.1 = (f16[4,32,512]{2,1,0:T(8,128)(2,1)S(1)}, f16[4,32,512]{2,1,0:T(8,128)(2,1)S(1)}, u32[]{:S(2)}, u32[]{:S(2)}) collective-permute-start(f16[4,32,512]{2,1,0:T(8,128)(2,1)S(1)} %get-tuple-element.27), channel_id=1, source_target_pairs={{0,4},{4,0},{8,12},{12,8},{16,20},{20,16},{24,28},{28,24},{1,5},{5... | collective-permute-start | bytes 393224 | tf_op jit(solution)/shard_map/ppermute | solution.py:311
  2.7 1.9 %collective-permute-start = (f16[4,32,512]{2,1,0:T(8,128)(2,1)S(1)}, f16[4,32,512]{2,1,0:T(8,128)(2,1)S(1)}, u32[]{:S(2)}, u32[]{:S(2)}) collective-permute-start(f16[4,32,512]{2,1,0:T(8,128)(2,1)S(1)} %get-tuple-element.28), channel_id=1, source_target_pairs={{4,8},{8,4},{12,16},{16,12},{20,24},{24,20},{5,9},{9,5},{13,17},{1... | collective-permute-start | bytes 393224 | tf_op jit(solution)/shard_map/ppermute | solution.py:310
  4.7 0.8 %inner_rows.1 = f32[4,264,128]{2,1,0:T(8,128)S(1)} custom-call(f32[4,32,4,512]{3,2,1,0:T(4,128)S(1)} %copy-done, f32[32,4,512]{2,1,0:T(4,128)S(1)} %copy-done.4, f32[32,4,512]{2,1,0:T(4,128)S(1)} %copy-done.5, f32[32,4,512]{2,1,0:T(4,128)S(1)} %copy-done.6, f32[2,4,32,512]{3,2,1,0:T(8,128)S(1)} %edge_rows.1.edges), custom_call_target="tpu_custom_call" | custom-call | flops 1000000000 | bytes 3000000 | tf_op jit(solution)/shard_map/inner_rows/pallas_call | solution.py:139
  5.6 0.0 copy-start.11
  5.6 1.4 %collective-permute-start.5 = (f16[264,128]{1,0:T(8,128)(2,1)S(1)}, f16[264,128]{1,0:T(8,128)(2,1)S(1)}, u32[]{:S(2)}, u32[]{:S(2)}) collective-permute-start(f16[264,128]{1,0:T(8,128)(2,1)S(1)} %get-tuple-element.23), channel_id=1, source_target_pairs={{0,2},{1,3},{2,0},{3,1},{4,6},{5,7},{6,4},{7,5},{8,10},{9,11},{10,... | collective-permute-start | bytes 202760 | tf_op jit(solution)/shard_map/ppermute | solution.py:32
  7.0 1.2 %collective-permute-start.4 = (f16[264,128]{1,0:T(8,128)(2,1)S(1)}, f16[264,128]{1,0:T(8,128)(2,1)S(1)}, u32[]{:S(2)}, u32[]{:S(2)}) collective-permute-start(f16[264,128]{1,0:T(8,128)(2,1)S(1)} %get-tuple-element.24), channel_id=1, source_target_pairs={{0,3},{1,2},{2,1},{3,0},{4,7},{5,6},{6,5},{7,4},{8,11},{9,10},{10,... | collective-permute-start | bytes 202760 | tf_op jit(solution)/shard_map/ppermute | solution.py:32
  8.3 0.3 %collective-permute-start.3 = (f16[264,128]{1,0:T(8,128)(2,1)S(1)}, f16[264,128]{1,0:T(8,128)(2,1)S(1)}, u32[]{:S(2)}, u32[]{:S(2)}) collective-permute-start(f16[264,128]{1,0:T(8,128)(2,1)S(1)} %get-tuple-element.25), channel_id=1, source_target_pairs={{0,1},{1,0},{2,3},{3,2},{4,5},{5,4},{6,7},{7,6},{8,9},{9,8},{10,11... | collective-permute-start | bytes 202760 | tf_op jit(solution)/shard_map/ppermute | solution.py:32
  8.6 0.5 %outer_rows.1 = (f32[2,4,32,512]{3,2,1,0:T(8,128)S(1)}, f32[2,32,512]{2,1,0:T(8,128)S(1)}, f32[2,32,512]{2,1,0:T(8,128)S(1)}) custom-call(f32[4,32,4,512]{3,2,1,0:T(4,128)S(1)} %copy-done, f32[32,4,512]{2,1,0:T(4,128)S(1)} %copy-done.4, f32[32,4,512]{2,1,0:T(4,128)S(1)} %copy-done.5, f32[32,4,512]{2,1,0:T(4,128)S(1)} %copy-done.6, ...), custom_call_target="tpu_custom_call" | custom-call | flops 1000000000 | bytes 3000000 | tf_op jit(solution)/shard_map/outer_rows/pallas_call | solution.py:139
  9.1 0.0 collective-permute-done.1
  9.1 0.2 %collective-permute-done = f16[4,32,512]{2,1,0:T(8,128)(2,1)S(1)} collective-permute-done((f16[4,32,512]{2,1,0:T(8,128)(2,1)S(1)}, f16[4,32,512]{2,1,0:T(8,128)(2,1)S(1)}, u32[]{:S(2)}, u32[]{:S(2)}) %collective-permute-start) | collective-permute-done | bytes 131104 | tf_op jit(solution)/shard_map/ppermute | solution.py:310
  9.3 0.1 convert_multiply_fusion
  9.4 0.0 copy-start.2
  9.4 0.0 copy-start.3
  9.4 0.2 %finish.1 = (f32[4,264,128]{2,1,0:T(8,128)S(1)}, f32[8,128]{1,0:T(8,128)S(1)}) custom-call(f32[2,4,32,512]{3,2,1,0:T(8,128)S(1)} %get-tuple-element.12.partial, f32[2,32,512]{2,1,0:T(8,128)S(1)} %get-tuple-element.13.weight, f32[2,32,512]{2,1,0:T(8,128)S(1)} %get-tuple-element.14.share, f32[4,32,512]{2,1,0:T(8,128)S(1)} %get-tuple-element.30.north, ...), custom_call_target="tpu_custom_call" | custom-call | tf_op jit(solution)/shard_map/finish/pallas_call | solution.py:165
  9.7 0.0 copy-start.1
  9.7 1.3 %collective-permute-start.7 = (f16[264,128]{1,0:T(8,128)(2,1)S(1)}, f16[264,128]{1,0:T(8,128)(2,1)S(1)}, u32[]{:S(2)}, u32[]{:S(2)}) collective-permute-start(f16[264,128]{1,0:T(8,128)(2,1)S(1)} %get-tuple-element.19), channel_id=1, source_target_pairs={{0,2},{1,3},{2,0},{3,1},{4,6},{5,7},{6,4},{7,5},{8,10},{9,11},{10,... | collective-permute-start | bytes 202760 | tf_op jit(solution)/shard_map/ppermute | solution.py:32
  11.0 2.5 %collective-permute-start.6 = (f16[264,128]{1,0:T(8,128)(2,1)S(1)}, f16[264,128]{1,0:T(8,128)(2,1)S(1)}, u32[]{:S(2)}, u32[]{:S(2)}) collective-permute-start(f16[264,128]{1,0:T(8,128)(2,1)S(1)} %get-tuple-element.20), channel_id=1, source_target_pairs={{0,3},{1,2},{2,1},{3,0},{4,7},{5,6},{6,5},{7,4},{8,11},{9,10},{10,... | collective-permute-start | bytes 202760 | tf_op jit(solution)/shard_map/ppermute | solution.py:32
  13.6 0.0 collective-permute-done.3
  13.6 0.0 copy-start.7
  13.6 0.0 copy-start.8
  13.6 0.0 copy-start.9
  13.7 0.6 %copy-done.7 = f32[512]{0:T(512)S(1)} copy-done((f32[512]{0:T(512)S(1)}, f32[512]{0:T(512)}, u32[]{:S(2)}) %copy-start.7) | copy-done | bytes 2072
  14.3 1.9 %physics.2 = (f32[512,4,128]{2,1,0:T(4,128)}, f32[8,128]{1,0:T(8,128)S(1)}) custom-call(f32[264,128]{1,0:T(8,128)S(1)} %get-tuple-element.26.refs_0_, f32[264,128]{1,0:T(8,128)S(1)} %get-tuple-element.36.refs_1_, f32[264,128]{1,0:T(8,128)S(1)} %get-tuple-element.35.refs_2_, f32[264,128]{1,0:T(8,128)S(1)} %get-tuple-element.34.refs_3_, ...), custom_call_target="tpu_custom_call" | custom-call | flops 20000000000 | bytes 5000000 | tf_op jit(solution)/shard_map/physics/pallas_call | solution.py:267
  16.2 0.0 collective-permute-done.7
  16.2 0.9 %collective-permute-done.6 = f16[264,128]{1,0:T(8,128)(2,1)S(1)} collective-permute-done((f16[264,128]{1,0:T(8,128)(2,1)S(1)}, f16[264,128]{1,0:T(8,128)(2,1)S(1)}, u32[]{:S(2)}, u32[]{:S(2)}) %collective-permute-start.6) | collective-permute-done | bytes 67616 | tf_op jit(solution)/shard_map/ppermute | solution.py:32
  17.1 1.9 %physics.3 = f32[512,4,128]{2,1,0:T(4,128)} custom-call(f32[264,128]{1,0:T(8,128)S(1)} %get-tuple-element.22.refs_0_, f32[264,128]{1,0:T(8,128)S(1)} %get-tuple-element.33.refs_1_, f32[264,128]{1,0:T(8,128)S(1)} %get-tuple-element.32.refs_2_, f32[264,128]{1,0:T(8,128)S(1)} %get-tuple-element.31.refs_3_, ...), custom_call_target="tpu_custom_call", output_to_operand_aliasing={{}: (12, {})} | custom-call | flops 20000000000 | bytes 5000000 | tf_op jit(solution)/shard_map/physics/pallas_call | solution.py:267
  (24 shorter events, 0.2 us)
Async XLA Ops:
  0.0 1.2 %copy-start = (f32[4,32,4,512]{3,2,1,0:T(4,128)S(1)}, f32[4,32,4,512]{3,2,1,0:T(4,128)}, u32[]{:S(2)}) copy-start(f32[4,32,4,512]{3,2,1,0:T(4,128)} %fields.5) | copy-start | bytes 3145732
  1.3 3.3 %copy-start.4 = (f32[32,4,512]{2,1,0:T(4,128)S(1)}, f32[32,4,512]{2,1,0:T(4,128)}, u32[]{:S(2)}) copy-start(f32[32,4,512]{2,1,0:T(4,128)} %along_lon.3) | copy-start | bytes 786436
  1.3 3.3 %copy-start.5 = (f32[32,4,512]{2,1,0:T(4,128)S(1)}, f32[32,4,512]{2,1,0:T(4,128)}, u32[]{:S(2)}) copy-start(f32[32,4,512]{2,1,0:T(4,128)} %along_lat.3) | copy-start | bytes 786436
  1.4 3.3 %copy-start.6 = (f32[32,4,512]{2,1,0:T(4,128)S(1)}, f32[32,4,512]{2,1,0:T(4,128)}, u32[]{:S(2)}) copy-start(f32[32,4,512]{2,1,0:T(4,128)} %displacement.3) | copy-start | bytes 786436
  1.4 7.7 %collective-permute-start.1 = (f16[4,32,512]{2,1,0:T(8,128)(2,1)S(1)}, f16[4,32,512]{2,1,0:T(8,128)(2,1)S(1)}, u32[]{:S(2)}, u32[]{:S(2)}) collective-permute-start(f16[4,32,512]{2,1,0:T(8,128)(2,1)S(1)} %get-tuple-element.27), channel_id=1, source_target_pairs={{0,4},{4,0},{8,12},{12,8},{16,20},{20,16},{24,28},{28,24},{1,5},{5... | collective-permute-start | bytes 393224 | tf_op jit(solution)/shard_map/ppermute | solution.py:311
  2.7 6.6 %collective-permute-start = (f16[4,32,512]{2,1,0:T(8,128)(2,1)S(1)}, f16[4,32,512]{2,1,0:T(8,128)(2,1)S(1)}, u32[]{:S(2)}, u32[]{:S(2)}) collective-permute-start(f16[4,32,512]{2,1,0:T(8,128)(2,1)S(1)} %get-tuple-element.28), channel_id=1, source_target_pairs={{4,8},{8,4},{12,16},{16,12},{20,24},{24,20},{5,9},{9,5},{13,17},{1... | collective-permute-start | bytes 393224 | tf_op jit(solution)/shard_map/ppermute | solution.py:310
  5.6 2.9 %copy-start.11 = (f32[640]{0:T(1024)S(1)}, f32[640]{0:T(1024)}, u32[]{:S(2)}) copy-start(f32[640]{0:T(1024)} %param.21) | copy-start | bytes 7684
  5.6 7.9 %collective-permute-start.5 = (f16[264,128]{1,0:T(8,128)(2,1)S(1)}, f16[264,128]{1,0:T(8,128)(2,1)S(1)}, u32[]{:S(2)}, u32[]{:S(2)}) collective-permute-start(f16[264,128]{1,0:T(8,128)(2,1)S(1)} %get-tuple-element.23), channel_id=1, source_target_pairs={{0,2},{1,3},{2,0},{3,1},{4,6},{5,7},{6,4},{7,5},{8,10},{9,11},{10,... | collective-permute-start | bytes 202760 | tf_op jit(solution)/shard_map/ppermute | solution.py:32
  7.0 1.5 %copy-start.10 = (f32[768]{0:T(1024)S(1)}, f32[768]{0:T(1024)}, u32[]{:S(2)}) copy-start(f32[768]{0:T(1024)} %param.19) | copy-start | bytes 9220
  7.0 6.5 %collective-permute-start.4 = (f16[264,128]{1,0:T(8,128)(2,1)S(1)}, f16[264,128]{1,0:T(8,128)(2,1)S(1)}, u32[]{:S(2)}, u32[]{:S(2)}) collective-permute-start(f16[264,128]{1,0:T(8,128)(2,1)S(1)} %get-tuple-element.24), channel_id=1, source_target_pairs={{0,3},{1,2},{2,1},{3,0},{4,7},{5,6},{6,5},{7,4},{8,11},{9,10},{10,... | collective-permute-start | bytes 202760 | tf_op jit(solution)/shard_map/ppermute | solution.py:32
  8.3 5.3 %collective-permute-start.3 = (f16[264,128]{1,0:T(8,128)(2,1)S(1)}, f16[264,128]{1,0:T(8,128)(2,1)S(1)}, u32[]{:S(2)}, u32[]{:S(2)}) collective-permute-start(f16[264,128]{1,0:T(8,128)(2,1)S(1)} %get-tuple-element.25), channel_id=1, source_target_pairs={{0,1},{1,0},{2,3},{3,2},{4,5},{5,4},{6,7},{7,6},{8,9},{9,8},{10,11... | collective-permute-start | bytes 202760 | tf_op jit(solution)/shard_map/ppermute | solution.py:32
  9.4 4.3 %copy-start.2 = (bf16[512,768]{1,0:T(8,128)(2,1)S(1)}, bf16[512,768]{1,0:T(8,128)(2,1)}, u32[]{:S(2)}) copy-start(bf16[512,768]{1,0:T(8,128)(2,1)} %refs_6_.3) | copy-start | bytes 2359300
  9.4 4.3 %copy-start.3 = (bf16[640,512]{1,0:T(8,128)(2,1)S(1)}, bf16[640,512]{1,0:T(8,128)(2,1)}, u32[]{:S(2)}) copy-start(bf16[640,512]{1,0:T(8,128)(2,1)} %refs_10_.3) | copy-start | bytes 1966084
  9.7 4.0 %copy-start.1 = (bf16[768,640]{1,0:T(8,128)(2,1)S(1)}, bf16[768,640]{1,0:T(8,128)(2,1)}, u32[]{:S(2)}) copy-start(bf16[768,640]{1,0:T(8,128)(2,1)} %refs_8_.3) | copy-start | bytes 2949124
  9.7 6.4 %collective-permute-start.7 = (f16[264,128]{1,0:T(8,128)(2,1)S(1)}, f16[264,128]{1,0:T(8,128)(2,1)S(1)}, u32[]{:S(2)}, u32[]{:S(2)}) collective-permute-start(f16[264,128]{1,0:T(8,128)(2,1)S(1)} %get-tuple-element.19), channel_id=1, source_target_pairs={{0,2},{1,3},{2,0},{3,1},{4,6},{5,7},{6,4},{7,5},{8,10},{9,11},{10,... | collective-permute-start | bytes 202760 | tf_op jit(solution)/shard_map/ppermute | solution.py:32
  11.0 6.0 %collective-permute-start.6 = (f16[264,128]{1,0:T(8,128)(2,1)S(1)}, f16[264,128]{1,0:T(8,128)(2,1)S(1)}, u32[]{:S(2)}, u32[]{:S(2)}) collective-permute-start(f16[264,128]{1,0:T(8,128)(2,1)S(1)} %get-tuple-element.20), channel_id=1, source_target_pairs={{0,3},{1,2},{2,1},{3,0},{4,7},{5,6},{6,5},{7,4},{8,11},{9,10},{10,... | collective-permute-start | bytes 202760 | tf_op jit(solution)/shard_map/ppermute | solution.py:32
  13.5 3.5 %collective-permute-start.2 = (f16[264,128]{1,0:T(8,128)(2,1)S(1)}, f16[264,128]{1,0:T(8,128)(2,1)S(1)}, u32[]{:S(2)}, u32[]{:S(2)}) collective-permute-start(f16[264,128]{1,0:T(8,128)(2,1)S(1)} %get-tuple-element.21), channel_id=1, source_target_pairs={{0,1},{1,0},{2,3},{3,2},{4,5},{5,4},{6,7},{7,6},{8,9},{9,8},{10,11... | collective-permute-start | bytes 202760 | tf_op jit(solution)/shard_map/ppermute | solution.py:32
  13.6 0.7 %copy-start.7 = (f32[512]{0:T(512)S(1)}, f32[512]{0:T(512)}, u32[]{:S(2)}) copy-start(f32[512]{0:T(512)} %param.23) | copy-start | bytes 6148
  13.6 0.7 %copy-start.8 = (s32[1,1,2]{2,1,0:T(1,128)S(1)}, s32[1,1,2]{2,1,0:T(1,128)}, u32[]{:S(2)}) copy-start(s32[1,1,2]{2,1,0:T(1,128)} %refs_4_.3) | copy-start | bytes 28
  13.6 0.7 %copy-start.9 = (s32[1,1,2]{2,1,0:T(1,128)S(1)}, s32[1,1,2]{2,1,0:T(1,128)}, u32[]{:S(2)}) copy-start(s32[1,1,2]{2,1,0:T(1,128)} %refs_5_.3) | copy-start | bytes 28

commit v6 on v5

--- a/solution.py
+++ b/solution.py
@@ -147,32 +147,56 @@
     )(fields, along_lon, along_lat, displacement, edges)
 
 
-def finish_kernel(groups, partial, weight, share, north, south, *refs):
-    message, unit = refs[-2:]
+def finish_row(groups, far, rows, partial, weight, share, halo, message):
     count = partial.shape[1]
     me = lax.axis_index("lev")
+    odd = lax.rem(lax.axis_index("lat"), 2)
+    index = odd if far else 1 - odd
+    wind, moved = weight[index], share[index]
+    for field in range(count):
+        advected = partial[index, field] + wind * halo[field]
+        store_message(message, int(far), rows, field, count, advected, moved, groups, me)
+
+
+def near_kernel(groups, partial, weight, share, halo, message):
+    finish_row(groups, False, 1, partial, weight, share, halo, message)
+
+
+def far_kernel(groups, partial, weight, share, halo, near, message, unit):
+    count, levels = partial.shape[1:3]
+    size = count * levels
     unit[...] = jnp.full(unit.shape, 1.0 / SCALE, jnp.float32)
-    for index, halo in enumerate((north, south)):
-        wind, moved = weight[index], share[index]
-        for field in range(count):
-            advected = partial[index, field] + wind * halo[field]
-            store_message(message, index, 2, field, count, advected, moved, groups, me)
-
-
-def finish(partial, weight, share, north, south, after, groups):
+    message[:, 0:size, :] = near[:, 0:size, :]
+    message[:, 2 * size : 2 * size + count, :] = near[:, size : size + count, :]
+    finish_row(groups, True, 2, partial, weight, share, halo, message)
+
+
+def near_finish(partial, weight, share, halo, groups):
+    _, count, levels, _ = partial.shape
+    return pl.pallas_call(
+        functools.partial(near_kernel, groups),
+        in_specs=[VMEM] * 4,
+        out_specs=VMEM,
+        out_shape=jax.ShapeDtypeStruct((groups, message_height(1, count, levels), LANES), jnp.float32),
+        compiler_params=params(),
+        name="near_finish",
+    )(partial, weight, share, halo)
+
+
+def far_finish(partial, weight, share, halo, near, groups):
     _, count, levels, _ = partial.shape
     f32 = jnp.float32
     return pl.pallas_call(
-        functools.partial(finish_kernel, groups),
-        in_specs=[VMEM] * (5 + len(after)),
+        functools.partial(far_kernel, groups),
+        in_specs=[VMEM] * 5,
         out_specs=[VMEM] * 2,
         out_shape=[
             jax.ShapeDtypeStruct((groups, message_height(2, count, levels), LANES), f32),
             jax.ShapeDtypeStruct((8, LANES), f32),
         ],
         compiler_params=params(),
-        name="finish",
-    )(partial, weight, share, north, south, *after)
+        name="far_finish",
+    )(partial, weight, share, halo, near)
 
 
 def silu(value):
@@ -326,16 +350,15 @@
     (inner,) = local_rows(True, *local)
     inner_moved = swap(inner)
     outer = local_rows(False, *local)
-    north = jnp.where(even, far, near).astype(f32) * (1.0 / SCALE)
-    south = jnp.where(even, near, far).astype(f32) * (1.0 / SCALE)
-    message, unit = finish(*outer, north, south, (), groups)
+    near_message = near_finish(*outer, near.astype(f32) * (1.0 / SCALE), groups)
+    message, unit = far_finish(*outer, far.astype(f32) * (1.0 / SCALE), near_message, groups)
     moved = swap(message)
     blocks = tuple((row, row) for row in range(1, rows - 1))
     order = [0, *range(1, min(groups, 2)), *range(groups - 1, 1, -1)]
     sets = (received(inner, inner_moved, unit[0:1, :]),)
     result, unit = physics(sets, order, network, rows, blocks, count, levels)
     sets = (received(message, moved, unit[0:1, :]),)
-    return physics(sets, order, network, rows, ((0, 0), (rows - 1, rows - 1)), count, levels, result)[0]
+    return physics(sets, order, network, rows, ((rows - 1, 0), (0, rows - 1)), count, levels, result)[0]
 
 
 def solution(mesh):

time: 19.1 us -> 19 us (level)
  transfers between devices with their start and end apart: 8 -> 8, of which waited for: 2 -> 1; matrix products, arithmetic and copies ran while one was open for 1% -> 1% of each run, Pallas kernels for 18% -> 19%
where the time goes in v6:
time: 19 us; the launch traced here: 18.8 us
  starting transfers between devices  9.94 us (52%)
  Pallas kernels  5.49 us (29%)
  local copies, waits for them, and re-layouts  1.92 us (10%)
  waiting for transfers between devices  0.9 us (5%)
  between operations  0.29 us (2%)
  other arithmetic  0.28 us (1%)
    ppermute x6, starting transfers between devices, exchange(): lax.ppermute(value, 'lev', [(i, i ^ step if power else (i + step) % count...  6.72 us
    pallas_call x2, Pallas kernels, physics(): pl.pallas_call(functools.partial(physics_kernel, groups, order, helds, bl...  3.71 us
    ppermute x1, starting transfers between devices, body(): lax.ppermute((jnp.where(even, edges[0], edges[1]) * SCALE).astype(half),...  1.94 us
    unnamed x24, local copies, waits for them, and re-layouts  1.91 us
    pallas_call x2, Pallas kernels, local_rows(): pl.pallas_call(functools.partial(local_kernel, groups, inner), in_specs=[...  1.38 us
    ppermute x1, starting transfers between devices, body(): lax.ppermute((jnp.where(even, edges[1], edges[0]) * SCALE).astype(half),...  1.28 us
    ppermute x6, waiting for transfers between devices, exchange(): lax.ppermute(value, 'lev', [(i, i ^ step if power else (i + step) % count...  0.87 us
  transfers between devices with their start and end apart: 8, of which 1 were waited for; matrix products, arithmetic and copies ran while one was open for 1% of the time, Pallas kernels for 19%

profile of v6, /device:TPU:9, one launch (start us, length us, event | category | flops | bytes accessed | tf_op | source)
XLA Modules:
  0.0 18.8 jit_solution(9715706371325227051)
XLA Ops:
  0.0 1.2 %copy-done = f32[4,32,4,512]{3,2,1,0:T(4,128)S(1)} copy-done((f32[4,32,4,512]{3,2,1,0:T(4,128)S(1)}, f32[4,32,4,512]{3,2,1,0:T(4,128)}, u32[]{:S(2)}) %copy-start) | copy-done | bytes 1048600
  1.2 0.1 edge_rows.1.edges
  1.3 0.0 copy-start.4
  1.3 0.0 copy-start.5
  1.4 0.0 copy-start.6
  1.4 0.1 fusion.4
  1.4 1.3 %collective-permute-start.1 = (f16[4,32,512]{2,1,0:T(8,128)(2,1)S(1)}, f16[4,32,512]{2,1,0:T(8,128)(2,1)S(1)}, u32[]{:S(2)}, u32[]{:S(2)}) collective-permute-start(f16[4,32,512]{2,1,0:T(8,128)(2,1)S(1)} %get-tuple-element.27), channel_id=1, source_target_pairs={{0,4},{4,0},{8,12},{12,8},{16,20},{20,16},{24,28},{28,24},{1,5},{5... | collective-permute-start | bytes 393224 | tf_op jit(solution)/shard_map/ppermute | solution.py:335
  2.7 1.9 %collective-permute-start = (f16[4,32,512]{2,1,0:T(8,128)(2,1)S(1)}, f16[4,32,512]{2,1,0:T(8,128)(2,1)S(1)}, u32[]{:S(2)}, u32[]{:S(2)}) collective-permute-start(f16[4,32,512]{2,1,0:T(8,128)(2,1)S(1)} %get-tuple-element.28), channel_id=1, source_target_pairs={{4,8},{8,4},{12,16},{16,12},{20,24},{24,20},{5,9},{9,5},{13,17},{1... | collective-permute-start | bytes 393224 | tf_op jit(solution)/shard_map/ppermute | solution.py:334
  4.7 0.8 %inner_rows.1 = f32[4,264,128]{2,1,0:T(8,128)S(1)} custom-call(f32[4,32,4,512]{3,2,1,0:T(4,128)S(1)} %copy-done, f32[32,4,512]{2,1,0:T(4,128)S(1)} %copy-done.4, f32[32,4,512]{2,1,0:T(4,128)S(1)} %copy-done.5, f32[32,4,512]{2,1,0:T(4,128)S(1)} %copy-done.6, f32[2,4,32,512]{3,2,1,0:T(8,128)S(1)} %edge_rows.1.edges), custom_call_target="tpu_custom_call" | custom-call | flops 1000000000 | bytes 3000000 | tf_op jit(solution)/shard_map/inner_rows/pallas_call | solution.py:139
  5.6 0.0 copy-start.11
  5.6 1.4 %collective-permute-start.5 = (f16[264,128]{1,0:T(8,128)(2,1)S(1)}, f16[264,128]{1,0:T(8,128)(2,1)S(1)}, u32[]{:S(2)}, u32[]{:S(2)}) collective-permute-start(f16[264,128]{1,0:T(8,128)(2,1)S(1)} %get-tuple-element.23), channel_id=1, source_target_pairs={{0,2},{1,3},{2,0},{3,1},{4,6},{5,7},{6,4},{7,5},{8,10},{9,11},{10,... | collective-permute-start | bytes 202760 | tf_op jit(solution)/shard_map/ppermute | solution.py:32
  7.0 1.2 %collective-permute-start.4 = (f16[264,128]{1,0:T(8,128)(2,1)S(1)}, f16[264,128]{1,0:T(8,128)(2,1)S(1)}, u32[]{:S(2)}, u32[]{:S(2)}) collective-permute-start(f16[264,128]{1,0:T(8,128)(2,1)S(1)} %get-tuple-element.24), channel_id=1, source_target_pairs={{0,3},{1,2},{2,1},{3,0},{4,7},{5,6},{6,5},{7,4},{8,11},{9,10},{10,... | collective-permute-start | bytes 202760 | tf_op jit(solution)/shard_map/ppermute | solution.py:32
  8.3 0.3 %collective-permute-start.3 = (f16[264,128]{1,0:T(8,128)(2,1)S(1)}, f16[264,128]{1,0:T(8,128)(2,1)S(1)}, u32[]{:S(2)}, u32[]{:S(2)}) collective-permute-start(f16[264,128]{1,0:T(8,128)(2,1)S(1)} %get-tuple-element.25), channel_id=1, source_target_pairs={{0,1},{1,0},{2,3},{3,2},{4,5},{5,4},{6,7},{7,6},{8,9},{9,8},{10,11... | collective-permute-start | bytes 202760 | tf_op jit(solution)/shard_map/ppermute | solution.py:32
  8.6 0.5 %outer_rows.1 = (f32[2,4,32,512]{3,2,1,0:T(8,128)S(1)}, f32[2,32,512]{2,1,0:T(8,128)S(1)}, f32[2,32,512]{2,1,0:T(8,128)S(1)}) custom-call(f32[4,32,4,512]{3,2,1,0:T(4,128)S(1)} %copy-done, f32[32,4,512]{2,1,0:T(4,128)S(1)} %copy-done.4, f32[32,4,512]{2,1,0:T(4,128)S(1)} %copy-done.5, f32[32,4,512]{2,1,0:T(4,128)S(1)} %copy-done.6, ...), custom_call_target="tpu_custom_call" | custom-call | flops 1000000000 | bytes 3000000 | tf_op jit(solution)/shard_map/outer_rows/pallas_call | solution.py:139
  9.1 0.0 collective-permute-done.1
  9.1 0.1 near_finish.1.near
  9.3 0.0 collective-permute-done
  9.3 0.0 copy-start.2
  9.4 0.0 copy-start.3
  9.4 0.2 far_finish.1
  9.5 0.0 copy-start.1
  9.6 1.4 %collective-permute-start.7 = (f16[264,128]{1,0:T(8,128)(2,1)S(1)}, f16[264,128]{1,0:T(8,128)(2,1)S(1)}, u32[]{:S(2)}, u32[]{:S(2)}) collective-permute-start(f16[264,128]{1,0:T(8,128)(2,1)S(1)} %get-tuple-element.19), channel_id=1, source_target_pairs={{0,2},{1,3},{2,0},{3,1},{4,6},{5,7},{6,4},{7,5},{8,10},{9,11},{10,... | collective-permute-start | bytes 202760 | tf_op jit(solution)/shard_map/ppermute | solution.py:32
  11.0 2.4 %collective-permute-start.6 = (f16[264,128]{1,0:T(8,128)(2,1)S(1)}, f16[264,128]{1,0:T(8,128)(2,1)S(1)}, u32[]{:S(2)}, u32[]{:S(2)}) collective-permute-start(f16[264,128]{1,0:T(8,128)(2,1)S(1)} %get-tuple-element.20), channel_id=1, source_target_pairs={{0,3},{1,2},{2,1},{3,0},{4,7},{5,6},{6,5},{7,4},{8,11},{9,10},{10,... | collective-permute-start | bytes 202760 | tf_op jit(solution)/shard_map/ppermute | solution.py:32
  13.4 0.0 collective-permute-done.5
  13.4 0.0 collective-permute-start.2
  13.5 0.0 copy-start.7
  13.5 0.0 copy-start.8
  13.5 0.0 copy-start.9
  13.5 0.6 %copy-done.7 = f32[512]{0:T(512)S(1)} copy-done((f32[512]{0:T(512)S(1)}, f32[512]{0:T(512)}, u32[]{:S(2)}) %copy-start.7) | copy-done | bytes 2072
  14.2 1.9 %physics.2 = (f32[512,4,128]{2,1,0:T(4,128)}, f32[8,128]{1,0:T(8,128)S(1)}) custom-call(f32[264,128]{1,0:T(8,128)S(1)} %get-tuple-element.26.refs_0_, f32[264,128]{1,0:T(8,128)S(1)} %get-tuple-element.34.refs_1_, f32[264,128]{1,0:T(8,128)S(1)} %get-tuple-element.33.refs_2_, f32[264,128]{1,0:T(8,128)S(1)} %get-tuple-element.32.refs_3_, ...), custom_call_target="tpu_custom_call" | custom-call | flops 20000000000 | bytes 5000000 | tf_op jit(solution)/shard_map/physics/pallas_call | solution.py:291
  16.1 0.9 %collective-permute-done.6 = f16[264,128]{1,0:T(8,128)(2,1)S(1)} collective-permute-done((f16[264,128]{1,0:T(8,128)(2,1)S(1)}, f16[264,128]{1,0:T(8,128)(2,1)S(1)}, u32[]{:S(2)}, u32[]{:S(2)}) %collective-permute-start.6) | collective-permute-done | bytes 67616 | tf_op jit(solution)/shard_map/ppermute | solution.py:32
  17.0 1.9 %physics.3 = f32[512,4,128]{2,1,0:T(4,128)} custom-call(f32[264,128]{1,0:T(8,128)S(1)} %get-tuple-element.22.refs_0_, f32[264,128]{1,0:T(8,128)S(1)} %get-tuple-element.31.refs_1_, f32[264,128]{1,0:T(8,128)S(1)} %get-tuple-element.30.refs_2_, f32[264,128]{1,0:T(8,128)S(1)} %get-tuple-element.29.refs_3_, ...), custom_call_target="tpu_custom_call", output_to_operand_aliasing={{}: (12, {})} | custom-call | flops 20000000000 | bytes 5000000 | tf_op jit(solution)/shard_map/physics/pallas_call | solution.py:291
  (26 shorter events, 0.3 us)
Async XLA Ops:
  0.0 1.2 %copy-start = (f32[4,32,4,512]{3,2,1,0:T(4,128)S(1)}, f32[4,32,4,512]{3,2,1,0:T(4,128)}, u32[]{:S(2)}) copy-start(f32[4,32,4,512]{3,2,1,0:T(4,128)} %fields.5) | copy-start | bytes 3145732
  1.3 3.3 %copy-start.4 = (f32[32,4,512]{2,1,0:T(4,128)S(1)}, f32[32,4,512]{2,1,0:T(4,128)}, u32[]{:S(2)}) copy-start(f32[32,4,512]{2,1,0:T(4,128)} %along_lon.3) | copy-start | bytes 786436
  1.3 3.3 %copy-start.5 = (f32[32,4,512]{2,1,0:T(4,128)S(1)}, f32[32,4,512]{2,1,0:T(4,128)}, u32[]{:S(2)}) copy-start(f32[32,4,512]{2,1,0:T(4,128)} %along_lat.3) | copy-start | bytes 786436
  1.4 3.3 %copy-start.6 = (f32[32,4,512]{2,1,0:T(4,128)S(1)}, f32[32,4,512]{2,1,0:T(4,128)}, u32[]{:S(2)}) copy-start(f32[32,4,512]{2,1,0:T(4,128)} %displacement.3) | copy-start | bytes 786436
  1.4 7.7 %collective-permute-start.1 = (f16[4,32,512]{2,1,0:T(8,128)(2,1)S(1)}, f16[4,32,512]{2,1,0:T(8,128)(2,1)S(1)}, u32[]{:S(2)}, u32[]{:S(2)}) collective-permute-start(f16[4,32,512]{2,1,0:T(8,128)(2,1)S(1)} %get-tuple-element.27), channel_id=1, source_target_pairs={{0,4},{4,0},{8,12},{12,8},{16,20},{20,16},{24,28},{28,24},{1,5},{5... | collective-permute-start | bytes 393224 | tf_op jit(solution)/shard_map/ppermute | solution.py:335
  2.7 6.6 %collective-permute-start = (f16[4,32,512]{2,1,0:T(8,128)(2,1)S(1)}, f16[4,32,512]{2,1,0:T(8,128)(2,1)S(1)}, u32[]{:S(2)}, u32[]{:S(2)}) collective-permute-start(f16[4,32,512]{2,1,0:T(8,128)(2,1)S(1)} %get-tuple-element.28), channel_id=1, source_target_pairs={{4,8},{8,4},{12,16},{16,12},{20,24},{24,20},{5,9},{9,5},{13,17},{1... | collective-permute-start | bytes 393224 | tf_op jit(solution)/shard_map/ppermute | solution.py:334
  5.6 2.9 %copy-start.11 = (f32[640]{0:T(1024)S(1)}, f32[640]{0:T(1024)}, u32[]{:S(2)}) copy-start(f32[640]{0:T(1024)} %param.21) | copy-start | bytes 7684
  5.6 7.8 %collective-permute-start.5 = (f16[264,128]{1,0:T(8,128)(2,1)S(1)}, f16[264,128]{1,0:T(8,128)(2,1)S(1)}, u32[]{:S(2)}, u32[]{:S(2)}) collective-permute-start(f16[264,128]{1,0:T(8,128)(2,1)S(1)} %get-tuple-element.23), channel_id=1, source_target_pairs={{0,2},{1,3},{2,0},{3,1},{4,6},{5,7},{6,4},{7,5},{8,10},{9,11},{10,... | collective-permute-start | bytes 202760 | tf_op jit(solution)/shard_map/ppermute | solution.py:32
  7.0 1.5 %copy-start.10 = (f32[768]{0:T(1024)S(1)}, f32[768]{0:T(1024)}, u32[]{:S(2)}) copy-start(f32[768]{0:T(1024)} %param.19) | copy-start | bytes 9220
  7.0 6.4 %collective-permute-start.4 = (f16[264,128]{1,0:T(8,128)(2,1)S(1)}, f16[264,128]{1,0:T(8,128)(2,1)S(1)}, u32[]{:S(2)}, u32[]{:S(2)}) collective-permute-start(f16[264,128]{1,0:T(8,128)(2,1)S(1)} %get-tuple-element.24), channel_id=1, source_target_pairs={{0,3},{1,2},{2,1},{3,0},{4,7},{5,6},{6,5},{7,4},{8,11},{9,10},{10,... | collective-permute-start | bytes 202760 | tf_op jit(solution)/shard_map/ppermute | solution.py:32
  8.3 5.2 %collective-permute-start.3 = (f16[264,128]{1,0:T(8,128)(2,1)S(1)}, f16[264,128]{1,0:T(8,128)(2,1)S(1)}, u32[]{:S(2)}, u32[]{:S(2)}) collective-permute-start(f16[264,128]{1,0:T(8,128)(2,1)S(1)} %get-tuple-element.25), channel_id=1, source_target_pairs={{0,1},{1,0},{2,3},{3,2},{4,5},{5,4},{6,7},{7,6},{8,9},{9,8},{10,11... | collective-permute-start | bytes 202760 | tf_op jit(solution)/shard_map/ppermute | solution.py:32
  9.3 4.2 %copy-start.2 = (bf16[512,768]{1,0:T(8,128)(2,1)S(1)}, bf16[512,768]{1,0:T(8,128)(2,1)}, u32[]{:S(2)}) copy-start(bf16[512,768]{1,0:T(8,128)(2,1)} %refs_6_.3) | copy-start | bytes 2359300
  9.4 4.2 %copy-start.3 = (bf16[640,512]{1,0:T(8,128)(2,1)S(1)}, bf16[640,512]{1,0:T(8,128)(2,1)}, u32[]{:S(2)}) copy-start(bf16[640,512]{1,0:T(8,128)(2,1)} %refs_10_.3) | copy-start | bytes 1966084
  9.5 4.0 %copy-start.1 = (bf16[768,640]{1,0:T(8,128)(2,1)S(1)}, bf16[768,640]{1,0:T(8,128)(2,1)}, u32[]{:S(2)}) copy-start(bf16[768,640]{1,0:T(8,128)(2,1)} %refs_8_.3) | copy-start | bytes 2949124
  9.6 6.4 %collective-permute-start.7 = (f16[264,128]{1,0:T(8,128)(2,1)S(1)}, f16[264,128]{1,0:T(8,128)(2,1)S(1)}, u32[]{:S(2)}, u32[]{:S(2)}) collective-permute-start(f16[264,128]{1,0:T(8,128)(2,1)S(1)} %get-tuple-element.19), channel_id=1, source_target_pairs={{0,2},{1,3},{2,0},{3,1},{4,6},{5,7},{6,4},{7,5},{8,10},{9,11},{10,... | collective-permute-start | bytes 202760 | tf_op jit(solution)/shard_map/ppermute | solution.py:32
  11.0 5.9 %collective-permute-start.6 = (f16[264,128]{1,0:T(8,128)(2,1)S(1)}, f16[264,128]{1,0:T(8,128)(2,1)S(1)}, u32[]{:S(2)}, u32[]{:S(2)}) collective-permute-start(f16[264,128]{1,0:T(8,128)(2,1)S(1)} %get-tuple-element.20), channel_id=1, source_target_pairs={{0,3},{1,2},{2,1},{3,0},{4,7},{5,6},{6,5},{7,4},{8,11},{9,10},{10,... | collective-permute-start | bytes 202760 | tf_op jit(solution)/shard_map/ppermute | solution.py:32
  13.4 3.5 %collective-permute-start.2 = (f16[264,128]{1,0:T(8,128)(2,1)S(1)}, f16[264,128]{1,0:T(8,128)(2,1)S(1)}, u32[]{:S(2)}, u32[]{:S(2)}) collective-permute-start(f16[264,128]{1,0:T(8,128)(2,1)S(1)} %get-tuple-element.21), channel_id=1, source_target_pairs={{0,1},{1,0},{2,3},{3,2},{4,5},{5,4},{6,7},{7,6},{8,9},{9,8},{10,11... | collective-permute-start | bytes 202760 | tf_op jit(solution)/shard_map/ppermute | solution.py:32
  13.5 0.7 %copy-start.7 = (f32[512]{0:T(512)S(1)}, f32[512]{0:T(512)}, u32[]{:S(2)}) copy-start(f32[512]{0:T(512)} %param.23) | copy-start | bytes 6148
  13.5 0.7 %copy-start.8 = (s32[1,1,2]{2,1,0:T(1,128)S(1)}, s32[1,1,2]{2,1,0:T(1,128)}, u32[]{:S(2)}) copy-start(s32[1,1,2]{2,1,0:T(1,128)} %refs_4_.3) | copy-start | bytes 28
  13.5 0.7 %copy-start.9 = (s32[1,1,2]{2,1,0:T(1,128)S(1)}, s32[1,1,2]{2,1,0:T(1,128)}, u32[]{:S(2)}) copy-start(s32[1,1,2]{2,1,0:T(1,128)} %refs_5_.3) | copy-start | bytes 28

commit v7 on v6

--- a/solution.py
+++ b/solution.py
@@ -41,8 +41,9 @@
 
 
 def edge_kernel(fields, out):
-    out[0] = fields[:, :, 0, :]
-    out[1] = fields[:, :, fields.shape[2] - 1, :]
+    odd = lax.rem(lax.axis_index("lat"), 2)
+    out[1 - odd] = fields[:, :, 0, :]
+    out[odd] = fields[:, :, fields.shape[2] - 1, :]
 
 
 def edge_rows(fields):
@@ -101,9 +102,10 @@
 def local_kernel(groups, inner, fields, along_lon, along_lat, displacement, edges, *outs):
     count, _, rows, _ = fields.shape
     me = lax.axis_index("lev")
+    odd = lax.rem(lax.axis_index("lat"), 2)
 
     def line(row, field):
-        return edges[int(row > 0), field] if row in (0, rows - 1) else fields[field, :, row, :]
+        return edges[odd if row else 1 - odd, field] if row in (0, rows - 1) else fields[field, :, row, :]
 
     for row in range(1, rows - 1) if inner else (0, rows - 1):
         east_wind, west_wind = winds(along_lon[:, row, :])
@@ -253,13 +255,13 @@
     value = jnp.concatenate([columns[index].astype(jnp.bfloat16) for index in range(many)], axis=1).T
     hidden = layer(value, first, bias_first, silu)
     hidden = layer(hidden, second, bias_second, silu)
-    tendency = layer(hidden, third, bias_third, lambda v: v).T.astype(jnp.float32)
+    tendency = layer(hidden, third, bias_third, lambda v: v)
 
     def send(index, row):
         return pltpu.make_async_copy(staged.at[index], out.at[:, row, :], sem.at[index])
 
     for index, block in enumerate(blocks):
-        part = tendency[:, index * LANES : (index + 1) * LANES]
+        part = tendency[index * LANES : (index + 1) * LANES, :].T.astype(jnp.float32)
         row = block[0] if block[0] == block[1] else jnp.where(odd == 1, block[1], block[0])
         staged[index] = columns[index] + jnp.where(active(own, lent, row) > 0.0, part, 0.0)
         if block[0] == block[1]:
@@ -323,7 +325,6 @@
     count, levels, rows, lon = fields.shape
     groups = lax.axis_size("lev")
     bands = lax.axis_size("lat")
-    even = lax.axis_index("lat") % 2 == 0
     half = jnp.float16
     f32 = jnp.float32
 
@@ -331,8 +332,8 @@
     far_pairs = [(i, i + 1 if i % 2 else i - 1) for i in range(bands)]
     far_pairs = [(i, j) for i, j in far_pairs if 0 <= j < bands]
     edges = edge_rows(fields)
-    far = lax.ppermute((jnp.where(even, edges[0], edges[1]) * SCALE).astype(half), "lat", far_pairs)
-    near = lax.ppermute((jnp.where(even, edges[1], edges[0]) * SCALE).astype(half), "lat", near_pairs)
+    far = lax.ppermute((edges[1] * SCALE).astype(half), "lat", far_pairs)
+    near = lax.ppermute((edges[0] * SCALE).astype(half), "lat", near_pairs)
 
     def swap(message):
         sent = [(message[step] * SCALE).astype(half) for step in range(1, groups)]

time: 19 us -> 19 us (level)
  no operation moved by 1% of the time
where the time goes in v7:
time: 19 us; the launch traced here: 18.8 us
  starting transfers between devices  9.94 us (52%)
  Pallas kernels  5.49 us (29%)
  local copies, waits for them, and re-layouts  1.92 us (10%)
  waiting for transfers between devices  0.9 us (5%)
  between operations  0.29 us (2%)
  other arithmetic  0.26 us (1%)
    ppermute x6, starting transfers between devices, exchange(): lax.ppermute(value, 'lev', [(i, i ^ step if power else (i + step) % count...  6.72 us
    pallas_call x2, Pallas kernels, physics(): pl.pallas_call(functools.partial(physics_kernel, groups, order, helds, bl...  3.71 us
    ppermute x1, starting transfers between devices, body(): far = lax.ppermute((edges[1] * SCALE).astype(half), 'lat', far_pairs)  1.94 us
    unnamed x24, local copies, waits for them, and re-layouts  1.91 us
    pallas_call x2, Pallas kernels, local_rows(): pl.pallas_call(functools.partial(local_kernel, groups, inner), in_specs=[...  1.37 us
    ppermute x1, starting transfers between devices, body(): near = lax.ppermute((edges[0] * SCALE).astype(half), 'lat', near_pairs)  1.28 us
    ppermute x6, waiting for transfers between devices, exchange(): lax.ppermute(value, 'lev', [(i, i ^ step if power else (i + step) % count...  0.87 us
  transfers between devices with their start and end apart: 8, of which 1 were waited for; matrix products, arithmetic and copies ran while one was open for 1% of the time, Pallas kernels for 19%

profile of v7, /device:TPU:9, one launch (start us, length us, event | category | flops | bytes accessed | tf_op | source)
XLA Modules:
  0.0 18.8 jit_solution(14624548173420501365)
XLA Ops:
  0.0 1.2 %copy-done = f32[4,32,4,512]{3,2,1,0:T(4,128)S(1)} copy-done((f32[4,32,4,512]{3,2,1,0:T(4,128)S(1)}, f32[4,32,4,512]{3,2,1,0:T(4,128)}, u32[]{:S(2)}) %copy-start) | copy-done | bytes 1048600
  1.2 0.1 edge_rows.1.edges
  1.3 0.0 copy-start.4
  1.3 0.0 copy-start.5
  1.4 0.0 copy-start.6
  1.4 1.3 %collective-permute-start.1 = (f16[4,32,512]{2,1,0:T(8,128)(2,1)S(1)}, f16[4,32,512]{2,1,0:T(8,128)(2,1)S(1)}, u32[]{:S(2)}, u32[]{:S(2)}) collective-permute-start(f16[4,32,512]{2,1,0:T(8,128)(2,1)S(1)} %get-tuple-element.27), channel_id=1, source_target_pairs={{0,4},{4,0},{8,12},{12,8},{16,20},{20,16},{24,28},{28,24},{1,5},{5... | collective-permute-start | bytes 393224 | tf_op jit(solution)/shard_map/ppermute | solution.py:336
  2.7 1.9 %collective-permute-start = (f16[4,32,512]{2,1,0:T(8,128)(2,1)S(1)}, f16[4,32,512]{2,1,0:T(8,128)(2,1)S(1)}, u32[]{:S(2)}, u32[]{:S(2)}) collective-permute-start(f16[4,32,512]{2,1,0:T(8,128)(2,1)S(1)} %get-tuple-element.28), channel_id=1, source_target_pairs={{4,8},{8,4},{12,16},{16,12},{20,24},{24,20},{5,9},{9,5},{13,17},{1... | collective-permute-start | bytes 393224 | tf_op jit(solution)/shard_map/ppermute | solution.py:335
  4.7 0.8 %inner_rows.1 = f32[4,264,128]{2,1,0:T(8,128)S(1)} custom-call(f32[4,32,4,512]{3,2,1,0:T(4,128)S(1)} %copy-done, f32[32,4,512]{2,1,0:T(4,128)S(1)} %copy-done.4, f32[32,4,512]{2,1,0:T(4,128)S(1)} %copy-done.5, f32[32,4,512]{2,1,0:T(4,128)S(1)} %copy-done.6, f32[2,4,32,512]{3,2,1,0:T(8,128)S(1)} %edge_rows.1.edges), custom_call_target="tpu_custom_call" | custom-call | flops 1000000000 | bytes 3000000 | tf_op jit(solution)/shard_map/inner_rows/pallas_call | solution.py:141
  5.6 0.0 copy-start.11
  5.6 1.4 %collective-permute-start.5 = (f16[264,128]{1,0:T(8,128)(2,1)S(1)}, f16[264,128]{1,0:T(8,128)(2,1)S(1)}, u32[]{:S(2)}, u32[]{:S(2)}) collective-permute-start(f16[264,128]{1,0:T(8,128)(2,1)S(1)} %get-tuple-element.23), channel_id=1, source_target_pairs={{0,2},{1,3},{2,0},{3,1},{4,6},{5,7},{6,4},{7,5},{8,10},{9,11},{10,... | collective-permute-start | bytes 202760 | tf_op jit(solution)/shard_map/ppermute | solution.py:32
  7.0 1.2 %collective-permute-start.4 = (f16[264,128]{1,0:T(8,128)(2,1)S(1)}, f16[264,128]{1,0:T(8,128)(2,1)S(1)}, u32[]{:S(2)}, u32[]{:S(2)}) collective-permute-start(f16[264,128]{1,0:T(8,128)(2,1)S(1)} %get-tuple-element.24), channel_id=1, source_target_pairs={{0,3},{1,2},{2,1},{3,0},{4,7},{5,6},{6,5},{7,4},{8,11},{9,10},{10,... | collective-permute-start | bytes 202760 | tf_op jit(solution)/shard_map/ppermute | solution.py:32
  8.2 0.3 %collective-permute-start.3 = (f16[264,128]{1,0:T(8,128)(2,1)S(1)}, f16[264,128]{1,0:T(8,128)(2,1)S(1)}, u32[]{:S(2)}, u32[]{:S(2)}) collective-permute-start(f16[264,128]{1,0:T(8,128)(2,1)S(1)} %get-tuple-element.25), channel_id=1, source_target_pairs={{0,1},{1,0},{2,3},{3,2},{4,5},{5,4},{6,7},{7,6},{8,9},{9,8},{10,11... | collective-permute-start | bytes 202760 | tf_op jit(solution)/shard_map/ppermute | solution.py:32
  8.5 0.5 %outer_rows.1 = (f32[2,4,32,512]{3,2,1,0:T(8,128)S(1)}, f32[2,32,512]{2,1,0:T(8,128)S(1)}, f32[2,32,512]{2,1,0:T(8,128)S(1)}) custom-call(f32[4,32,4,512]{3,2,1,0:T(4,128)S(1)} %copy-done, f32[32,4,512]{2,1,0:T(4,128)S(1)} %copy-done.4, f32[32,4,512]{2,1,0:T(4,128)S(1)} %copy-done.5, f32[32,4,512]{2,1,0:T(4,128)S(1)} %copy-done.6, ...), custom_call_target="tpu_custom_call" | custom-call | flops 1000000000 | bytes 3000000 | tf_op jit(solution)/shard_map/outer_rows/pallas_call | solution.py:141
  9.1 0.0 collective-permute-done.1
  9.1 0.1 near_finish.1.near
  9.3 0.0 collective-permute-done
  9.3 0.0 copy-start.2
  9.3 0.0 copy-start.3
  9.4 0.2 far_finish.1
  9.5 0.0 copy-start.1
  9.6 1.4 %collective-permute-start.7 = (f16[264,128]{1,0:T(8,128)(2,1)S(1)}, f16[264,128]{1,0:T(8,128)(2,1)S(1)}, u32[]{:S(2)}, u32[]{:S(2)}) collective-permute-start(f16[264,128]{1,0:T(8,128)(2,1)S(1)} %get-tuple-element.19), channel_id=1, source_target_pairs={{0,2},{1,3},{2,0},{3,1},{4,6},{5,7},{6,4},{7,5},{8,10},{9,11},{10,... | collective-permute-start | bytes 202760 | tf_op jit(solution)/shard_map/ppermute | solution.py:32
  11.0 2.4 %collective-permute-start.6 = (f16[264,128]{1,0:T(8,128)(2,1)S(1)}, f16[264,128]{1,0:T(8,128)(2,1)S(1)}, u32[]{:S(2)}, u32[]{:S(2)}) collective-permute-start(f16[264,128]{1,0:T(8,128)(2,1)S(1)} %get-tuple-element.20), channel_id=1, source_target_pairs={{0,3},{1,2},{2,1},{3,0},{4,7},{5,6},{6,5},{7,4},{8,11},{9,10},{10,... | collective-permute-start | bytes 202760 | tf_op jit(solution)/shard_map/ppermute | solution.py:32
  13.4 0.0 collective-permute-done.5
  13.4 0.0 collective-permute-start.2
  13.4 0.0 collective-permute-done.3
  13.5 0.0 copy-start.7
  13.5 0.0 copy-start.8
  13.5 0.0 copy-start.9
  13.5 0.6 %copy-done.7 = f32[512]{0:T(512)S(1)} copy-done((f32[512]{0:T(512)S(1)}, f32[512]{0:T(512)}, u32[]{:S(2)}) %copy-start.7) | copy-done | bytes 2072
  14.2 1.9 %physics.2 = (f32[512,4,128]{2,1,0:T(4,128)}, f32[8,128]{1,0:T(8,128)S(1)}) custom-call(f32[264,128]{1,0:T(8,128)S(1)} %get-tuple-element.26.refs_0_, f32[264,128]{1,0:T(8,128)S(1)} %get-tuple-element.34.refs_1_, f32[264,128]{1,0:T(8,128)S(1)} %get-tuple-element.33.refs_2_, f32[264,128]{1,0:T(8,128)S(1)} %get-tuple-element.32.refs_3_, ...), custom_call_target="tpu_custom_call" | custom-call | flops 20000000000 | bytes 5000000 | tf_op jit(solution)/shard_map/physics/pallas_call | solution.py:293
  16.0 0.9 %collective-permute-done.6 = f16[264,128]{1,0:T(8,128)(2,1)S(1)} collective-permute-done((f16[264,128]{1,0:T(8,128)(2,1)S(1)}, f16[264,128]{1,0:T(8,128)(2,1)S(1)}, u32[]{:S(2)}, u32[]{:S(2)}) %collective-permute-start.6) | collective-permute-done | bytes 67616 | tf_op jit(solution)/shard_map/ppermute | solution.py:32
  16.9 1.9 %physics.3 = f32[512,4,128]{2,1,0:T(4,128)} custom-call(f32[264,128]{1,0:T(8,128)S(1)} %get-tuple-element.22.refs_0_, f32[264,128]{1,0:T(8,128)S(1)} %get-tuple-element.31.refs_1_, f32[264,128]{1,0:T(8,128)S(1)} %get-tuple-element.30.refs_2_, f32[264,128]{1,0:T(8,128)S(1)} %get-tuple-element.29.refs_3_, ...), custom_call_target="tpu_custom_call", output_to_operand_aliasing={{}: (12, {})} | custom-call | flops 20000000000 | bytes 5000000 | tf_op jit(solution)/shard_map/physics/pallas_call | solution.py:293
  (26 shorter events, 0.3 us)
Async XLA Ops:
  0.0 1.2 %copy-start = (f32[4,32,4,512]{3,2,1,0:T(4,128)S(1)}, f32[4,32,4,512]{3,2,1,0:T(4,128)}, u32[]{:S(2)}) copy-start(f32[4,32,4,512]{3,2,1,0:T(4,128)} %fields.5) | copy-start | bytes 3145732
  1.3 3.3 %copy-start.4 = (f32[32,4,512]{2,1,0:T(4,128)S(1)}, f32[32,4,512]{2,1,0:T(4,128)}, u32[]{:S(2)}) copy-start(f32[32,4,512]{2,1,0:T(4,128)} %along_lon.3) | copy-start | bytes 786436
  1.3 3.3 %copy-start.5 = (f32[32,4,512]{2,1,0:T(4,128)S(1)}, f32[32,4,512]{2,1,0:T(4,128)}, u32[]{:S(2)}) copy-start(f32[32,4,512]{2,1,0:T(4,128)} %along_lat.3) | copy-start | bytes 786436
  1.4 3.3 %copy-start.6 = (f32[32,4,512]{2,1,0:T(4,128)S(1)}, f32[32,4,512]{2,1,0:T(4,128)}, u32[]{:S(2)}) copy-start(f32[32,4,512]{2,1,0:T(4,128)} %displacement.3) | copy-start | bytes 786436
  1.4 7.7 %collective-permute-start.1 = (f16[4,32,512]{2,1,0:T(8,128)(2,1)S(1)}, f16[4,32,512]{2,1,0:T(8,128)(2,1)S(1)}, u32[]{:S(2)}, u32[]{:S(2)}) collective-permute-start(f16[4,32,512]{2,1,0:T(8,128)(2,1)S(1)} %get-tuple-element.27), channel_id=1, source_target_pairs={{0,4},{4,0},{8,12},{12,8},{16,20},{20,16},{24,28},{28,24},{1,5},{5... | collective-permute-start | bytes 393224 | tf_op jit(solution)/shard_map/ppermute | solution.py:336
  2.7 6.6 %collective-permute-start = (f16[4,32,512]{2,1,0:T(8,128)(2,1)S(1)}, f16[4,32,512]{2,1,0:T(8,128)(2,1)S(1)}, u32[]{:S(2)}, u32[]{:S(2)}) collective-permute-start(f16[4,32,512]{2,1,0:T(8,128)(2,1)S(1)} %get-tuple-element.28), channel_id=1, source_target_pairs={{4,8},{8,4},{12,16},{16,12},{20,24},{24,20},{5,9},{9,5},{13,17},{1... | collective-permute-start | bytes 393224 | tf_op jit(solution)/shard_map/ppermute | solution.py:335
  5.6 2.9 %copy-start.11 = (f32[640]{0:T(1024)S(1)}, f32[640]{0:T(1024)}, u32[]{:S(2)}) copy-start(f32[640]{0:T(1024)} %param.21) | copy-start | bytes 7684
  5.6 7.8 %collective-permute-start.5 = (f16[264,128]{1,0:T(8,128)(2,1)S(1)}, f16[264,128]{1,0:T(8,128)(2,1)S(1)}, u32[]{:S(2)}, u32[]{:S(2)}) collective-permute-start(f16[264,128]{1,0:T(8,128)(2,1)S(1)} %get-tuple-element.23), channel_id=1, source_target_pairs={{0,2},{1,3},{2,0},{3,1},{4,6},{5,7},{6,4},{7,5},{8,10},{9,11},{10,... | collective-permute-start | bytes 202760 | tf_op jit(solution)/shard_map/ppermute | solution.py:32
  7.0 1.5 %copy-start.10 = (f32[768]{0:T(1024)S(1)}, f32[768]{0:T(1024)}, u32[]{:S(2)}) copy-start(f32[768]{0:T(1024)} %param.19) | copy-start | bytes 9220
  7.0 6.4 %collective-permute-start.4 = (f16[264,128]{1,0:T(8,128)(2,1)S(1)}, f16[264,128]{1,0:T(8,128)(2,1)S(1)}, u32[]{:S(2)}, u32[]{:S(2)}) collective-permute-start(f16[264,128]{1,0:T(8,128)(2,1)S(1)} %get-tuple-element.24), channel_id=1, source_target_pairs={{0,3},{1,2},{2,1},{3,0},{4,7},{5,6},{6,5},{7,4},{8,11},{9,10},{10,... | collective-permute-start | bytes 202760 | tf_op jit(solution)/shard_map/ppermute | solution.py:32
  8.2 5.2 %collective-permute-start.3 = (f16[264,128]{1,0:T(8,128)(2,1)S(1)}, f16[264,128]{1,0:T(8,128)(2,1)S(1)}, u32[]{:S(2)}, u32[]{:S(2)}) collective-permute-start(f16[264,128]{1,0:T(8,128)(2,1)S(1)} %get-tuple-element.25), channel_id=1, source_target_pairs={{0,1},{1,0},{2,3},{3,2},{4,5},{5,4},{6,7},{7,6},{8,9},{9,8},{10,11... | collective-permute-start | bytes 202760 | tf_op jit(solution)/shard_map/ppermute | solution.py:32
  9.3 4.2 %copy-start.2 = (bf16[512,768]{1,0:T(8,128)(2,1)S(1)}, bf16[512,768]{1,0:T(8,128)(2,1)}, u32[]{:S(2)}) copy-start(bf16[512,768]{1,0:T(8,128)(2,1)} %refs_6_.3) | copy-start | bytes 2359300
  9.3 4.2 %copy-start.3 = (bf16[640,512]{1,0:T(8,128)(2,1)S(1)}, bf16[640,512]{1,0:T(8,128)(2,1)}, u32[]{:S(2)}) copy-start(bf16[640,512]{1,0:T(8,128)(2,1)} %refs_10_.3) | copy-start | bytes 1966084
  9.5 4.0 %copy-start.1 = (bf16[768,640]{1,0:T(8,128)(2,1)S(1)}, bf16[768,640]{1,0:T(8,128)(2,1)}, u32[]{:S(2)}) copy-start(bf16[768,640]{1,0:T(8,128)(2,1)} %refs_8_.3) | copy-start | bytes 2949124
  9.6 6.4 %collective-permute-start.7 = (f16[264,128]{1,0:T(8,128)(2,1)S(1)}, f16[264,128]{1,0:T(8,128)(2,1)S(1)}, u32[]{:S(2)}, u32[]{:S(2)}) collective-permute-start(f16[264,128]{1,0:T(8,128)(2,1)S(1)} %get-tuple-element.19), channel_id=1, source_target_pairs={{0,2},{1,3},{2,0},{3,1},{4,6},{5,7},{6,4},{7,5},{8,10},{9,11},{10,... | collective-permute-start | bytes 202760 | tf_op jit(solution)/shard_map/ppermute | solution.py:32
  11.0 5.9 %collective-permute-start.6 = (f16[264,128]{1,0:T(8,128)(2,1)S(1)}, f16[264,128]{1,0:T(8,128)(2,1)S(1)}, u32[]{:S(2)}, u32[]{:S(2)}) collective-permute-start(f16[264,128]{1,0:T(8,128)(2,1)S(1)} %get-tuple-element.20), channel_id=1, source_target_pairs={{0,3},{1,2},{2,1},{3,0},{4,7},{5,6},{6,5},{7,4},{8,11},{9,10},{10,... | collective-permute-start | bytes 202760 | tf_op jit(solution)/shard_map/ppermute | solution.py:32
  13.4 3.5 %collective-permute-start.2 = (f16[264,128]{1,0:T(8,128)(2,1)S(1)}, f16[264,128]{1,0:T(8,128)(2,1)S(1)}, u32[]{:S(2)}, u32[]{:S(2)}) collective-permute-start(f16[264,128]{1,0:T(8,128)(2,1)S(1)} %get-tuple-element.21), channel_id=1, source_target_pairs={{0,1},{1,0},{2,3},{3,2},{4,5},{5,4},{6,7},{7,6},{8,9},{9,8},{10,11... | collective-permute-start | bytes 202760 | tf_op jit(solution)/shard_map/ppermute | solution.py:32
  13.5 0.7 %copy-start.7 = (f32[512]{0:T(512)S(1)}, f32[512]{0:T(512)}, u32[]{:S(2)}) copy-start(f32[512]{0:T(512)} %param.23) | copy-start | bytes 6148
  13.5 0.7 %copy-start.8 = (s32[1,1,2]{2,1,0:T(1,128)S(1)}, s32[1,1,2]{2,1,0:T(1,128)}, u32[]{:S(2)}) copy-start(s32[1,1,2]{2,1,0:T(1,128)} %refs_4_.3) | copy-start | bytes 28
  13.5 0.7 %copy-start.9 = (s32[1,1,2]{2,1,0:T(1,128)S(1)}, s32[1,1,2]{2,1,0:T(1,128)}, u32[]{:S(2)}) copy-start(s32[1,1,2]{2,1,0:T(1,128)} %refs_5_.3) | copy-start | bytes 28

commit v8 on v7

--- a/solution.py
+++ b/solution.py
@@ -149,7 +149,7 @@
     )(fields, along_lon, along_lat, displacement, edges)
 
 
-def finish_row(groups, far, rows, partial, weight, share, halo, message):
+def finish_row(groups, far, partial, weight, share, halo, message):
     count = partial.shape[1]
     me = lax.axis_index("lev")
     odd = lax.rem(lax.axis_index("lat"), 2)
@@ -157,20 +157,16 @@
     wind, moved = weight[index], share[index]
     for field in range(count):
         advected = partial[index, field] + wind * halo[field]
-        store_message(message, int(far), rows, field, count, advected, moved, groups, me)
+        store_message(message, 0, 1, field, count, advected, moved, groups, me)
 
 
 def near_kernel(groups, partial, weight, share, halo, message):
-    finish_row(groups, False, 1, partial, weight, share, halo, message)
-
-
-def far_kernel(groups, partial, weight, share, halo, near, message, unit):
-    count, levels = partial.shape[1:3]
-    size = count * levels
+    finish_row(groups, False, partial, weight, share, halo, message)
+
+
+def far_kernel(groups, partial, weight, share, halo, _, message, unit):
     unit[...] = jnp.full(unit.shape, 1.0 / SCALE, jnp.float32)
-    message[:, 0:size, :] = near[:, 0:size, :]
-    message[:, 2 * size : 2 * size + count, :] = near[:, size : size + count, :]
-    finish_row(groups, True, 2, partial, weight, share, halo, message)
+    finish_row(groups, True, partial, weight, share, halo, message)
 
 
 def near_finish(partial, weight, share, halo, groups):
@@ -190,10 +186,10 @@
     f32 = jnp.float32
     return pl.pallas_call(
         functools.partial(far_kernel, groups),
-        in_specs=[VMEM] * 5,
+        in_specs=[VMEM] * 4 + [ANY],
         out_specs=[VMEM] * 2,
         out_shape=[
-            jax.ShapeDtypeStruct((groups, message_height(2, count, levels), LANES), f32),
+            jax.ShapeDtypeStruct((groups, message_height(1, count, levels), LANES), f32),
             jax.ShapeDtypeStruct((8, LANES), f32),
         ],
         compiler_params=params(),
@@ -352,14 +348,23 @@
     inner_moved = swap(inner)
     outer = local_rows(False, *local)
     near_message = near_finish(*outer, near.astype(f32) * (1.0 / SCALE), groups)
-    message, unit = far_finish(*outer, far.astype(f32) * (1.0 / SCALE), near_message, groups)
-    moved = swap(message)
+    far_message, unit = far_finish(*outer, far.astype(f32) * (1.0 / SCALE), near_message, groups)
+    tall = near_message.shape[1]
+    moved = []
+    for step in range(1, groups):
+        both = [(message[step] * SCALE).astype(half) for message in (far_message, near_message)]
+        moved.append(exchange(jnp.concatenate(both, axis=0), step, groups))
+
     blocks = tuple((row, row) for row in range(1, rows - 1))
     order = [0, *range(1, min(groups, 2)), *range(groups - 1, 1, -1)]
     sets = (received(inner, inner_moved, unit[0:1, :]),)
     result, unit = physics(sets, order, network, rows, blocks, count, levels)
-    sets = (received(message, moved, unit[0:1, :]),)
-    return physics(sets, order, network, rows, ((rows - 1, 0), (0, rows - 1)), count, levels, result)[0]
+    order = [0, *range(2, groups), *range(1, min(groups, 2))]
+    sets = tuple(
+        received(message, [value[at : at + tall] for value in moved], unit[0:1, :])
+        for message, at in ((far_message, 0), (near_message, tall))
+    )
+    return physics(sets, order, network, rows, ((0, rows - 1), (rows - 1, 0)), count, levels, result)[0]
 
 
 def solution(mesh):

time: 19 us -> 19 us (level)
  waiting for transfers between devices: 0.9 us -> 0.68 us
    ppermute x6, waiting for transfers between devices: 0.87 us -> 0.65 us  [exchange(): lax.ppermute(value, 'lev', [(i, i ^ step if power else (i + step) % count...]
where the time goes in v8:
time: 19 us; the launch traced here: 18.8 us
  starting transfers between devices  10.1 us (53%)
  Pallas kernels  5.48 us (29%)
  local copies, waits for them, and re-layouts  1.92 us (10%)
  waiting for transfers between devices  0.68 us (4%)
  other arithmetic  0.34 us (2%)
  between operations  0.32 us (2%)
    ppermute x6, starting transfers between devices, exchange(): lax.ppermute(value, 'lev', [(i, i ^ step if power else (i + step) % count...  6.86 us
    pallas_call x2, Pallas kernels, physics(): pl.pallas_call(functools.partial(physics_kernel, groups, order, helds, bl...  3.72 us
    ppermute x1, starting transfers between devices, body(): far = lax.ppermute((edges[1] * SCALE).astype(half), 'lat', far_pairs)  1.94 us
    unnamed x24, local copies, waits for them, and re-layouts  1.91 us
    pallas_call x2, Pallas kernels, local_rows(): pl.pallas_call(functools.partial(local_kernel, groups, inner), in_specs=[...  1.37 us
    ppermute x1, starting transfers between devices, body(): near = lax.ppermute((edges[0] * SCALE).astype(half), 'lat', near_pairs)  1.28 us
    ppermute x6, waiting for transfers between devices, exchange(): lax.ppermute(value, 'lev', [(i, i ^ step if power else (i + step) % count...  0.65 us
  transfers between devices with their start and end apart: 8, of which 1 were waited for; matrix products, arithmetic and copies ran while one was open for 1% of the time, Pallas kernels for 19%

profile of v8, /device:TPU:9, one launch (start us, length us, event | category | flops | bytes accessed | tf_op | source)
XLA Modules:
  0.0 18.8 jit_solution(8286539362349219605)
XLA Ops:
  0.0 1.2 %copy-done = f32[4,32,4,512]{3,2,1,0:T(4,128)S(1)} copy-done((f32[4,32,4,512]{3,2,1,0:T(4,128)S(1)}, f32[4,32,4,512]{3,2,1,0:T(4,128)}, u32[]{:S(2)}) %copy-start) | copy-done | bytes 1048600
  1.2 0.1 edge_rows.1.edges
  1.3 0.0 copy-start.4
  1.3 0.0 copy-start.5
  1.4 0.0 copy-start.6
  1.4 1.3 %collective-permute-start.1 = (f16[4,32,512]{2,1,0:T(8,128)(2,1)S(1)}, f16[4,32,512]{2,1,0:T(8,128)(2,1)S(1)}, u32[]{:S(2)}, u32[]{:S(2)}) collective-permute-start(f16[4,32,512]{2,1,0:T(8,128)(2,1)S(1)} %get-tuple-element.23), channel_id=1, source_target_pairs={{0,4},{4,0},{8,12},{12,8},{16,20},{20,16},{24,28},{28,24},{1,5},{5... | collective-permute-start | bytes 393224 | tf_op jit(solution)/shard_map/ppermute | solution.py:332
  2.7 1.9 %collective-permute-start = (f16[4,32,512]{2,1,0:T(8,128)(2,1)S(1)}, f16[4,32,512]{2,1,0:T(8,128)(2,1)S(1)}, u32[]{:S(2)}, u32[]{:S(2)}) collective-permute-start(f16[4,32,512]{2,1,0:T(8,128)(2,1)S(1)} %get-tuple-element.24), channel_id=1, source_target_pairs={{4,8},{8,4},{12,16},{16,12},{20,24},{24,20},{5,9},{9,5},{13,17},{1... | collective-permute-start | bytes 393224 | tf_op jit(solution)/shard_map/ppermute | solution.py:331
  4.7 0.8 %inner_rows.1 = f32[4,264,128]{2,1,0:T(8,128)S(1)} custom-call(f32[4,32,4,512]{3,2,1,0:T(4,128)S(1)} %copy-done, f32[32,4,512]{2,1,0:T(4,128)S(1)} %copy-done.4, f32[32,4,512]{2,1,0:T(4,128)S(1)} %copy-done.5, f32[32,4,512]{2,1,0:T(4,128)S(1)} %copy-done.6, f32[2,4,32,512]{3,2,1,0:T(8,128)S(1)} %edge_rows.1.edges), custom_call_target="tpu_custom_call" | custom-call | flops 1000000000 | bytes 3000000 | tf_op jit(solution)/shard_map/inner_rows/pallas_call | solution.py:141
  5.6 0.0 copy-start.11
  5.6 1.4 %collective-permute-start.5 = (f16[264,128]{1,0:T(8,128)(2,1)S(1)}, f16[264,128]{1,0:T(8,128)(2,1)S(1)}, u32[]{:S(2)}, u32[]{:S(2)}) collective-permute-start(f16[264,128]{1,0:T(8,128)(2,1)S(1)} %get-tuple-element.19), channel_id=1, source_target_pairs={{0,2},{1,3},{2,0},{3,1},{4,6},{5,7},{6,4},{7,5},{8,10},{9,11},{10,... | collective-permute-start | bytes 202760 | tf_op jit(solution)/shard_map/ppermute | solution.py:32
  7.0 1.2 %collective-permute-start.4 = (f16[264,128]{1,0:T(8,128)(2,1)S(1)}, f16[264,128]{1,0:T(8,128)(2,1)S(1)}, u32[]{:S(2)}, u32[]{:S(2)}) collective-permute-start(f16[264,128]{1,0:T(8,128)(2,1)S(1)} %get-tuple-element.20), channel_id=1, source_target_pairs={{0,3},{1,2},{2,1},{3,0},{4,7},{5,6},{6,5},{7,4},{8,11},{9,10},{10,... | collective-permute-start | bytes 202760 | tf_op jit(solution)/shard_map/ppermute | solution.py:32
  8.2 0.3 %collective-permute-start.3 = (f16[264,128]{1,0:T(8,128)(2,1)S(1)}, f16[264,128]{1,0:T(8,128)(2,1)S(1)}, u32[]{:S(2)}, u32[]{:S(2)}) collective-permute-start(f16[264,128]{1,0:T(8,128)(2,1)S(1)} %get-tuple-element.21), channel_id=1, source_target_pairs={{0,1},{1,0},{2,3},{3,2},{4,5},{5,4},{6,7},{7,6},{8,9},{9,8},{10,11... | collective-permute-start | bytes 202760 | tf_op jit(solution)/shard_map/ppermute | solution.py:32
  8.5 0.5 %outer_rows.1 = (f32[2,4,32,512]{3,2,1,0:T(8,128)S(1)}, f32[2,32,512]{2,1,0:T(8,128)S(1)}, f32[2,32,512]{2,1,0:T(8,128)S(1)}) custom-call(f32[4,32,4,512]{3,2,1,0:T(4,128)S(1)} %copy-done, f32[32,4,512]{2,1,0:T(4,128)S(1)} %copy-done.4, f32[32,4,512]{2,1,0:T(4,128)S(1)} %copy-done.5, f32[32,4,512]{2,1,0:T(4,128)S(1)} %copy-done.6, ...), custom_call_target="tpu_custom_call" | custom-call | flops 1000000000 | bytes 3000000 | tf_op jit(solution)/shard_map/outer_rows/pallas_call | solution.py:141
  9.1 0.0 collective-permute-done.1
  9.1 0.1 near_finish.1._
  9.3 0.0 collective-permute-done
  9.3 0.0 copy-start.3
  9.3 0.1 far_finish.1
  9.5 0.0 copy-start.1
  9.5 0.0 copy-start.2
  9.5 0.1 slice_bitcast_fusion.1
  9.6 1.4 %collective-permute-start.2 = (f16[272,128]{1,0:T(8,128)(2,1)S(1)}, f16[272,128]{1,0:T(8,128)(2,1)S(1)}, u32[]{:S(2)}, u32[]{:S(2)}) collective-permute-start(f16[272,128]{1,0:T(8,128)(2,1)S(1)} %pad_maximum_fusion), channel_id=1, source_target_pairs={{0,2},{1,3},{2,0},{3,1},{4,6},{5,7},{6,4},{7,5},{8,10},{9,11},{10,... | collective-permute-start | bytes 208904 | tf_op jit(solution)/shard_map/ppermute | solution.py:32
  11.1 2.5 %collective-permute-start.6 = (f16[272,128]{1,0:T(8,128)(2,1)S(1)}, f16[272,128]{1,0:T(8,128)(2,1)S(1)}, u32[]{:S(2)}, u32[]{:S(2)}) collective-permute-start(f16[272,128]{1,0:T(8,128)(2,1)S(1)} %pad_maximum_fusion.1), channel_id=1, source_target_pairs={{0,3},{1,2},{2,1},{3,0},{4,7},{5,6},{6,5},{7,4},{8,11},{9,10},{10,... | collective-permute-start | bytes 208904 | tf_op jit(solution)/shard_map/ppermute | solution.py:32
  13.5 0.0 collective-permute-done.5
  13.6 0.1 collective-permute-start.7
  13.7 0.0 copy-start.7
  13.7 0.0 copy-start.8
  13.7 0.0 copy-start.9
  13.8 0.6 %copy-done.7 = f32[512]{0:T(512)S(1)} copy-done((f32[512]{0:T(512)S(1)}, f32[512]{0:T(512)}, u32[]{:S(2)}) %copy-start.7) | copy-done | bytes 2072
  14.4 1.9 %physics.2 = (f32[512,4,128]{2,1,0:T(4,128)}, f32[8,128]{1,0:T(8,128)S(1)}) custom-call(f32[264,128]{1,0:T(8,128)S(1)} %get-tuple-element.22.refs_0_, f32[264,128]{1,0:T(8,128)S(1)} %get-tuple-element.45.refs_1_, f32[264,128]{1,0:T(8,128)S(1)} %get-tuple-element.44.refs_2_, f32[264,128]{1,0:T(8,128)S(1)} %get-tuple-element.43.refs_3_, ...), custom_call_target="tpu_custom_call" | custom-call | flops 20000000000 | bytes 5000000 | tf_op jit(solution)/shard_map/physics/pallas_call | solution.py:289
  16.3 0.6 %collective-permute-done.6 = f16[272,128]{1,0:T(8,128)(2,1)S(1)} collective-permute-done((f16[272,128]{1,0:T(8,128)(2,1)S(1)}, f16[272,128]{1,0:T(8,128)(2,1)S(1)}, u32[]{:S(2)}, u32[]{:S(2)}) %collective-permute-start.6) | collective-permute-done | bytes 69664 | tf_op jit(solution)/shard_map/ppermute | solution.py:32
  16.9 1.9 %physics.3 = f32[512,4,128]{2,1,0:T(4,128)} custom-call(f32[136,128]{1,0:T(8,128)S(1)} %get-tuple-element.46.refs_0_, f32[136,128]{1,0:T(8,128)S(1)} %get-tuple-element.39.refs_1_, f32[136,128]{1,0:T(8,128)S(1)} %get-tuple-element.41.refs_2_, f32[136,128]{1,0:T(8,128)S(1)} %get-tuple-element.34.refs_3_, ...), custom_call_target="tpu_custom_call", output_to_operand_aliasing={{}: (16, {})} | custom-call | flops 20000000000 | bytes 5000000 | tf_op jit(solution)/shard_map/physics/pallas_call | solution.py:289
  (29 shorter events, 0.3 us)
Async XLA Ops:
  0.0 1.2 %copy-start = (f32[4,32,4,512]{3,2,1,0:T(4,128)S(1)}, f32[4,32,4,512]{3,2,1,0:T(4,128)}, u32[]{:S(2)}) copy-start(f32[4,32,4,512]{3,2,1,0:T(4,128)} %fields.5) | copy-start | bytes 3145732
  1.3 3.3 %copy-start.4 = (f32[32,4,512]{2,1,0:T(4,128)S(1)}, f32[32,4,512]{2,1,0:T(4,128)}, u32[]{:S(2)}) copy-start(f32[32,4,512]{2,1,0:T(4,128)} %along_lon.3) | copy-start | bytes 786436
  1.3 3.3 %copy-start.5 = (f32[32,4,512]{2,1,0:T(4,128)S(1)}, f32[32,4,512]{2,1,0:T(4,128)}, u32[]{:S(2)}) copy-start(f32[32,4,512]{2,1,0:T(4,128)} %along_lat.3) | copy-start | bytes 786436
  1.4 3.3 %copy-start.6 = (f32[32,4,512]{2,1,0:T(4,128)S(1)}, f32[32,4,512]{2,1,0:T(4,128)}, u32[]{:S(2)}) copy-start(f32[32,4,512]{2,1,0:T(4,128)} %displacement.3) | copy-start | bytes 786436
  1.4 7.7 %collective-permute-start.1 = (f16[4,32,512]{2,1,0:T(8,128)(2,1)S(1)}, f16[4,32,512]{2,1,0:T(8,128)(2,1)S(1)}, u32[]{:S(2)}, u32[]{:S(2)}) collective-permute-start(f16[4,32,512]{2,1,0:T(8,128)(2,1)S(1)} %get-tuple-element.23), channel_id=1, source_target_pairs={{0,4},{4,0},{8,12},{12,8},{16,20},{20,16},{24,28},{28,24},{1,5},{5... | collective-permute-start | bytes 393224 | tf_op jit(solution)/shard_map/ppermute | solution.py:332
  2.7 6.6 %collective-permute-start = (f16[4,32,512]{2,1,0:T(8,128)(2,1)S(1)}, f16[4,32,512]{2,1,0:T(8,128)(2,1)S(1)}, u32[]{:S(2)}, u32[]{:S(2)}) collective-permute-start(f16[4,32,512]{2,1,0:T(8,128)(2,1)S(1)} %get-tuple-element.24), channel_id=1, source_target_pairs={{4,8},{8,4},{12,16},{16,12},{20,24},{24,20},{5,9},{9,5},{13,17},{1... | collective-permute-start | bytes 393224 | tf_op jit(solution)/shard_map/ppermute | solution.py:331
  5.6 2.9 %copy-start.11 = (f32[640]{0:T(1024)S(1)}, f32[640]{0:T(1024)}, u32[]{:S(2)}) copy-start(f32[640]{0:T(1024)} %param.21) | copy-start | bytes 7684
  5.6 8.0 %collective-permute-start.5 = (f16[264,128]{1,0:T(8,128)(2,1)S(1)}, f16[264,128]{1,0:T(8,128)(2,1)S(1)}, u32[]{:S(2)}, u32[]{:S(2)}) collective-permute-start(f16[264,128]{1,0:T(8,128)(2,1)S(1)} %get-tuple-element.19), channel_id=1, source_target_pairs={{0,2},{1,3},{2,0},{3,1},{4,6},{5,7},{6,4},{7,5},{8,10},{9,11},{10,... | collective-permute-start | bytes 202760 | tf_op jit(solution)/shard_map/ppermute | solution.py:32
  7.0 1.5 %copy-start.10 = (f32[768]{0:T(1024)S(1)}, f32[768]{0:T(1024)}, u32[]{:S(2)}) copy-start(f32[768]{0:T(1024)} %param.19) | copy-start | bytes 9220
  7.0 6.6 %collective-permute-start.4 = (f16[264,128]{1,0:T(8,128)(2,1)S(1)}, f16[264,128]{1,0:T(8,128)(2,1)S(1)}, u32[]{:S(2)}, u32[]{:S(2)}) collective-permute-start(f16[264,128]{1,0:T(8,128)(2,1)S(1)} %get-tuple-element.20), channel_id=1, source_target_pairs={{0,3},{1,2},{2,1},{3,0},{4,7},{5,6},{6,5},{7,4},{8,11},{9,10},{10,... | collective-permute-start | bytes 202760 | tf_op jit(solution)/shard_map/ppermute | solution.py:32
  8.2 5.4 %collective-permute-start.3 = (f16[264,128]{1,0:T(8,128)(2,1)S(1)}, f16[264,128]{1,0:T(8,128)(2,1)S(1)}, u32[]{:S(2)}, u32[]{:S(2)}) collective-permute-start(f16[264,128]{1,0:T(8,128)(2,1)S(1)} %get-tuple-element.21), channel_id=1, source_target_pairs={{0,1},{1,0},{2,3},{3,2},{4,5},{5,4},{6,7},{7,6},{8,9},{9,8},{10,11... | collective-permute-start | bytes 202760 | tf_op jit(solution)/shard_map/ppermute | solution.py:32
  9.3 4.4 %copy-start.3 = (bf16[640,512]{1,0:T(8,128)(2,1)S(1)}, bf16[640,512]{1,0:T(8,128)(2,1)}, u32[]{:S(2)}) copy-start(bf16[640,512]{1,0:T(8,128)(2,1)} %refs_14_.1) | copy-start | bytes 1966084
  9.5 4.2 %copy-start.1 = (bf16[768,640]{1,0:T(8,128)(2,1)S(1)}, bf16[768,640]{1,0:T(8,128)(2,1)}, u32[]{:S(2)}) copy-start(bf16[768,640]{1,0:T(8,128)(2,1)} %refs_12_.1) | copy-start | bytes 2949124
  9.5 4.2 %copy-start.2 = (bf16[512,768]{1,0:T(8,128)(2,1)S(1)}, bf16[512,768]{1,0:T(8,128)(2,1)}, u32[]{:S(2)}) copy-start(bf16[512,768]{1,0:T(8,128)(2,1)} %refs_10_.3) | copy-start | bytes 2359300
  9.6 6.6 %collective-permute-start.2 = (f16[272,128]{1,0:T(8,128)(2,1)S(1)}, f16[272,128]{1,0:T(8,128)(2,1)S(1)}, u32[]{:S(2)}, u32[]{:S(2)}) collective-permute-start(f16[272,128]{1,0:T(8,128)(2,1)S(1)} %pad_maximum_fusion), channel_id=1, source_target_pairs={{0,2},{1,3},{2,0},{3,1},{4,6},{5,7},{6,4},{7,5},{8,10},{9,11},{10,... | collective-permute-start | bytes 208904 | tf_op jit(solution)/shard_map/ppermute | solution.py:32
  11.1 5.8 %collective-permute-start.6 = (f16[272,128]{1,0:T(8,128)(2,1)S(1)}, f16[272,128]{1,0:T(8,128)(2,1)S(1)}, u32[]{:S(2)}, u32[]{:S(2)}) collective-permute-start(f16[272,128]{1,0:T(8,128)(2,1)S(1)} %pad_maximum_fusion.1), channel_id=1, source_target_pairs={{0,3},{1,2},{2,1},{3,0},{4,7},{5,6},{6,5},{7,4},{8,11},{9,10},{10,... | collective-permute-start | bytes 208904 | tf_op jit(solution)/shard_map/ppermute | solution.py:32
  13.6 3.4 %collective-permute-start.7 = (f16[272,128]{1,0:T(8,128)(2,1)S(1)}, f16[272,128]{1,0:T(8,128)(2,1)S(1)}, u32[]{:S(2)}, u32[]{:S(2)}) collective-permute-start(f16[272,128]{1,0:T(8,128)(2,1)S(1)} %pad_maximum_fusion.2), channel_id=1, source_target_pairs={{0,1},{1,0},{2,3},{3,2},{4,5},{5,4},{6,7},{7,6},{8,9},{9,8},{10,11... | collective-permute-start | bytes 208904 | tf_op jit(solution)/shard_map/ppermute | solution.py:32
  13.7 0.7 %copy-start.7 = (f32[512]{0:T(512)S(1)}, f32[512]{0:T(512)}, u32[]{:S(2)}) copy-start(f32[512]{0:T(512)} %param.23) | copy-start | bytes 6148
  13.7 0.7 %copy-start.8 = (s32[1,1,2]{2,1,0:T(1,128)S(1)}, s32[1,1,2]{2,1,0:T(1,128)}, u32[]{:S(2)}) copy-start(s32[1,1,2]{2,1,0:T(1,128)} %refs_8_.3) | copy-start | bytes 28
  13.7 0.7 %copy-start.9 = (s32[1,1,2]{2,1,0:T(1,128)S(1)}, s32[1,1,2]{2,1,0:T(1,128)}, u32[]{:S(2)}) copy-start(s32[1,1,2]{2,1,0:T(1,128)} %refs_9_.1) | copy-start | bytes 28

commit v9 on v6

--- a/solution.py
+++ b/solution.py
@@ -250,16 +250,16 @@
                 row = field * depth + level * levels
                 line = index * count + field
                 columns[index, row : row + 1, :] += carried[level - 1, line : line + 1, :]
-    value = jnp.concatenate([columns[index].astype(jnp.bfloat16) for index in range(many)], axis=1).T
+    value = jnp.concatenate([columns[index].astype(jnp.bfloat16).T for index in range(many)], axis=0)
     hidden = layer(value, first, bias_first, silu)
     hidden = layer(hidden, second, bias_second, silu)
-    tendency = layer(hidden, third, bias_third, lambda v: v).T.astype(jnp.float32)
+    tendency = layer(hidden, third, bias_third, lambda v: v)
 
     def send(index, row):
         return pltpu.make_async_copy(staged.at[index], out.at[:, row, :], sem.at[index])
 
     for index, block in enumerate(blocks):
-        part = tendency[:, index * LANES : (index + 1) * LANES]
+        part = tendency[index * LANES : (index + 1) * LANES, :].T.astype(jnp.float32)
         row = block[0] if block[0] == block[1] else jnp.where(odd == 1, block[1], block[0])
         staged[index] = columns[index] + jnp.where(active(own, lent, row) > 0.0, part, 0.0)
         if block[0] == block[1]:

time: 19 us -> 19 us (level)
  no operation moved by 1% of the time
where the time goes in v9:
time: 19 us; the launch traced here: 18.8 us
  starting transfers between devices  9.94 us (52%)
  Pallas kernels  5.49 us (29%)
  local copies, waits for them, and re-layouts  1.92 us (10%)
  waiting for transfers between devices  0.9 us (5%)
  between operations  0.29 us (2%)
  other arithmetic  0.28 us (1%)
    ppermute x6, starting transfers between devices, exchange(): lax.ppermute(value, 'lev', [(i, i ^ step if power else (i + step) % count...  6.72 us
    pallas_call x2, Pallas kernels, physics(): pl.pallas_call(functools.partial(physics_kernel, groups, order, helds, bl...  3.71 us
    ppermute x1, starting transfers between devices, body(): lax.ppermute((jnp.where(even, edges[0], edges[1]) * SCALE).astype(half),...  1.94 us
    unnamed x24, local copies, waits for them, and re-layouts  1.91 us
    pallas_call x2, Pallas kernels, local_rows(): pl.pallas_call(functools.partial(local_kernel, groups, inner), in_specs=[...  1.38 us
    ppermute x1, starting transfers between devices, body(): lax.ppermute((jnp.where(even, edges[1], edges[0]) * SCALE).astype(half),...  1.28 us
    ppermute x6, waiting for transfers between devices, exchange(): lax.ppermute(value, 'lev', [(i, i ^ step if power else (i + step) % count...  0.87 us
  transfers between devices with their start and end apart: 8, of which 1 were waited for; matrix products, arithmetic and copies ran while one was open for 1% of the time, Pallas kernels for 19%

profile of v9, /device:TPU:9, one launch (start us, length us, event | category | flops | bytes accessed | tf_op | source)
XLA Modules:
  0.0 18.8 jit_solution(18177561988990332413)
XLA Ops:
  0.0 1.2 %copy-done = f32[4,32,4,512]{3,2,1,0:T(4,128)S(1)} copy-done((f32[4,32,4,512]{3,2,1,0:T(4,128)S(1)}, f32[4,32,4,512]{3,2,1,0:T(4,128)}, u32[]{:S(2)}) %copy-start) | copy-done | bytes 1048600
  1.2 0.1 edge_rows.1.edges
  1.3 0.0 copy-start.4
  1.3 0.0 copy-start.5
  1.4 0.0 copy-start.6
  1.4 0.1 fusion.4
  1.4 1.3 %collective-permute-start.1 = (f16[4,32,512]{2,1,0:T(8,128)(2,1)S(1)}, f16[4,32,512]{2,1,0:T(8,128)(2,1)S(1)}, u32[]{:S(2)}, u32[]{:S(2)}) collective-permute-start(f16[4,32,512]{2,1,0:T(8,128)(2,1)S(1)} %get-tuple-element.27), channel_id=1, source_target_pairs={{0,4},{4,0},{8,12},{12,8},{16,20},{20,16},{24,28},{28,24},{1,5},{5... | collective-permute-start | bytes 393224 | tf_op jit(solution)/shard_map/ppermute | solution.py:335
  2.7 1.9 %collective-permute-start = (f16[4,32,512]{2,1,0:T(8,128)(2,1)S(1)}, f16[4,32,512]{2,1,0:T(8,128)(2,1)S(1)}, u32[]{:S(2)}, u32[]{:S(2)}) collective-permute-start(f16[4,32,512]{2,1,0:T(8,128)(2,1)S(1)} %get-tuple-element.28), channel_id=1, source_target_pairs={{4,8},{8,4},{12,16},{16,12},{20,24},{24,20},{5,9},{9,5},{13,17},{1... | collective-permute-start | bytes 393224 | tf_op jit(solution)/shard_map/ppermute | solution.py:334
  4.7 0.8 %inner_rows.1 = f32[4,264,128]{2,1,0:T(8,128)S(1)} custom-call(f32[4,32,4,512]{3,2,1,0:T(4,128)S(1)} %copy-done, f32[32,4,512]{2,1,0:T(4,128)S(1)} %copy-done.4, f32[32,4,512]{2,1,0:T(4,128)S(1)} %copy-done.5, f32[32,4,512]{2,1,0:T(4,128)S(1)} %copy-done.6, f32[2,4,32,512]{3,2,1,0:T(8,128)S(1)} %edge_rows.1.edges), custom_call_target="tpu_custom_call" | custom-call | flops 1000000000 | bytes 3000000 | tf_op jit(solution)/shard_map/inner_rows/pallas_call | solution.py:139
  5.6 0.0 copy-start.11
  5.6 1.4 %collective-permute-start.5 = (f16[264,128]{1,0:T(8,128)(2,1)S(1)}, f16[264,128]{1,0:T(8,128)(2,1)S(1)}, u32[]{:S(2)}, u32[]{:S(2)}) collective-permute-start(f16[264,128]{1,0:T(8,128)(2,1)S(1)} %get-tuple-element.23), channel_id=1, source_target_pairs={{0,2},{1,3},{2,0},{3,1},{4,6},{5,7},{6,4},{7,5},{8,10},{9,11},{10,... | collective-permute-start | bytes 202760 | tf_op jit(solution)/shard_map/ppermute | solution.py:32
  7.0 1.2 %collective-permute-start.4 = (f16[264,128]{1,0:T(8,128)(2,1)S(1)}, f16[264,128]{1,0:T(8,128)(2,1)S(1)}, u32[]{:S(2)}, u32[]{:S(2)}) collective-permute-start(f16[264,128]{1,0:T(8,128)(2,1)S(1)} %get-tuple-element.24), channel_id=1, source_target_pairs={{0,3},{1,2},{2,1},{3,0},{4,7},{5,6},{6,5},{7,4},{8,11},{9,10},{10,... | collective-permute-start | bytes 202760 | tf_op jit(solution)/shard_map/ppermute | solution.py:32
  8.3 0.3 %collective-permute-start.3 = (f16[264,128]{1,0:T(8,128)(2,1)S(1)}, f16[264,128]{1,0:T(8,128)(2,1)S(1)}, u32[]{:S(2)}, u32[]{:S(2)}) collective-permute-start(f16[264,128]{1,0:T(8,128)(2,1)S(1)} %get-tuple-element.25), channel_id=1, source_target_pairs={{0,1},{1,0},{2,3},{3,2},{4,5},{5,4},{6,7},{7,6},{8,9},{9,8},{10,11... | collective-permute-start | bytes 202760 | tf_op jit(solution)/shard_map/ppermute | solution.py:32
  8.6 0.5 %outer_rows.1 = (f32[2,4,32,512]{3,2,1,0:T(8,128)S(1)}, f32[2,32,512]{2,1,0:T(8,128)S(1)}, f32[2,32,512]{2,1,0:T(8,128)S(1)}) custom-call(f32[4,32,4,512]{3,2,1,0:T(4,128)S(1)} %copy-done, f32[32,4,512]{2,1,0:T(4,128)S(1)} %copy-done.4, f32[32,4,512]{2,1,0:T(4,128)S(1)} %copy-done.5, f32[32,4,512]{2,1,0:T(4,128)S(1)} %copy-done.6, ...), custom_call_target="tpu_custom_call" | custom-call | flops 1000000000 | bytes 3000000 | tf_op jit(solution)/shard_map/outer_rows/pallas_call | solution.py:139
  9.1 0.0 collective-permute-done.1
  9.1 0.1 near_finish.1.near
  9.3 0.0 collective-permute-done
  9.3 0.0 copy-start.2
  9.4 0.0 copy-start.3
  9.4 0.2 far_finish.1
  9.5 0.0 copy-start.1
  9.6 1.4 %collective-permute-start.7 = (f16[264,128]{1,0:T(8,128)(2,1)S(1)}, f16[264,128]{1,0:T(8,128)(2,1)S(1)}, u32[]{:S(2)}, u32[]{:S(2)}) collective-permute-start(f16[264,128]{1,0:T(8,128)(2,1)S(1)} %get-tuple-element.19), channel_id=1, source_target_pairs={{0,2},{1,3},{2,0},{3,1},{4,6},{5,7},{6,4},{7,5},{8,10},{9,11},{10,... | collective-permute-start | bytes 202760 | tf_op jit(solution)/shard_map/ppermute | solution.py:32
  11.0 2.4 %collective-permute-start.6 = (f16[264,128]{1,0:T(8,128)(2,1)S(1)}, f16[264,128]{1,0:T(8,128)(2,1)S(1)}, u32[]{:S(2)}, u32[]{:S(2)}) collective-permute-start(f16[264,128]{1,0:T(8,128)(2,1)S(1)} %get-tuple-element.20), channel_id=1, source_target_pairs={{0,3},{1,2},{2,1},{3,0},{4,7},{5,6},{6,5},{7,4},{8,11},{9,10},{10,... | collective-permute-start | bytes 202760 | tf_op jit(solution)/shard_map/ppermute | solution.py:32
  13.4 0.0 collective-permute-done.5
  13.4 0.0 collective-permute-start.2
  13.5 0.0 copy-start.7
  13.5 0.0 copy-start.8
  13.5 0.0 copy-start.9
  13.5 0.6 %copy-done.7 = f32[512]{0:T(512)S(1)} copy-done((f32[512]{0:T(512)S(1)}, f32[512]{0:T(512)}, u32[]{:S(2)}) %copy-start.7) | copy-done | bytes 2072
  14.2 1.9 %physics.2 = (f32[512,4,128]{2,1,0:T(4,128)}, f32[8,128]{1,0:T(8,128)S(1)}) custom-call(f32[264,128]{1,0:T(8,128)S(1)} %get-tuple-element.26.refs_0_, f32[264,128]{1,0:T(8,128)S(1)} %get-tuple-element.34.refs_1_, f32[264,128]{1,0:T(8,128)S(1)} %get-tuple-element.33.refs_2_, f32[264,128]{1,0:T(8,128)S(1)} %get-tuple-element.32.refs_3_, ...), custom_call_target="tpu_custom_call" | custom-call | flops 20000000000 | bytes 5000000 | tf_op jit(solution)/shard_map/physics/pallas_call | solution.py:291
  16.1 0.9 %collective-permute-done.6 = f16[264,128]{1,0:T(8,128)(2,1)S(1)} collective-permute-done((f16[264,128]{1,0:T(8,128)(2,1)S(1)}, f16[264,128]{1,0:T(8,128)(2,1)S(1)}, u32[]{:S(2)}, u32[]{:S(2)}) %collective-permute-start.6) | collective-permute-done | bytes 67616 | tf_op jit(solution)/shard_map/ppermute | solution.py:32
  17.0 1.9 %physics.3 = f32[512,4,128]{2,1,0:T(4,128)} custom-call(f32[264,128]{1,0:T(8,128)S(1)} %get-tuple-element.22.refs_0_, f32[264,128]{1,0:T(8,128)S(1)} %get-tuple-element.31.refs_1_, f32[264,128]{1,0:T(8,128)S(1)} %get-tuple-element.30.refs_2_, f32[264,128]{1,0:T(8,128)S(1)} %get-tuple-element.29.refs_3_, ...), custom_call_target="tpu_custom_call", output_to_operand_aliasing={{}: (12, {})} | custom-call | flops 20000000000 | bytes 5000000 | tf_op jit(solution)/shard_map/physics/pallas_call | solution.py:291
  (26 shorter events, 0.3 us)
Async XLA Ops:
  0.0 1.2 %copy-start = (f32[4,32,4,512]{3,2,1,0:T(4,128)S(1)}, f32[4,32,4,512]{3,2,1,0:T(4,128)}, u32[]{:S(2)}) copy-start(f32[4,32,4,512]{3,2,1,0:T(4,128)} %fields.5) | copy-start | bytes 3145732
  1.3 3.3 %copy-start.4 = (f32[32,4,512]{2,1,0:T(4,128)S(1)}, f32[32,4,512]{2,1,0:T(4,128)}, u32[]{:S(2)}) copy-start(f32[32,4,512]{2,1,0:T(4,128)} %along_lon.3) | copy-start | bytes 786436
  1.3 3.3 %copy-start.5 = (f32[32,4,512]{2,1,0:T(4,128)S(1)}, f32[32,4,512]{2,1,0:T(4,128)}, u32[]{:S(2)}) copy-start(f32[32,4,512]{2,1,0:T(4,128)} %along_lat.3) | copy-start | bytes 786436
  1.4 3.3 %copy-start.6 = (f32[32,4,512]{2,1,0:T(4,128)S(1)}, f32[32,4,512]{2,1,0:T(4,128)}, u32[]{:S(2)}) copy-start(f32[32,4,512]{2,1,0:T(4,128)} %displacement.3) | copy-start | bytes 786436
  1.4 7.7 %collective-permute-start.1 = (f16[4,32,512]{2,1,0:T(8,128)(2,1)S(1)}, f16[4,32,512]{2,1,0:T(8,128)(2,1)S(1)}, u32[]{:S(2)}, u32[]{:S(2)}) collective-permute-start(f16[4,32,512]{2,1,0:T(8,128)(2,1)S(1)} %get-tuple-element.27), channel_id=1, source_target_pairs={{0,4},{4,0},{8,12},{12,8},{16,20},{20,16},{24,28},{28,24},{1,5},{5... | collective-permute-start | bytes 393224 | tf_op jit(solution)/shard_map/ppermute | solution.py:335
  2.7 6.6 %collective-permute-start = (f16[4,32,512]{2,1,0:T(8,128)(2,1)S(1)}, f16[4,32,512]{2,1,0:T(8,128)(2,1)S(1)}, u32[]{:S(2)}, u32[]{:S(2)}) collective-permute-start(f16[4,32,512]{2,1,0:T(8,128)(2,1)S(1)} %get-tuple-element.28), channel_id=1, source_target_pairs={{4,8},{8,4},{12,16},{16,12},{20,24},{24,20},{5,9},{9,5},{13,17},{1... | collective-permute-start | bytes 393224 | tf_op jit(solution)/shard_map/ppermute | solution.py:334
  5.6 2.9 %copy-start.11 = (f32[640]{0:T(1024)S(1)}, f32[640]{0:T(1024)}, u32[]{:S(2)}) copy-start(f32[640]{0:T(1024)} %param.21) | copy-start | bytes 7684
  5.6 7.8 %collective-permute-start.5 = (f16[264,128]{1,0:T(8,128)(2,1)S(1)}, f16[264,128]{1,0:T(8,128)(2,1)S(1)}, u32[]{:S(2)}, u32[]{:S(2)}) collective-permute-start(f16[264,128]{1,0:T(8,128)(2,1)S(1)} %get-tuple-element.23), channel_id=1, source_target_pairs={{0,2},{1,3},{2,0},{3,1},{4,6},{5,7},{6,4},{7,5},{8,10},{9,11},{10,... | collective-permute-start | bytes 202760 | tf_op jit(solution)/shard_map/ppermute | solution.py:32
  7.0 1.5 %copy-start.10 = (f32[768]{0:T(1024)S(1)}, f32[768]{0:T(1024)}, u32[]{:S(2)}) copy-start(f32[768]{0:T(1024)} %param.19) | copy-start | bytes 9220
  7.0 6.4 %collective-permute-start.4 = (f16[264,128]{1,0:T(8,128)(2,1)S(1)}, f16[264,128]{1,0:T(8,128)(2,1)S(1)}, u32[]{:S(2)}, u32[]{:S(2)}) collective-permute-start(f16[264,128]{1,0:T(8,128)(2,1)S(1)} %get-tuple-element.24), channel_id=1, source_target_pairs={{0,3},{1,2},{2,1},{3,0},{4,7},{5,6},{6,5},{7,4},{8,11},{9,10},{10,... | collective-permute-start | bytes 202760 | tf_op jit(solution)/shard_map/ppermute | solution.py:32
  8.3 5.2 %collective-permute-start.3 = (f16[264,128]{1,0:T(8,128)(2,1)S(1)}, f16[264,128]{1,0:T(8,128)(2,1)S(1)}, u32[]{:S(2)}, u32[]{:S(2)}) collective-permute-start(f16[264,128]{1,0:T(8,128)(2,1)S(1)} %get-tuple-element.25), channel_id=1, source_target_pairs={{0,1},{1,0},{2,3},{3,2},{4,5},{5,4},{6,7},{7,6},{8,9},{9,8},{10,11... | collective-permute-start | bytes 202760 | tf_op jit(solution)/shard_map/ppermute | solution.py:32
  9.3 4.2 %copy-start.2 = (bf16[512,768]{1,0:T(8,128)(2,1)S(1)}, bf16[512,768]{1,0:T(8,128)(2,1)}, u32[]{:S(2)}) copy-start(bf16[512,768]{1,0:T(8,128)(2,1)} %refs_6_.3) | copy-start | bytes 2359300
  9.4 4.2 %copy-start.3 = (bf16[640,512]{1,0:T(8,128)(2,1)S(1)}, bf16[640,512]{1,0:T(8,128)(2,1)}, u32[]{:S(2)}) copy-start(bf16[640,512]{1,0:T(8,128)(2,1)} %refs_10_.3) | copy-start | bytes 1966084
  9.5 4.0 %copy-start.1 = (bf16[768,640]{1,0:T(8,128)(2,1)S(1)}, bf16[768,640]{1,0:T(8,128)(2,1)}, u32[]{:S(2)}) copy-start(bf16[768,640]{1,0:T(8,128)(2,1)} %refs_8_.3) | copy-start | bytes 2949124
  9.6 6.4 %collective-permute-start.7 = (f16[264,128]{1,0:T(8,128)(2,1)S(1)}, f16[264,128]{1,0:T(8,128)(2,1)S(1)}, u32[]{:S(2)}, u32[]{:S(2)}) collective-permute-start(f16[264,128]{1,0:T(8,128)(2,1)S(1)} %get-tuple-element.19), channel_id=1, source_target_pairs={{0,2},{1,3},{2,0},{3,1},{4,6},{5,7},{6,4},{7,5},{8,10},{9,11},{10,... | collective-permute-start | bytes 202760 | tf_op jit(solution)/shard_map/ppermute | solution.py:32
  11.0 5.9 %collective-permute-start.6 = (f16[264,128]{1,0:T(8,128)(2,1)S(1)}, f16[264,128]{1,0:T(8,128)(2,1)S(1)}, u32[]{:S(2)}, u32[]{:S(2)}) collective-permute-start(f16[264,128]{1,0:T(8,128)(2,1)S(1)} %get-tuple-element.20), channel_id=1, source_target_pairs={{0,3},{1,2},{2,1},{3,0},{4,7},{5,6},{6,5},{7,4},{8,11},{9,10},{10,... | collective-permute-start | bytes 202760 | tf_op jit(solution)/shard_map/ppermute | solution.py:32
  13.4 3.5 %collective-permute-start.2 = (f16[264,128]{1,0:T(8,128)(2,1)S(1)}, f16[264,128]{1,0:T(8,128)(2,1)S(1)}, u32[]{:S(2)}, u32[]{:S(2)}) collective-permute-start(f16[264,128]{1,0:T(8,128)(2,1)S(1)} %get-tuple-element.21), channel_id=1, source_target_pairs={{0,1},{1,0},{2,3},{3,2},{4,5},{5,4},{6,7},{7,6},{8,9},{9,8},{10,11... | collective-permute-start | bytes 202760 | tf_op jit(solution)/shard_map/ppermute | solution.py:32
  13.5 0.7 %copy-start.7 = (f32[512]{0:T(512)S(1)}, f32[512]{0:T(512)}, u32[]{:S(2)}) copy-start(f32[512]{0:T(512)} %param.23) | copy-start | bytes 6148
  13.5 0.7 %copy-start.8 = (s32[1,1,2]{2,1,0:T(1,128)S(1)}, s32[1,1,2]{2,1,0:T(1,128)}, u32[]{:S(2)}) copy-start(s32[1,1,2]{2,1,0:T(1,128)} %refs_4_.3) | copy-start | bytes 28
  13.5 0.7 %copy-start.9 = (s32[1,1,2]{2,1,0:T(1,128)S(1)}, s32[1,1,2]{2,1,0:T(1,128)}, u32[]{:S(2)}) copy-start(s32[1,1,2]{2,1,0:T(1,128)} %refs_5_.3) | copy-start | bytes 28
